TPU v7x, 128 devices: a whole 4x4x4 slice. The times are simulated.
128 devices in a mesh: axial: 8 (over z, core), azim: 16 (over x, y).
Axes of the slice: x: 4, y: 4, z: 4, core: 2. Of those that a mesh axis runs over, the one named last changes fastest.
Arguments:
- fields: float32 [16384, 4, 1024], P(('axial', 'azim')), may hold values from -6 to 6
- new_owner: int32 [16384, 1], P(('axial', 'azim')), may hold values from 0 to 127; in each aligned block of 128 rows (0 to 127, 128 to 255, ...) at most 2 rows name the same one
- leaflet: bfloat16 [64, 256, 4096], P(None, 'axial', 'azim'), may hold values from -6 to 6
- stiffness: bfloat16 [64, 64], replicated, may hold values from -0.75 to 0.75
- coarse: float32 [8192, 256], P(('axial', 'azim')), may hold values from -6 to 6
- coarse_of_slot: int32 [32768], P(('axial', 'azim')), may hold values from 0 to 63
- viscosity: float32 [4], replicated, may hold values from 0.02 to 0.2
Outputs:
- regridded: float32 [32768, 4, 1024], P(('axial', 'azim'))
Inputs may be any that keep to these rules, and one draw needn't show every extreme that they name: `new_owner`: among the patches of one device, at most 2 share a new owner; in some device's patches exactly 2 do.
All inputs are finite; a program needn't handle non-finite values.
Results may differ from a plain program's by a relative error of at most 0.004.
Values may be sent and summed in bfloat16 or wider, within the bound.
No kernel may reach another device: no remote copies, remote signals or barrier semaphores. Data moves between devices by JAX's collectives and lax.ppermute only.
A program may use at most 64 MiB of HBM per device.

v0:
```python
import jax
import jax.numpy as jnp
from jax import lax
from jax.sharding import PartitionSpec as P

PC = 64
FIELDS = 4
STEPS = 2


SPREAD = 0.25


def padded(shard, sides, width, wrap):
    for axis, dim in sides:
        size, length = (lax.axis_size(axis), shard.shape[dim])
        up = [(i, (i + 1) % size) for i in range(size if wrap else size - 1)]
        down = [(j, i) for i, j in up]
        last = lax.slice_in_dim(shard, length - width, length, axis=dim)
        initial = lax.slice_in_dim(shard, 0, width, axis=dim)
        before = lax.ppermute(last, axis, up)
        after = lax.ppermute(initial, axis, down)
        shard = jnp.concatenate([before, shard, after], axis=dim)
    return shard


def interp_table(coarse_cols):
    fine_col = jnp.arange(2 * coarse_cols)
    nearest = fine_col // 2
    second = jnp.where(
        fine_col % 2 == 0, jnp.maximum(nearest - 1, 0), jnp.minimum(nearest + 1, coarse_cols - 1)
    )
    coarse_row = jnp.arange(coarse_cols)[:, None]
    return 0.75 * (coarse_row == nearest[None, :]).astype(jnp.float32) + 0.25 * (
        coarse_row == second[None, :]
    ).astype(jnp.float32)


def viscous(state, ghosts, viscosity):
    row_pad = jnp.concatenate([ghosts[:, :, 0:1, :], state, ghosts[:, :, 1:2, :]], axis=2)
    col_pad = jnp.pad(state, ((0, 0), (0, 0), (0, 0), (1, 1)))
    laplace = (
        row_pad[:, :, 2:, :]
        + row_pad[:, :, :-2, :]
        + col_pad[:, :, :, 2:]
        + col_pad[:, :, :, :-2]
        - 4.0 * state
    )
    return state + viscosity[None, :, None, None] * laplace


def leaflet_sheets(leaflet, stiffness):
    records, rows_axial, cols_azim = leaflet.shape
    patch_cols = cols_azim // PC
    points = leaflet.astype(jnp.float32)
    axial_pad = padded(leaflet, (("axial", 1),), 1, False).astype(jnp.float32)
    azim_pad = padded(leaflet, (("azim", 2),), 1, True).astype(jnp.float32)
    laplace = (
        axial_pad[:, 2:, :]
        + axial_pad[:, :-2, :]
        + azim_pad[:, :, :-2]
        + azim_pad[:, :, 2:]
        - 4.0 * points
    )
    laplace = laplace.astype(jnp.bfloat16)
    tension = jnp.dot(
        stiffness, laplace.reshape(records, -1), preferred_element_type=jnp.float32
    ).astype(jnp.bfloat16)
    tension = tension.reshape(records, rows_axial, patch_cols, PC).transpose(1, 2, 0, 3)
    return tension.reshape(rows_axial * patch_cols, FIELDS, records // FIELDS * PC)


def place_slots(values, target, total_slots):
    empty = jnp.zeros((total_slots,) + values.shape[1:], values.dtype)
    return empty.at[target].set(values)


def relocate(packed, devices, slots_each):
    shaped = packed.reshape((devices, slots_each) + packed.shape[1:])
    arrived = lax.all_to_all(shaped, ("axial", "azim"), split_axis=0, concat_axis=0, tiled=True)
    return arrived.reshape((devices * slots_each,) + packed.shape[1:])


def shards(fields, new_owner, leaflet, stiffness, coarse, coarse_of_slot, viscosity):
    devices = lax.axis_size("axial") * lax.axis_size("azim")
    patch_count = fields.shape[0]
    slots_each = max(2, 3 * patch_count // (2 * devices))
    received = devices * slots_each
    owners = new_owner[:, 0]
    position = jnp.arange(patch_count)
    earlier = (owners[:, None] == owners[None, :]) & (position[None, :] < position[:, None])
    ranked = jnp.sum(earlier.astype(jnp.int32), axis=1)
    target = owners * slots_each + ranked
    sheets = leaflet_sheets(leaflet, stiffness)
    forced = fields + SPREAD * sheets.astype(jnp.float32)
    placed = relocate(place_slots(forced, target, received), devices, slots_each)
    strip_count = coarse.shape[0]
    onehot = (coarse_of_slot[:, None] == jnp.arange(strip_count)[None, :]).astype(jnp.float32)
    chosen = jnp.dot(onehot, coarse, precision=lax.Precision.HIGHEST).reshape(
        received, FIELDS, 2, PC // 2
    )
    interp = interp_table(PC // 2)
    ghosts = jnp.einsum("sfgk,kc->sfgc", chosen, interp, precision=lax.Precision.HIGHEST)
    row_count = fields.shape[2] // PC
    state = placed.reshape(received, FIELDS, row_count, PC)
    for sweep in range(STEPS):
        state = viscous(state, ghosts, viscosity)
    return state.reshape(received, FIELDS, row_count * PC)


def solution(mesh):
    placed = (
        P(("axial", "azim"), None, None),
        P(("axial", "azim"), None),
        P(None, "axial", "azim"),
        P(),
        P(("axial", "azim"), None),
        P(("axial", "azim")),
        P(),
    )
    return jax.shard_map(
        shards,
        mesh=mesh,
        in_specs=placed,
        out_specs=P(("axial", "azim"), None, None),
        check_vma=False,
    )
```

profile of v0, /device:TPU:1, one launch (start us, length us, event | category | flops | bytes accessed | tf_op | source)
XLA Modules:
  0.0 180.3 jit_solution(3819290571783424061)
XLA Ops:
  0.0 1.2 fusion.34
  1.2 4.9 %collective-permute-start = (bf16[64,1,256]{2,1,0:T(2,128)(2,1)S(1)}, bf16[64,1,256]{2,1,0:T(2,128)(2,1)S(1)}, u32[]{:S(2)}, u32[]{:S(2)}) collective-permute-start(bf16[64,1,256]{2,1,0:T(2,128)(2,1)S(1)} %get-tuple-element.5), channel_id=1, source_target_pairs={{0,16},{16,32},{32,48},{48,64},{64,80},{80,96},{96,112},{1,17},{17... | collective-permute-start | bytes 98312 | tf_op jit(solution)/shard_map/ppermute | solution.py:21
  6.2 1.9 %collective-permute-start.1 = (bf16[64,1,256]{2,1,0:T(2,128)(2,1)S(1)}, bf16[64,1,256]{2,1,0:T(2,128)(2,1)S(1)}, u32[]{:S(2)}, u32[]{:S(2)}) collective-permute-start(bf16[64,1,256]{2,1,0:T(2,128)(2,1)S(1)} %get-tuple-element.6), channel_id=1, source_target_pairs={{16,0},{32,16},{48,32},{64,48},{80,64},{96,80},{112,96},{17,1},{33... | collective-permute-start | bytes 98312 | tf_op jit(solution)/shard_map/ppermute | solution.py:22
  8.1 1.4 fusion.35
  9.5 1.4 collective-permute-start.2
  10.9 3.7 %collective-permute-start.3 = (bf16[64,32,1]{2,1,0:T(8,128)(2,1)S(1)}, bf16[64,32,1]{2,1,0:T(8,128)(2,1)S(1)}, u32[]{:S(2)}, u32[]{:S(2)}) collective-permute-start(bf16[64,32,1]{2,1,0:T(8,128)(2,1)S(1)} %get-tuple-element.8), channel_id=1, source_target_pairs={{1,0},{2,1},{3,2},{4,3},{5,4},{6,5},{7,6},{8,7},{9,8},{10,9},{11,1... | collective-permute-start | bytes 12296 | tf_op jit(solution)/shard_map/ppermute | solution.py:22
  14.6 0.9 convert_reduce_fusion
  15.5 0.7 fusion.30
  16.2 8.4 %collective-permute-done.2 = bf16[64,32,1]{2,1,0:T(8,128)(2,1)S(1)} collective-permute-done((bf16[64,32,1]{2,1,0:T(8,128)(2,1)S(1)}, bf16[64,32,1]{2,1,0:T(8,128)(2,1)S(1)}, u32[]{:S(2)}, u32[]{:S(2)}) %collective-permute-start.2) | collective-permute-done | bytes 4128 | tf_op jit(solution)/shard_map/ppermute | solution.py:21
  24.6 2.1 %maximum_convert_fusion = f32[64,32,258]{2,1,0:T(8,128)S(1)} fusion(bf16[64,32,1]{2,1,0:T(8,128)(2,1)S(1)} %collective-permute-done.3, bf16[64,32,256]{2,1,0:T(8,128)(2,1)} %param.9, bf16[64,32,1]{2,1,0:T(8,128)(2,1)S(1)} %collective-permute-done.2), kind=kLoop, calls=%fused_computation.26 | loop fusion | flops 3170304 | bytes 3170304 | tf_op jit(solution)/shard_map/convert_element_type | solution.py:57
  27.3 1.1 fusion.16
  29.5 4.2 %mul.66 = f32[64,32,4,64]{3,2,1,0:T(4,128)} reshape(f32[64,8192]{1,0:T(8,128)S(1)} %fusion.2) | data formatting | bytes 4194304 | tf_op jit(solution)/shard_map/mul | solution.py:95
  33.7 6.6 %copy.31 = f32[32,4,64,64]{3,2,1,0:T(8,128)} copy(f32[32,4,64,64]{3,1,0,2:T(4,128)} %bitcast.29) | data formatting | bytes 4194304 | tf_op jit(solution)/shard_map/mul | solution.py:95
  40.3 5.1 %mul.68 = f32[128,4,1024]{2,1,0:T(4,128)} reshape(f32[32,4,64,64]{3,2,1,0:T(8,128)} %copy.31) | data formatting | bytes 4194304 | tf_op jit(solution)/shard_map/mul | solution.py:95
  45.4 3.2 %add.90 = f32[128,4,1024]{2,1,0:T(4,128)S(1)} add(f32[128,4,1024]{2,1,0:T(4,128)} %param.7, f32[128,4,1024]{2,1,0:T(4,128)} %mul.68) | non-fusion elementwise | flops 524288 | bytes 6291456 | tf_op jit(solution)/shard_map/add | solution.py:95
  48.5 3.1 %broadcast_in_dim.2 = f32[256,4,1024]{2,1,0:T(4,128)} broadcast(f32[]{:T(128)} %constant.44.clone.1), dimensions={} | broadcast | bytes 4194308 | tf_op jit(solution)/shard_map/broadcast_in_dim | solution.py:74
  51.6 15.7 %scatter_fusion = f32[256,4,1024]{2,1,0:T(4,128)} fusion(f32[256,4,1024]{2,1,0:T(4,128)} %broadcast_in_dim.2, s32[128]{0:T(128)S(1)} %fusion.30, f32[128,4,1024]{2,1,0:T(4,128)S(1)} %add.90), kind=kCustom, calls=%fused_computation | custom fusion | bytes 6291968 | tf_op jit(solution)/shard_map/scatter | solution.py:75
  67.3 12.3 %all-to-all-start = ((f32[128,2,4,1024]{3,2,1,0:T(4,128)}), f32[128,2,4,1024]{3,2,1,0:T(4,128)}, u32[]{:S(2)}, u32[]{:S(2)}) async-start(f32[128,2,4,1024]{3,2,1,0:T(4,128)} %bitcast.27), calls=%async_computation | async-start | bytes 8388608 | tf_op jit(solution)/shard_map/all_to_all | solution.py:80
  81.5 50.5 %all-to-all-done = f32[128,2,4,1024]{3,2,1,0:T(4,128)} async-done(((f32[128,2,4,1024]{3,2,1,0:T(4,128)}), f32[128,2,4,1024]{3,2,1,0:T(4,128)}, u32[]{:S(2)}, u32[]{:S(2)}) %all-to-all-start) | async-done | bytes 4194336 | tf_op jit(solution)/shard_map/all_to_all | solution.py:80
  132.0 7.8 %reshape_reshape.3 = f32[256,4,16,64]{3,2,1,0:T(8,128)} reshape(f32[128,2,4,1024]{3,2,1,0:T(4,128)} %all-to-all-done) | data formatting | bytes 8388608 | tf_op jit(solution)/shard_map/reshape;reshape | solution.py:105
  139.8 19.0 %fusion.8 = f32[256,4,16,64]{3,2,1,0:T(8,128)S(1)} fusion(f32[256,4,16,64]{3,2,1,0:T(8,128)} %reshape_reshape.3, f32[256,4,1,64]{3,2,1,0:T(1,128)S(1)} %copy.32, f32[256,4,1,64]{3,2,1,0:T(1,128)S(1)} %copy.33, f32[4]{0:T(128)S(1)} %copy-done.4), kind=kLoop, calls=%fused_computation.14 | loop fusion | flops 9437184 | bytes 8912912 | tf_op jit(solution)/shard_map/add | solution.py:49
  158.8 8.1 %fusion.14 = f32[256,4,16,64]{3,2,1,0:T(8,128)} fusion(f32[256,4,16,64]{3,2,1,0:T(8,128)S(1)} %fusion.8, f32[256,4,1,64]{3,2,1,0:T(1,128)S(1)} %copy.32, f32[256,4,1,64]{3,2,1,0:T(1,128)S(1)} %copy.33, f32[4]{0:T(128)S(1)} %copy-done.4), kind=kLoop, calls=%fused_computation.20 | loop fusion | flops 9437184 | bytes 8912912 | tf_op jit(solution)/shard_map/add | solution.py:49
  166.9 7.8 %copy.36 = f32[256,4,16,64]{0,3,2,1:T(8,128)} copy(f32[256,4,16,64]{3,2,1,0:T(8,128)} %fusion.14) | data formatting | bytes 8388608 | tf_op jit(solution)/shard_map/add | solution.py:49
  174.7 5.5 %copy.37 = f32[256,4,1024]{2,1,0:T(4,128)} copy(f32[256,4,1024]{0,2,1:T(8,128)} %bitcast.28) | data formatting | bytes 8388608 | tf_op jit(solution)/shard_map/reshape | solution.py:108
  (24 shorter events, 3.4 us)
Async XLA Ops:
  0.0 79.7 %copy-start = (f32[64,256]{1,0:T(8,128)S(1)}, f32[64,256]{1,0:T(8,128)}, u32[]{:S(2)}) copy-start(f32[64,256]{1,0:T(8,128)} %param.11) | copy-start | bytes 196612
  0.0 26.7 %copy-start.2 = (bf16[64,32,256]{2,1,0:T(8,128)(2,1)S(1)}, bf16[64,32,256]{2,1,0:T(8,128)(2,1)}, u32[]{:S(2)}) copy-start(bf16[64,32,256]{2,1,0:T(8,128)(2,1)} %param.9) | copy-start | bytes 3145732
  1.2 25.4 %collective-permute-start = (bf16[64,1,256]{2,1,0:T(2,128)(2,1)S(1)}, bf16[64,1,256]{2,1,0:T(2,128)(2,1)S(1)}, u32[]{:S(2)}, u32[]{:S(2)}) collective-permute-start(bf16[64,1,256]{2,1,0:T(2,128)(2,1)S(1)} %get-tuple-element.5), channel_id=1, source_target_pairs={{0,16},{16,32},{32,48},{48,64},{64,80},{80,96},{96,112},{1,17},{17... | collective-permute-start | bytes 98312 | tf_op jit(solution)/shard_map/ppermute | solution.py:21
  6.2 20.5 %collective-permute-start.1 = (bf16[64,1,256]{2,1,0:T(2,128)(2,1)S(1)}, bf16[64,1,256]{2,1,0:T(2,128)(2,1)S(1)}, u32[]{:S(2)}, u32[]{:S(2)}) collective-permute-start(bf16[64,1,256]{2,1,0:T(2,128)(2,1)S(1)} %get-tuple-element.6), channel_id=1, source_target_pairs={{16,0},{32,16},{48,32},{64,48},{80,64},{96,80},{112,96},{17,1},{33... | collective-permute-start | bytes 98312 | tf_op jit(solution)/shard_map/ppermute | solution.py:22
  9.5 15.0 %collective-permute-start.2 = (bf16[64,32,1]{2,1,0:T(8,128)(2,1)S(1)}, bf16[64,32,1]{2,1,0:T(8,128)(2,1)S(1)}, u32[]{:S(2)}, u32[]{:S(2)}) collective-permute-start(bf16[64,32,1]{2,1,0:T(8,128)(2,1)S(1)} %get-tuple-element.7), channel_id=1, source_target_pairs={{0,1},{1,2},{2,3},{3,4},{4,5},{5,6},{6,7},{7,8},{8,9},{9,10},{10,1... | collective-permute-start | bytes 12296 | tf_op jit(solution)/shard_map/ppermute | solution.py:21
  10.9 13.7 %collective-permute-start.3 = (bf16[64,32,1]{2,1,0:T(8,128)(2,1)S(1)}, bf16[64,32,1]{2,1,0:T(8,128)(2,1)S(1)}, u32[]{:S(2)}, u32[]{:S(2)}) collective-permute-start(bf16[64,32,1]{2,1,0:T(8,128)(2,1)S(1)} %get-tuple-element.8), channel_id=1, source_target_pairs={{1,0},{2,1},{3,2},{4,3},{5,4},{6,5},{7,6},{8,7},{9,8},{10,9},{11,1... | collective-permute-start | bytes 12296 | tf_op jit(solution)/shard_map/ppermute | solution.py:22
  27.3 1.8 copy-start.3
  67.3 12.4 %copy-start.5 = (s32[256]{0:T(256)S(1)}, s32[256]{0:T(256)}, u32[]{:S(2)}) copy-start(s32[256]{0:T(256)} %param.12) | copy-start | bytes 3076
  67.3 64.6 %all-to-all-start = ((f32[128,2,4,1024]{3,2,1,0:T(4,128)}), f32[128,2,4,1024]{3,2,1,0:T(4,128)}, u32[]{:S(2)}, u32[]{:S(2)}) async-start(f32[128,2,4,1024]{3,2,1,0:T(4,128)} %bitcast.27), calls=%async_computation | async-start | bytes 8388608 | tf_op jit(solution)/shard_map/all_to_all | solution.py:80
  81.5 58.3 %copy-start.4 = (f32[4]{0:T(128)S(1)}, f32[4]{0:T(128)}, u32[]{:S(2)}) copy-start(f32[4]{0:T(128)} %param.13) | copy-start | bytes 52
  174.7 5.5 %copy-start.1 = (f32[64,256]{1,0:T(8,128)S(1)}, f32[64,256]{1,0:T(8,128)}, u32[]{:S(2)}) copy-start(f32[64,256]{1,0:T(8,128)} %param.11) | copy-start | bytes 196612
where the time goes:
time: 182 us; the launch traced here: 180 us
  local copies, waits for them, and re-layouts  59.9 us (33%)
  waiting for transfers between devices  58.9 us (32%)
  other arithmetic  35.6 us (20%)
  starting transfers between devices  24.3 us (13%)
    all_to_all x1, waiting for transfers between devices, relocate(): lax.all_to_all(shaped, ('axial', 'azim'), split_axis=0, concat_axis=0, ti...  50.5 us
    add x2, other arithmetic, viscous(): return state + viscosity[None, :, None, None] * laplace  27.1 us
    mul x3, local copies, waits for them, and re-layouts, shards(): forced = fields + SPREAD * sheets.astype(jnp.float32)  15.9 us
    scatter x1, local copies, waits for them, and re-layouts, place_slots(): return empty.at[target].set(values)  15.7 us
    all_to_all x1, starting transfers between devices, relocate(): lax.all_to_all(shaped, ('axial', 'azim'), split_axis=0, concat_axis=0, ti...  12.3 us
    ppermute x2, waiting for transfers between devices, padded(): before = lax.ppermute(last, axis, up)  8.4 us
    another operation x1, local copies, waits for them, and re-layouts, shards(): state = placed.reshape(received, FIELDS, row_count, PC)  7.83 us
    add x1, local copies, waits for them, and re-layouts, viscous(): return state + viscosity[None, :, None, None] * laplace  7.77 us
  transfers between devices with their start and end apart: 5, of which 2 were waited for; matrix products, arithmetic and copies ran while one was open for 4% of the time, Pallas kernels for 0%

commit v1 on v0

v1 whole, which is shorter than its diff:
```python
import jax
import jax.numpy as jnp
import numpy as np
from jax import lax
from jax.experimental import pallas as pl
from jax.experimental.pallas import tpu as pltpu
from jax.sharding import PartitionSpec as P

PC = 64
FIELDS = 4
STEPS = 2
SPREAD = 0.25
LANES = 128
SUB = 8
SLOTS_EACH = 2
ALL = ("axial", "azim")


def to_tiles(x):
    n = x.shape[0]
    return x.reshape(n, FIELDS, -1, LANES).transpose(0, 2, 1, 3).reshape(n, -1, LANES)


def from_tiles(x):
    n = x.shape[0]
    return x.reshape(n, -1, FIELDS, LANES).transpose(0, 2, 1, 3).reshape(n, FIELDS, -1)


def halo(first, last, axis, wrap):
    size = lax.axis_size(axis)
    up = [(i, (i + 1) % size) for i in range(size if wrap else size - 1)]
    down = [(j, i) for i, j in up]
    return lax.ppermute(last, axis, up), lax.ppermute(first, axis, down)


def pack_kernel(target, fields, leaf, coupling, above, below, sides, out, lap, spread):
    block = pl.program_id(0)
    records, rows, cols = leaf.shape
    half = records // 2
    lane = lax.broadcasted_iota(jnp.int32, (half, LANES), 1)
    low = lane < PC

    @pl.when(block == 0)
    def _():
        def clear(i, _):
            out[pl.ds(i * 8, 8)] = jnp.zeros((8,) + out.shape[1:], out.dtype)
            return 0

        lax.fori_loop(0, out.shape[0] // 8, clear, 0)

        row_id = lax.broadcasted_iota(jnp.int32, (2, rows, cols), 1)
        col_id = lax.broadcasted_iota(jnp.int32, (2, rows, cols), 2)

        def one(i, _):
            x = leaf[pl.ds(2 * i, 2)].astype(jnp.float32)
            up = jnp.where(row_id == 0, 0.0, pltpu.roll(x, 1, 1))
            down = jnp.where(row_id == rows - 1, 0.0, pltpu.roll(x, rows - 1, 1))
            left = jnp.where(col_id == 0, 0.0, pltpu.roll(x, 1, 2))
            right = jnp.where(col_id == cols - 1, 0.0, pltpu.roll(x, cols - 1, 2))
            y = up + down + left + right - 4.0 * x
            for b in range(rows // SUB):
                part = y[:, b * SUB : (b + 1) * SUB].reshape(2 * SUB, cols)
                lap[b, pl.ds(pl.multiple_of(i * 2 * SUB, 2 * SUB), 2 * SUB)] = part.astype(lap.dtype)
            return 0

        lax.fori_loop(0, records // 2, one, 0)

        wide = records * SUB
        lift = (
            lax.broadcasted_iota(jnp.int32, (records, wide), 1) // SUB
            == lax.broadcasted_iota(jnp.int32, (records, wide), 0)
        ).astype(jnp.bfloat16)
        lifted = jnp.dot(coupling[...], lift, preferred_element_type=jnp.float32)
        within = lax.broadcasted_iota(jnp.int32, (half, wide), 1) % SUB
        for p in range(2):
            for r in range(SUB):
                part = jnp.where(within == r, lifted[p * half : (p + 1) * half], 0.0)
                at = (p * SUB + r) * half
                spread[at : at + half] = part.astype(spread.dtype)

    tension = jnp.dot(spread[...], lap[block], preferred_element_type=jnp.float32)
    edge = jnp.where(block == 0, above[...], jnp.zeros_like(above))
    edge_above = jnp.dot(coupling[...], edge, preferred_element_type=jnp.float32)
    edge = jnp.where(block == pl.num_programs(0) - 1, below[...], jnp.zeros_like(below))
    edge_below = jnp.dot(coupling[...], edge, preferred_element_type=jnp.float32)
    side = jnp.dot(coupling[...], sides[...], preferred_element_type=jnp.float32)
    quarters = cols // PC
    for r in range(SUB):
        row = block * SUB + r
        for t in range(cols // LANES):
            at = r * half
            a = tension[at : at + half, t * LANES : (t + 1) * LANES]
            at = (SUB + r) * half
            b = tension[at : at + half, t * LANES : (t + 1) * LANES]
            if r == 0:
                a = a + edge_above[:half, t * LANES : (t + 1) * LANES]
                b = b + edge_above[half:, t * LANES : (t + 1) * LANES]
            if r == SUB - 1:
                a = a + edge_below[:half, t * LANES : (t + 1) * LANES]
                b = b + edge_below[half:, t * LANES : (t + 1) * LANES]
            for h in range(2):
                q = 2 * t + h
                if h == 0:
                    sheet = jnp.where(low, a, pltpu.roll(b, PC, 1))
                else:
                    sheet = jnp.where(low, pltpu.roll(a, PC, 1), b)
                for which, cell in ((0, 0), (1, PC - 1)):
                    if q == which * (quarters - 1):
                        for p in range(2):
                            to = p * PC + cell
                            turn = lax.rem(to - which * rows - row + 2 * LANES, LANES)
                            moved = pltpu.roll(side[p * half : (p + 1) * half], turn, 1)
                            sheet = sheet + jnp.where(lane == to, moved, 0.0)
                n = quarters * r + q
                forced = fields[n] + sheet
                out[target[block * SUB * quarters + n]] = forced.astype(out.dtype)


def pack(target, fields, leaf, coupling, above, below, sides, slots):
    records, rows, cols = leaf.shape
    blocks = rows // SUB
    patches = fields.shape[0]
    whole = lambda *shape: pl.BlockSpec(shape, lambda b, *_: (0,) * len(shape))
    return pl.pallas_call(
        pack_kernel,
        grid_spec=pltpu.PrefetchScalarGridSpec(
            num_scalar_prefetch=1,
            grid=(blocks,),
            in_specs=[
                pl.BlockSpec((patches // blocks, records // 2, LANES), lambda b, *_: (b, 0, 0)),
                whole(records, rows, cols),
                whole(records, records),
                whole(records, cols),
                whole(records, cols),
                whole(records, LANES),
            ],
            out_specs=whole(slots, records // 2, LANES),
            scratch_shapes=[
                pltpu.VMEM((blocks, records * SUB, cols), jnp.bfloat16),
                pltpu.VMEM((records * SUB, records * SUB), jnp.bfloat16),
            ],
        ),
        out_shape=jax.ShapeDtypeStruct((slots, records // 2, LANES), jnp.bfloat16),
        compiler_params=pltpu.CompilerParams(vmem_limit_bytes=40 * 2**20),
    )(target, fields, leaf, coupling, above, below, sides)


def sweep_kernel(strip, state, ghosts, rate, out):
    block = pl.program_id(0)
    count = state.shape[0]
    lane = lax.broadcasted_iota(jnp.int32, (SUB, LANES), 1)
    row = lax.broadcasted_iota(jnp.int32, (SUB, LANES), 0)
    first = (lane < PC) & (row < FIELDS)
    last = (lane >= PC) & (row >= FIELDS)
    start = lane % PC == 0
    stop = lane % PC == PC - 1
    v = rate[...]
    keep = 1.0 - 4.0 * v
    tiles = state.shape[1] // SUB

    def one(s, _):
        g = ghosts[strip[block * count + s]]
        x = state[s].astype(jnp.float32)
        x = [x[k * SUB : (k + 1) * SUB] for k in range(tiles)]
        for _ in range(STEPS):
            across = [pltpu.roll(y, PC, 1) for y in x]
            ext = [g] + [pltpu.roll(y, FIELDS, 0) for y in across] + [g]
            new = []
            for k in range(tiles):
                vertical = across[k] + jnp.where(first, ext[k], jnp.where(last, ext[k + 2], ext[k + 1]))
                left = jnp.where(start, 0.0, pltpu.roll(x[k], 1, 1))
                right = jnp.where(stop, 0.0, pltpu.roll(x[k], LANES - 1, 1))
                new.append(keep * x[k] + v * (vertical + (left + right)))
            x = new
        for k in range(tiles):
            out[s, k * SUB : (k + 1) * SUB] = x[k]
        return 0

    lax.fori_loop(0, count, one, 0, unroll=4)


def sweeps(strip, state, ghosts, rate):
    slots, rows, _ = state.shape
    count = 32
    whole = lambda *shape: pl.BlockSpec(shape, lambda b, *_: (0,) * len(shape))
    return pl.pallas_call(
        sweep_kernel,
        grid_spec=pltpu.PrefetchScalarGridSpec(
            num_scalar_prefetch=1,
            grid=(slots // count,),
            in_specs=[
                pl.BlockSpec((count, rows, LANES), lambda b, *_: (b, 0, 0)),
                whole(*ghosts.shape),
                whole(SUB, LANES),
            ],
            out_specs=pl.BlockSpec((count, rows, LANES), lambda b, *_: (b, 0, 0)),
        ),
        out_shape=jax.ShapeDtypeStruct((slots, rows, LANES), jnp.float32),
        compiler_params=pltpu.CompilerParams(vmem_limit_bytes=40 * 2**20),
    )(strip, state, ghosts, rate)


def interp_table():
    coarse = PC // 2
    table = np.zeros((2, coarse, 2, PC), np.float32)
    for side in range(2):
        for c in range(PC):
            near = c // 2
            second = max(near - 1, 0) if c % 2 == 0 else min(near + 1, coarse - 1)
            table[side, near, side, c] += 0.75
            table[side, second, side, c] += 0.25
    return table.reshape(2 * coarse, 2 * PC)


def shards(fields, new_owner, leaflet, stiffness, coarse, coarse_of_slot, viscosity):
    devices = lax.axis_size("axial") * lax.axis_size("azim")
    patch_count = fields.shape[0]
    slots = devices * SLOTS_EACH
    records, rows, cols = leaflet.shape

    above, below = halo(leaflet[:, 0, :], leaflet[:, rows - 1, :], "axial", False)
    left, right = halo(leaflet[:, :, 0], leaflet[:, :, cols - 1], "azim", True)
    sides = jnp.concatenate([left, right, jnp.zeros((records, LANES - 2 * rows), leaflet.dtype)], axis=1)

    owners = new_owner[:, 0]
    position = jnp.arange(patch_count)
    earlier = (owners[:, None] == owners[None, :]) & (position[None, :] < position[:, None])
    ranked = jnp.sum(earlier.astype(jnp.int32), axis=1)
    target = owners * SLOTS_EACH + ranked

    coupling = (
        (stiffness * SPREAD).reshape(FIELDS, -1, 2, records).transpose(2, 1, 0, 3).reshape(records, records)
    )
    packed = pack(target, to_tiles(fields), leaflet, coupling, above, below, sides, slots)
    shaped = packed.reshape(devices, -1, LANES)
    arrived = lax.all_to_all(shaped, ALL, split_axis=0, concat_axis=0, tiled=True)
    state = arrived.reshape(slots, -1, LANES)

    strips = coarse.shape[0]
    ghosts = jnp.dot(
        coarse.reshape(strips * FIELDS, -1), jnp.asarray(interp_table()), precision=lax.Precision.HIGHEST
    ).reshape(strips, FIELDS, LANES)
    ghosts = jnp.concatenate([ghosts, ghosts], axis=1)
    rate = jnp.broadcast_to(jnp.concatenate([viscosity, viscosity])[:, None], (SUB, LANES))
    return from_tiles(sweeps(coarse_of_slot, state, ghosts, rate))


def solution(mesh):
    placed = (
        P(ALL, None, None),
        P(ALL, None),
        P(None, "axial", "azim"),
        P(),
        P(ALL, None),
        P(ALL),
        P(),
    )
    return jax.shard_map(
        shards,
        mesh=mesh,
        in_specs=placed,
        out_specs=P(ALL, None, None),
        check_vma=False,
    )
```

time: 182 us -> 83.8 us (0.46)
  local copies, waits for them, and re-layouts: 59.9 us -> 8.31 us
  other arithmetic: 35.6 us -> 0.38 us
  waiting for transfers between devices: 58.9 us -> 34.7 us
  Pallas kernels: 0 us -> 21.1 us
  starting transfers between devices: 24.3 us -> 18.5 us
    add x3 -> x1, other arithmetic: 30.3 us -> 0.01 us  [shards(): target = owners * SLOTS_EACH + ranked]
    all_to_all x1, waiting for transfers between devices: 50.5 us -> 29.1 us  [shards(): lax.all_to_all(shaped, ALL, split_axis=0, concat_axis=0, tiled=True)]
    pallas_call x0 -> x2, Pallas kernels: none -> 21.1 us  [the longest x1 14.6 us: sweeps(): pl.pallas_call(sweep_kernel, grid_spec=pltpu.PrefetchScalarGridSpec(num_s...]
    mul x3 -> x0, local copies, waits for them, and re-layouts: 15.9 us -> none  [shards(): forced = fields + SPREAD * sheets.astype(jnp.float32)]
    scatter x1 -> x0, local copies, waits for them, and re-layouts: 15.7 us -> none  [place_slots(): return empty.at[target].set(values)]
    another operation x1 -> x0, local copies, waits for them, and re-layouts: 7.83 us -> none  [shards(): state = placed.reshape(received, FIELDS, row_count, PC)]
    add x1 -> x0, local copies, waits for them, and re-layouts: 7.77 us -> none  [viscous(): return state + viscosity[None, :, None, None] * laplace]
    all_to_all x1, starting transfers between devices: 12.3 us -> 6.55 us  [shards(): lax.all_to_all(shaped, ALL, split_axis=0, concat_axis=0, tiled=True)]
  transfers between devices with their start and end apart: 5 -> 5, of which waited for: 2 -> 2; matrix products, arithmetic and copies ran while one was open for 4% -> 7% of each run, Pallas kernels for 0% -> 0%
where the time goes in v1:
time: 83.8 us; the launch traced here: 83.4 us
  waiting for transfers between devices  34.7 us (41%)
  Pallas kernels  21.1 us (25%)
  starting transfers between devices  18.5 us (22%)
  local copies, waits for them, and re-layouts  8.31 us (10%)
    all_to_all x1, waiting for transfers between devices, shards(): lax.all_to_all(shaped, ALL, split_axis=0, concat_axis=0, tiled=True)  29.1 us
    pallas_call x1, Pallas kernels, sweeps(): pl.pallas_call(sweep_kernel, grid_spec=pltpu.PrefetchScalarGridSpec(num_s...  14.6 us
    ppermute x4, starting transfers between devices, halo(): return (lax.ppermute(last, axis, up), lax.ppermute(first, axis, down))  11.9 us
    all_to_all x1, starting transfers between devices, shards(): lax.all_to_all(shaped, ALL, split_axis=0, concat_axis=0, tiled=True)  6.55 us
    pallas_call x1, Pallas kernels, pack(): pl.pallas_call(pack_kernel, grid_spec=pltpu.PrefetchScalarGridSpec(num_sc...  6.5 us
    ppermute x4, waiting for transfers between devices, halo(): return (lax.ppermute(last, axis, up), lax.ppermute(first, axis, down))  5.58 us
    unnamed x22, local copies, waits for them, and re-layouts  4.31 us
    slice x1, local copies, waits for them, and re-layouts, shards(): left, right = halo(leaflet[:, :, 0], leaflet[:, :, cols - 1], 'azim', True)  2.35 us
  transfers between devices with their start and end apart: 5, of which 2 were waited for; matrix products, arithmetic and copies ran while one was open for 7% of the time, Pallas kernels for 0%

profile of v1, /device:TPU:1, one launch (start us, length us, event | category | flops | bytes accessed | tf_op | source)
XLA Modules:
  0.0 83.4 jit_solution(16218131191003979660)
XLA Ops:
  0.0 1.3 %fusion.4 = (bf16[64,1,256]{2,1,0:T(2,128)(2,1)S(1)}, bf16[64,1,256]{2,1,0:T(2,128)(2,1)S(1)}) fusion(bf16[64,32,256]{2,1,0:T(8,128)(2,1)} %leaf.1), kind=kLoop, calls=%fused_computation.14 | loop fusion | bytes 131072 | tf_op jit(solution)/shard_map/slice | solution.py:221
  1.3 4.9 %collective-permute-start = (bf16[64,256]{1,0:T(8,128)(2,1)S(1)}, bf16[64,256]{1,0:T(8,128)(2,1)S(1)}, u32[]{:S(2)}, u32[]{:S(2)}) collective-permute-start(bf16[64,256]{1,0:T(8,128)(2,1)S(1)} %bitcast.37), channel_id=1, source_target_pairs={{0,16},{16,32},{32,48},{48,64},{64,80},{80,96},{96,112},{1,17},{17... | collective-permute-start | bytes 98312 | tf_op jit(solution)/shard_map/ppermute | solution.py:33
  6.3 1.9 %collective-permute-start.1 = (bf16[64,256]{1,0:T(8,128)(2,1)S(1)}, bf16[64,256]{1,0:T(8,128)(2,1)S(1)}, u32[]{:S(2)}, u32[]{:S(2)}) collective-permute-start(bf16[64,256]{1,0:T(8,128)(2,1)S(1)} %bitcast.38), channel_id=1, source_target_pairs={{16,0},{32,16},{48,32},{64,48},{80,64},{96,80},{112,96},{17,1},{33... | collective-permute-start | bytes 98312 | tf_op jit(solution)/shard_map/ppermute | solution.py:33
  8.2 2.4 %fusion.3 = (bf16[64,32,1]{2,1,0:T(8,128)(2,1)}, bf16[64,32,1]{2,1,0:T(8,128)(2,1)}) fusion(bf16[64,32,256]{2,1,0:T(8,128)(2,1)} %leaf.1), kind=kLoop, calls=%fused_computation.13 | loop fusion | bytes 16384 | tf_op jit(solution)/shard_map/slice | solution.py:222
  10.6 1.5 %copy.30 = bf16[64,32,1]{1,0,2:T(8,128)(2,1)S(1)} copy(bf16[64,32,1]{2,1,0:T(8,128)(2,1)} %get-tuple-element.6) | data formatting | bytes 8192
  12.0 5.0 %collective-permute-start.3 = (bf16[64,32]{1,0:T(8,128)(2,1)S(1)}, bf16[64,32]{1,0:T(8,128)(2,1)S(1)}, u32[]{:S(2)}, u32[]{:S(2)}) collective-permute-start(bf16[64,32]{1,0:T(8,128)(2,1)S(1)} %bitcast.39), channel_id=1, source_target_pairs={{1,0},{2,1},{3,2},{4,3},{5,4},{6,5},{7,6},{8,7},{9,8},{10,9},{11,1... | collective-permute-start | bytes 12296 | tf_op jit(solution)/shard_map/ppermute | solution.py:33
  17.0 1.5 %copy.29 = bf16[64,32,1]{1,0,2:T(8,128)(2,1)S(1)} copy(bf16[64,32,1]{2,1,0:T(8,128)(2,1)} %get-tuple-element.5) | data formatting | bytes 8192
  18.5 0.1 collective-permute-start.2
  18.6 0.2 convert_reduce_fusion
  18.8 0.1 pad.6.clone
  18.9 5.6 %collective-permute-done.2 = bf16[64,32]{1,0:T(8,128)(2,1)S(1)} collective-permute-done((bf16[64,32]{1,0:T(8,128)(2,1)S(1)}, bf16[64,32]{1,0:T(8,128)(2,1)S(1)}, u32[]{:S(2)}, u32[]{:S(2)}) %collective-permute-start.2) | collective-permute-done | bytes 4128 | tf_op jit(solution)/shard_map/ppermute | solution.py:33
  24.5 0.1 maximum_maximum_fusion.sides
  24.6 0.0 collective-permute-done.above
  24.6 6.5 %shard_map.82 = bf16[256,32,128]{2,1,0:T(8,128)(2,1)S(1)} custom-call(s32[128]{0:T(128)S(1)} %multiply_add_fusion.target, f32[128,32,128]{2,1,0:T(8,128)S(1)} %bitcast.33, bf16[64,32,256]{2,1,0:T(8,128)(2,1)S(1)} %copy-done.1, bf16[64,64]{1,0:T(8,128)(2,1)S(1)} %bitcast.34, bf16[64,256]{1,0:T(8,128)(2,1)S(1)} %collective-permute-done.above, ...), custom_call_target="tpu_custom_call" | custom-call | tf_op jit(solution)/shard_map/pallas_call | solution.py:124
  31.1 0.0 copy-start
  31.1 1.3 %copy-done = bf16[256,32,128]{2,1,0:T(8,128)(2,1)} copy-done((bf16[256,32,128]{2,1,0:T(8,128)(2,1)}, bf16[256,32,128]{2,1,0:T(8,128)(2,1)S(1)}, u32[]{:S(2)}) %copy-start) | copy-done | bytes 2097176
  32.4 6.5 %all-to-all-start = ((bf16[128,64,128]{2,1,0:T(8,128)(2,1)}), bf16[128,64,128]{2,1,0:T(8,128)(2,1)S(1)}, u32[]{:S(2)}, u32[]{:S(2)}) async-start(bf16[128,64,128]{2,1,0:T(8,128)(2,1)} %bitcast.32), calls=%async_computation | async-start | bytes 4194304 | tf_op jit(solution)/shard_map/all_to_all | solution.py:236
  39.0 0.1 dot_general.5
  39.1 0.2 fusion
  39.4 0.1 copy.36
  39.5 0.1 pad_maximum_fusion.1
  39.6 29.1 %all-to-all-done = bf16[128,64,128]{2,1,0:T(8,128)(2,1)S(1)} async-done(((bf16[128,64,128]{2,1,0:T(8,128)(2,1)}), bf16[128,64,128]{2,1,0:T(8,128)(2,1)S(1)}, u32[]{:S(2)}, u32[]{:S(2)}) %all-to-all-start) | async-done | bytes 2097184 | tf_op jit(solution)/shard_map/all_to_all | solution.py:236
  68.8 0.1 broadcast_in_dim.5.rate
  68.8 14.6 %shard_map.83 = f32[256,32,128]{2,1,0:T(8,128)} custom-call(s32[256]{0:T(256)S(1)} %copy-done.3, bf16[256,32,128]{2,1,0:T(8,128)(2,1)S(1)} %bitcast.31, f32[64,8,128]{2,1,0:T(8,128)S(1)} %pad_maximum_fusion.ghosts, f32[8,128]{1,0:T(8,128)S(1)} %broadcast_in_dim.5.rate), custom_call_target="tpu_custom_call" | custom-call | tf_op jit(solution)/shard_map/pallas_call | solution.py:186
  (25 shorter events, 0.1 us)
Async XLA Ops:
  0.0 24.6 %copy-start.1 = (bf16[64,32,256]{2,1,0:T(8,128)(2,1)S(1)}, bf16[64,32,256]{2,1,0:T(8,128)(2,1)}, u32[]{:S(2)}) copy-start(bf16[64,32,256]{2,1,0:T(8,128)(2,1)} %leaf.1) | copy-start | bytes 3145732
  0.0 18.6 %copy-start.7 = (s32[128,1]{0,1:T(1,128)S(1)}, s32[128,1]{0,1:T(1,128)}, u32[]{:S(2)}) copy-start(s32[128,1]{0,1:T(1,128)} %param.9) | copy-start | bytes 1540
  0.0 18.8 %copy-start.6 = (bf16[64,64]{1,0:T(8,128)(2,1)S(1)}, bf16[64,64]{1,0:T(8,128)(2,1)}, u32[]{:S(2)}) copy-start(bf16[64,64]{1,0:T(8,128)(2,1)} %param.11) | copy-start | bytes 24580
  0.0 24.6 %copy-start.2 = (f32[128,4,1024]{2,1,0:T(4,128)S(1)}, f32[128,4,1024]{2,1,0:T(4,128)}, u32[]{:S(2)}) copy-start(f32[128,4,1024]{2,1,0:T(4,128)} %param.8) | copy-start | bytes 6291460
  1.3 23.2 %collective-permute-start = (bf16[64,256]{1,0:T(8,128)(2,1)S(1)}, bf16[64,256]{1,0:T(8,128)(2,1)S(1)}, u32[]{:S(2)}, u32[]{:S(2)}) collective-permute-start(bf16[64,256]{1,0:T(8,128)(2,1)S(1)} %bitcast.37), channel_id=1, source_target_pairs={{0,16},{16,32},{32,48},{48,64},{64,80},{80,96},{96,112},{1,17},{17... | collective-permute-start | bytes 98312 | tf_op jit(solution)/shard_map/ppermute | solution.py:33
  6.3 18.3 %collective-permute-start.1 = (bf16[64,256]{1,0:T(8,128)(2,1)S(1)}, bf16[64,256]{1,0:T(8,128)(2,1)S(1)}, u32[]{:S(2)}, u32[]{:S(2)}) collective-permute-start(bf16[64,256]{1,0:T(8,128)(2,1)S(1)} %bitcast.38), channel_id=1, source_target_pairs={{16,0},{32,16},{48,32},{64,48},{80,64},{96,80},{112,96},{17,1},{33... | collective-permute-start | bytes 98312 | tf_op jit(solution)/shard_map/ppermute | solution.py:33
  12.0 6.9 %collective-permute-start.3 = (bf16[64,32]{1,0:T(8,128)(2,1)S(1)}, bf16[64,32]{1,0:T(8,128)(2,1)S(1)}, u32[]{:S(2)}, u32[]{:S(2)}) collective-permute-start(bf16[64,32]{1,0:T(8,128)(2,1)S(1)} %bitcast.39), channel_id=1, source_target_pairs={{1,0},{2,1},{3,2},{4,3},{5,4},{6,5},{7,6},{8,7},{9,8},{10,9},{11,1... | collective-permute-start | bytes 12296 | tf_op jit(solution)/shard_map/ppermute | solution.py:33
  18.5 6.0 %collective-permute-start.2 = (bf16[64,32]{1,0:T(8,128)(2,1)S(1)}, bf16[64,32]{1,0:T(8,128)(2,1)S(1)}, u32[]{:S(2)}, u32[]{:S(2)}) collective-permute-start(bf16[64,32]{1,0:T(8,128)(2,1)S(1)} %bitcast.40), channel_id=1, source_target_pairs={{0,1},{1,2},{2,3},{3,4},{4,5},{5,6},{6,7},{7,8},{8,9},{9,10},{10,1... | collective-permute-start | bytes 12296 | tf_op jit(solution)/shard_map/ppermute | solution.py:33
  31.1 1.3 %copy-start = (bf16[256,32,128]{2,1,0:T(8,128)(2,1)}, bf16[256,32,128]{2,1,0:T(8,128)(2,1)S(1)}, u32[]{:S(2)}) copy-start(bf16[256,32,128]{2,1,0:T(8,128)(2,1)S(1)} %shard_map.82) | copy-start | bytes 6291460
  32.4 6.6 %copy-start.4 = (f32[64,256]{1,0:T(8,128)S(1)}, f32[64,256]{1,0:T(8,128)}, u32[]{:S(2)}) copy-start(f32[64,256]{1,0:T(8,128)} %param.12) | copy-start | bytes 196612
  32.4 6.7 %copy-start.5 = (f32[64,128,1]{1,0,2:T(8,128)S(1)}, f32[64,128,1]{1,0,2:T(8,128)}, u32[]{:S(2)}) copy-start(f32[64,128,1]{1,0,2:T(8,128)} %constant.12) | copy-start | bytes 98308
  32.4 7.1 %copy-start.8 = (f32[4]{0:T(128)S(1)}, f32[4]{0:T(128)}, u32[]{:S(2)}) copy-start(f32[4]{0:T(128)} %param.14) | copy-start | bytes 52
  32.4 36.4 %copy-start.3 = (s32[256]{0:T(256)S(1)}, s32[256]{0:T(256)}, u32[]{:S(2)}) copy-start(s32[256]{0:T(256)} %strip.1) | copy-start | bytes 3076
  32.4 36.3 %all-to-all-start = ((bf16[128,64,128]{2,1,0:T(8,128)(2,1)}), bf16[128,64,128]{2,1,0:T(8,128)(2,1)S(1)}, u32[]{:S(2)}, u32[]{:S(2)}) async-start(bf16[128,64,128]{2,1,0:T(8,128)(2,1)} %bitcast.32), calls=%async_computation | async-start | bytes 4194304 | tf_op jit(solution)/shard_map/all_to_all | solution.py:236

commit v2 on v1

v2 whole, which is shorter than its diff:
```python
import jax
import jax.numpy as jnp
import numpy as np
from jax import lax
from jax.experimental import pallas as pl
from jax.experimental.pallas import tpu as pltpu
from jax.sharding import PartitionSpec as P

PC = 64
FIELDS = 4
STEPS = 2
SPREAD = 0.25
LANES = 128
SUB = 8
SLOTS_EACH = 2
ALL = ("axial", "azim")
F32 = jnp.float32
BF16 = jnp.bfloat16
MIB = 2**20


def to_tiles(x):
    n = x.shape[0]
    return x.reshape(n, FIELDS, -1, LANES).transpose(0, 2, 1, 3).reshape(n, -1, LANES)


def from_tiles(x):
    n = x.shape[0]
    return x.reshape(n, -1, FIELDS, LANES).transpose(0, 2, 1, 3).reshape(n, FIELDS, -1)


def iota(shape, dim):
    return lax.broadcasted_iota(jnp.int32, shape, dim)


def dot(a, b):
    return jnp.dot(a, b, preferred_element_type=F32)


def where_one(mask):
    return jnp.where(mask, 1.0, 0.0).astype(BF16)


def edges_kernel(leaf, first, last, sides):
    records, rows, cols = leaf.shape
    half = rows // 2
    pick = iota((records, records * half), 1) - iota((records, records * half), 0) * half
    first[...] = dot(where_one(pick == 0), leaf[:, :half].reshape(-1, cols)).astype(BF16)
    last[...] = dot(where_one(pick == half - 1), leaf[:, half:].reshape(-1, cols)).astype(BF16)
    spot = jnp.where(iota((cols, LANES), 1) // rows % 2 == 0, 0, cols - 1)
    wide = dot(leaf[...].reshape(-1, cols), where_one(iota((cols, LANES), 0) == spot))
    r = iota((records * rows, LANES), 0) % rows
    wide = jnp.where(iota((records * rows, LANES), 1) % rows == r, wide, 0.0).astype(BF16)
    gather = iota((records, records * rows), 1) // rows == iota((records, records * rows), 0)
    sides[...] = dot(where_one(gather), wide).astype(BF16)


def edges(leaf):
    records, rows, cols = leaf.shape
    shapes = [(records, cols), (records, cols), (records, LANES)]
    return pl.pallas_call(
        edges_kernel,
        out_shape=[jax.ShapeDtypeStruct(s, BF16) for s in shapes],
        compiler_params=pltpu.CompilerParams(vmem_limit_bytes=16 * MIB),
        cost_estimate=pl.CostEstimate(flops=10**8, bytes_accessed=MIB, transcendentals=0),
    )(leaf)


def halves(a, b, low, t):
    a, b = a[:, t * LANES : (t + 1) * LANES], b[:, t * LANES : (t + 1) * LANES]
    return jnp.where(low, a, pltpu.roll(b, PC, 1)), jnp.where(low, pltpu.roll(a, PC, 1), b)


def edge_patches(rows, quarters):
    return [
        (r, q) for r in range(rows) for q in range(quarters) if r in (0, rows - 1) or q in (0, quarters - 1)
    ]


def main_kernel(
    target, fields_hbm, leaf_hbm, coupling, sent, rest, fields, leaf, lap, spread, stage, zero, sem, zero_sem, load_sem, leaf_sem
):
    records, rows, cols = leaf.shape
    blocks = rows // SUB
    size = fields.shape[0] // blocks
    leaf_load = pltpu.make_async_copy(leaf_hbm, leaf, leaf_sem)
    leaf_load.start()
    loads = [
        pltpu.make_async_copy(fields_hbm.at[pl.ds(n * size, size)], fields.at[pl.ds(n * size, size)], load_sem.at[n])
        for n in range(blocks)
    ]
    for c in loads:
        c.start()
    half = records // 2
    quarters = cols // PC
    low = iota((half, LANES), 1) < PC

    zero[...] = jnp.zeros_like(zero)
    size = zero.shape[0]
    clears = [
        pltpu.make_async_copy(zero, sent.at[pl.ds(i * size, size)], zero_sem) for i in range(sent.shape[0] // size)
    ]
    for c in clears:
        c.start()

    wide = records * SUB
    lift = where_one(iota((records, wide), 1) // SUB == iota((records, wide), 0))
    lifted = dot(coupling[...], lift)
    within = iota((half, wide), 1) % SUB
    for p in range(2):
        for r in range(SUB):
            part = jnp.where(within == r, lifted[p * half : (p + 1) * half], 0.0)
            at = (p * SUB + r) * half
            spread[at : at + half] = part.astype(BF16)

    leaf_load.wait()
    group = 256 // rows
    a, b = iota((group * rows, group * rows), 0), iota((group * rows, group * rows), 1)
    beside = where_one((jnp.abs(a - b) == 1) & (a // rows == b // rows))
    a, b = iota((cols, cols), 0), iota((cols, cols), 1)
    along = jnp.where(a == b, -4.0, jnp.where(jnp.abs(a - b) == 1, 1.0, 0.0)).astype(BF16)
    for g in range(records // group):
        x = leaf[g * group : (g + 1) * group].reshape(group * rows, cols)
        y = (dot(beside, x) + dot(x, along)).reshape(group, rows, cols)
        for n in range(rows // SUB):
            part = y[:, n * SUB : (n + 1) * SUB].reshape(group * SUB, cols)
            lap[n, g * group * SUB : (g + 1) * group * SUB] = part.astype(BF16)

    for c in clears:
        c.wait()

    edge = {rq: i for i, rq in enumerate(edge_patches(rows, quarters))}
    for n in range(rows // SUB):
        tension = dot(spread[...], lap[n])
        loads[n].wait()
        for k in range(SUB):
            r = n * SUB + k
            a = tension[k * half : (k + 1) * half]
            b = tension[(SUB + k) * half : (SUB + k + 1) * half]
            for t in range(cols // LANES):
                for h, sheet in enumerate(halves(a, b, low, t)):
                    q = 2 * t + h
                    patch = r * quarters + q
                    forced = fields[patch] + sheet
                    if (r, q) in edge:
                        rest[edge[r, q]] = forced
                    else:
                        stage[patch] = forced.astype(BF16)
                        pltpu.make_async_copy(stage.at[patch], sent.at[target[patch]], sem).start()
    count = rows * quarters - len(edge)
    pltpu.make_async_copy(stage.at[pl.ds(0, count)], sent.at[pl.ds(0, count)], sem).wait()


def main_part(target, fields, leaf, coupling, slots):
    records, rows, cols = leaf.shape
    patches, tall, _ = fields.shape
    vmem = pl.BlockSpec(memory_space=pltpu.VMEM)
    hbm = pl.BlockSpec(memory_space=pltpu.HBM)
    count = len(edge_patches(rows, cols // PC))
    return pl.pallas_call(
        main_kernel,
        in_specs=[pl.BlockSpec(memory_space=pltpu.SMEM), hbm, hbm, vmem],
        out_specs=[hbm, vmem],
        out_shape=[
            pltpu.HBM((slots, tall, LANES), BF16),
            jax.ShapeDtypeStruct((count, tall, LANES), F32),
        ],
        scratch_shapes=[
            pltpu.VMEM(fields.shape, F32),
            pltpu.VMEM(leaf.shape, BF16),
            pltpu.VMEM((rows // SUB, records * SUB, cols), BF16),
            pltpu.VMEM((records * SUB, records * SUB), BF16),
            pltpu.VMEM((patches, tall, LANES), BF16),
            pltpu.VMEM((32, tall, LANES), BF16),
            pltpu.SemaphoreType.DMA,
            pltpu.SemaphoreType.DMA,
            pltpu.SemaphoreType.DMA((rows // SUB,)),
            pltpu.SemaphoreType.DMA,
        ],
        compiler_params=pltpu.CompilerParams(vmem_limit_bytes=24 * MIB),
        cost_estimate=pl.CostEstimate(flops=2 * 10**9, bytes_accessed=8 * MIB, transcendentals=0),
    )(target, fields, leaf, coupling)


def edge_kernel(target, rest, coupling, above, below, left, right, sent_in, sent, stage, sem):
    del sent_in
    records, cols = above.shape
    half = records // 2
    quarters = cols // PC
    rows = LANES // 4
    low = iota((half, LANES), 1) < PC

    lane = iota((records, LANES), 1)
    near = jnp.where(lane // rows % 2 == 0, right[...].astype(F32), left[...].astype(F32)).astype(BF16)
    both = dot(coupling[...], near)
    both = jnp.where(low, both[:half], both[half:])
    lane = iota((half, LANES), 1)
    column = jnp.concatenate([jnp.where(lane % rows == r, both, 0.0) for r in range(rows)], axis=0)
    high = column.astype(BF16)
    split = jnp.concatenate([high, (column - high.astype(F32)).astype(BF16)], axis=1)
    a, b = iota((2 * LANES, 2 * LANES), 0), iota((2 * LANES, 2 * LANES), 1)
    p, s = a // PC % 2, a // rows % 2
    split = dot(split, where_one(b == jnp.where(s == 1, p * PC, LANES + p * PC + PC - 1)))

    ends = {}
    for r, row in ((0, above), (rows - 1, below)):
        whole = dot(coupling[...], row[...])
        for t in range(cols // LANES):
            for h, sheet in enumerate(halves(whole[:half], whole[half:], low, t)):
                ends[r, 2 * t + h] = sheet

    listed = edge_patches(rows, quarters)
    for i, (r, q) in enumerate(listed):
        forced = rest[i]
        if q == 0:
            forced = forced + split[r * half : (r + 1) * half, :LANES]
        if q == quarters - 1:
            forced = forced + split[r * half : (r + 1) * half, LANES:]
        if (r, q) in ends:
            forced = forced + ends[r, q]
        stage[i] = forced.astype(BF16)
        pltpu.make_async_copy(stage.at[i], sent.at[target[r * quarters + q]], sem).start()
    count = len(listed)
    pltpu.make_async_copy(stage, sent.at[pl.ds(0, count)], sem).wait()


def edge_part(target, rest, coupling, above, below, left, right, sent):
    vmem = pl.BlockSpec(memory_space=pltpu.VMEM)
    return pl.pallas_call(
        edge_kernel,
        in_specs=[pl.BlockSpec(memory_space=pltpu.SMEM)] + [vmem] * 6 + [pl.BlockSpec(memory_space=pltpu.HBM)],
        out_specs=pl.BlockSpec(memory_space=pltpu.HBM),
        out_shape=pltpu.HBM(sent.shape, sent.dtype),
        scratch_shapes=[pltpu.VMEM(rest.shape, BF16), pltpu.SemaphoreType.DMA],
        input_output_aliases={7: 0},
        compiler_params=pltpu.CompilerParams(vmem_limit_bytes=16 * MIB),
        cost_estimate=pl.CostEstimate(flops=2 * 10**8, bytes_accessed=2 * MIB, transcendentals=0),
    )(target, rest, coupling, above, below, left, right, sent)


def sweep_kernel(strip, state, ghosts, rate, shift, out):
    block = pl.program_id(0)
    count, tall, _ = state.shape
    lane = iota((SUB, LANES), 1)
    row = iota((SUB, LANES), 0)
    first = (lane < PC) & (row < FIELDS)
    last = (lane >= PC) & (row >= FIELDS)
    v = rate[...]
    tiles = tall // SUB
    chunk = 8

    def sweep(x, g, y):
        flat = [y[k * SUB : (k + 1) * SUB, :LANES] for k in range(tiles)]
        across = [y[k * SUB : (k + 1) * SUB, LANES:] for k in range(tiles)]
        ext = [g] + [pltpu.roll(z, FIELDS, 0) for z in across] + [g]
        new = []
        for k in range(tiles):
            vertical = jnp.where(first, ext[k], jnp.where(last, ext[k + 2], ext[k + 1]))
            new.append(x[k] + v * ((flat[k] + across[k]) + vertical))
        return new

    for c in range(count // chunk):
        slots = range(c * chunk, (c + 1) * chunk)
        x = state[c * chunk : (c + 1) * chunk].reshape(chunk * tall, LANES)
        y = dot(x, shift[:LANES])
        xs = []
        gs = []
        for i, s in enumerate(slots):
            gs.append(ghosts[strip[block * count + s]])
            mine = x[i * tall : (i + 1) * tall].astype(F32)
            mine = [mine[k * SUB : (k + 1) * SUB] for k in range(tiles)]
            xs.append(sweep(mine, gs[i], y[i * tall : (i + 1) * tall]))
        for step in range(STEPS - 1):
            flat = jnp.concatenate([z for mine in xs for z in mine], axis=0)
            high = flat.astype(BF16)
            y = dot(jnp.concatenate([high, (flat - high.astype(F32)).astype(BF16)], axis=1), shift[...])
            xs = [sweep(xs[i], gs[i], y[i * tall : (i + 1) * tall]) for i in range(chunk)]
        for i, s in enumerate(slots):
            for k in range(tiles):
                out[s, k * SUB : (k + 1) * SUB] = xs[i][k]


def shift_table():
    table = np.zeros((LANES, 2 * LANES), np.float32)
    for i in range(LANES):
        table[i, i] = -4.0
        for j in (i - 1, i + 1):
            if 0 <= j and j // PC == i // PC:
                table[i, j] = 1.0
        table[i, LANES + (i + PC) % LANES] = 1.0
    return np.concatenate([table, table], axis=0)


def sweeps(strip, state, ghosts, rate):
    slots, rows, _ = state.shape
    count = 32
    whole = lambda *shape: pl.BlockSpec(shape, lambda b, *_: (0,) * len(shape))
    return pl.pallas_call(
        sweep_kernel,
        grid_spec=pltpu.PrefetchScalarGridSpec(
            num_scalar_prefetch=1,
            grid=(slots // count,),
            in_specs=[
                pl.BlockSpec((count, rows, LANES), lambda b, *_: (b, 0, 0)),
                whole(*ghosts.shape),
                whole(SUB, LANES),
                whole(2 * LANES, 2 * LANES),
            ],
            out_specs=pl.BlockSpec((count, rows, LANES), lambda b, *_: (b, 0, 0)),
        ),
        out_shape=jax.ShapeDtypeStruct((slots, rows, LANES), F32),
        compiler_params=pltpu.CompilerParams(vmem_limit_bytes=24 * MIB),
    )(strip, state, ghosts, rate, jnp.asarray(shift_table(), BF16))


def interp_table():
    coarse = PC // 2
    table = np.zeros((2, coarse, 2, PC), np.float32)
    for side in range(2):
        for c in range(PC):
            near = c // 2
            second = max(near - 1, 0) if c % 2 == 0 else min(near + 1, coarse - 1)
            table[side, near, side, c] += 0.75
            table[side, second, side, c] += 0.25
    return table.reshape(2 * coarse, 2 * PC)


def shards(fields, new_owner, leaflet, stiffness, coarse, coarse_of_slot, viscosity):
    devices = lax.axis_size("axial") * lax.axis_size("azim")
    patch_count = fields.shape[0]
    slots = devices * SLOTS_EACH
    records = leaflet.shape[0]

    first, last, sides = edges(leaflet)
    size = lax.axis_size("axial")
    up = [(i, i + 1) for i in range(size - 1)]
    above = lax.ppermute(last, "axial", up)
    below = lax.ppermute(first, "axial", [(j, i) for i, j in up])
    size = lax.axis_size("azim")
    around = [(i, (i + 1) % size) for i in range(size)]
    left = lax.ppermute(sides, "azim", around)
    right = lax.ppermute(sides, "azim", [(j, i) for i, j in around])

    owners = new_owner[:, 0]
    position = jnp.arange(patch_count)
    earlier = (owners[:, None] == owners[None, :]) & (position[None, :] < position[:, None])
    ranked = jnp.sum(earlier.astype(jnp.int32), axis=1)
    target = owners * SLOTS_EACH + ranked

    coupling = (
        (stiffness * SPREAD).reshape(FIELDS, -1, 2, records).transpose(2, 1, 0, 3).reshape(records, records)
    )
    hbm = lambda x: pltpu.with_memory_space_constraint(x, pltpu.HBM)
    sent, rest = main_part(target, hbm(to_tiles(fields)), hbm(leaflet), coupling, slots)
    sent = edge_part(target, rest, coupling, above, below, left, right, sent)
    arrived = lax.all_to_all(sent.reshape(devices, -1, LANES), ALL, split_axis=0, concat_axis=0, tiled=True)
    state = arrived.reshape(slots, -1, LANES)

    strips = coarse.shape[0]
    ghosts = jnp.dot(
        coarse.reshape(strips * FIELDS, -1), jnp.asarray(interp_table()), precision=lax.Precision.HIGHEST
    ).reshape(strips, FIELDS, LANES)
    ghosts = jnp.concatenate([ghosts, ghosts], axis=1)
    rate = jnp.broadcast_to(jnp.concatenate([viscosity, viscosity])[:, None], (SUB, LANES))
    return from_tiles(sweeps(coarse_of_slot, state, ghosts, rate))


def solution(mesh):
    placed = (
        P(ALL, None, None),
        P(ALL, None),
        P(None, "axial", "azim"),
        P(),
        P(ALL, None),
        P(ALL),
        P(),
    )
    return jax.shard_map(
        shards,
        mesh=mesh,
        in_specs=placed,
        out_specs=P(ALL, None, None),
        check_vma=False,
    )
```

time: 83.8 us -> 71.4 us (0.85)
  local copies, waits for them, and re-layouts: 8.31 us -> 1.54 us
  Pallas kernels: 21.1 us -> 15.5 us
  waiting for transfers between devices: 34.7 us -> 29.1 us
  starting transfers between devices: 18.5 us -> 22 us
  other arithmetic: 0.38 us -> 2.41 us
    pallas_call x1, Pallas kernels: 14.6 us -> 6.62 us  [sweeps(): pl.pallas_call(sweep_kernel, grid_spec=pltpu.PrefetchScalarGridSpec(num_s...]
    ppermute x4, waiting for transfers between devices: 5.58 us -> 0.01 us  [the longest x1 0.01 us: shards(): left = lax.ppermute(sides, 'azim', around)]
    slice x2 -> x0, local copies, waits for them, and re-layouts: 3.64 us -> none  [the longest x1 2.35 us: shards(): left, right = halo(leaflet[:, :, 0], leaflet[:, :, cols - 1], 'azim', True)]
    all_to_all x1, starting transfers between devices: 6.55 us -> 9.89 us  [shards(): lax.all_to_all(sent.reshape(devices, -1, LANES), ALL, split_axis=0, conca...]
    unnamed x22 -> x12, local copies, waits for them, and re-layouts: 4.31 us -> 1.26 us
    pallas_call x1 -> x3, Pallas kernels: 6.5 us -> 8.84 us  [the longest x1 6.09 us: main_part(): pl.pallas_call(main_kernel, in_specs=[pl.BlockSpec(memory_space=pltpu.SME...]
  transfers between devices with their start and end apart: 5 -> 5, of which waited for: 2 -> 1; matrix products, arithmetic and copies ran while one was open for 7% -> 4% of each run, Pallas kernels for 0% -> 9%
where the time goes in v2:
time: 71.4 us; the launch traced here: 71 us
  waiting for transfers between devices  29.1 us (41%)
  starting transfers between devices  22 us (31%)
  Pallas kernels  15.5 us (22%)
  other arithmetic  2.41 us (3%)
  local copies, waits for them, and re-layouts  1.54 us (2%)
    all_to_all x1, waiting for transfers between devices, shards(): lax.all_to_all(sent.reshape(devices, -1, LANES), ALL, split_axis=0, conca...  29.1 us
    all_to_all x1, starting transfers between devices, shards(): lax.all_to_all(sent.reshape(devices, -1, LANES), ALL, split_axis=0, conca...  9.89 us
    pallas_call x1, Pallas kernels, sweeps(): pl.pallas_call(sweep_kernel, grid_spec=pltpu.PrefetchScalarGridSpec(num_s...  6.62 us
    pallas_call x1, Pallas kernels, main_part(): pl.pallas_call(main_kernel, in_specs=[pl.BlockSpec(memory_space=pltpu.SME...  6.09 us
    ppermute x1, starting transfers between devices, shards(): right = lax.ppermute(sides, 'azim', [(j, i) for i, j in around])  5.83 us
    ppermute x1, starting transfers between devices, shards(): above = lax.ppermute(last, 'axial', up)  4.38 us
    ppermute x1, starting transfers between devices, shards(): below = lax.ppermute(first, 'axial', [(j, i) for i, j in up])  1.92 us
    pallas_call x1, Pallas kernels, edge_part(): pl.pallas_call(edge_kernel, in_specs=[pl.BlockSpec(memory_space=pltpu.SME...  1.89 us
  transfers between devices with their start and end apart: 5, of which 1 were waited for; matrix products, arithmetic and copies ran while one was open for 4% of the time, Pallas kernels for 9%

profile of v2, /device:TPU:1, one launch (start us, length us, event | category | flops | bytes accessed | tf_op | source)
XLA Modules:
  0.0 71.0 jit_solution(17631248100772591761)
XLA Ops:
  0.0 1.2 %copy-done = bf16[64,32,256]{2,1,0:T(8,128)(2,1)S(1)} copy-done((bf16[64,32,256]{2,1,0:T(8,128)(2,1)S(1)}, bf16[64,32,256]{2,1,0:T(8,128)(2,1)}, u32[]{:S(2)}) %copy-start) | copy-done | bytes 1048600
  1.2 0.9 %shard_map.92 = (bf16[64,256]{1,0:T(8,128)(2,1)S(1)}, bf16[64,256]{1,0:T(8,128)(2,1)S(1)}, bf16[64,128]{1,0:T(8,128)(2,1)S(1)}) custom-call(bf16[64,32,256]{2,1,0:T(8,128)(2,1)S(1)} %copy-done), custom_call_target="tpu_custom_call" | custom-call | flops 100000000 | bytes 1048576 | tf_op jit(solution)/shard_map/pallas_call | solution.py:61
  2.1 5.8 %collective-permute-start.3 = (bf16[64,128]{1,0:T(8,128)(2,1)S(1)}, bf16[64,128]{1,0:T(8,128)(2,1)S(1)}, u32[]{:S(2)}, u32[]{:S(2)}) collective-permute-start(bf16[64,128]{1,0:T(8,128)(2,1)S(1)} %get-tuple-element.13), channel_id=1, source_target_pairs={{1,0},{2,1},{3,2},{4,3},{5,4},{6,5},{7,6},{8,7},{9,8},{10,9},{11,1... | collective-permute-start | bytes 49160 | tf_op jit(solution)/shard_map/ppermute | solution.py:342
  7.9 0.0 collective-permute-start.2
  7.9 4.4 %collective-permute-start = (bf16[64,256]{1,0:T(8,128)(2,1)S(1)}, bf16[64,256]{1,0:T(8,128)(2,1)S(1)}, u32[]{:S(2)}, u32[]{:S(2)}) collective-permute-start(bf16[64,256]{1,0:T(8,128)(2,1)S(1)} %get-tuple-element.11), channel_id=1, source_target_pairs={{0,16},{16,32},{32,48},{48,64},{64,80},{80,96},{96,112},{1,17},{17... | collective-permute-start | bytes 98312 | tf_op jit(solution)/shard_map/ppermute | solution.py:337
  12.3 1.9 %collective-permute-start.1 = (bf16[64,256]{1,0:T(8,128)(2,1)S(1)}, bf16[64,256]{1,0:T(8,128)(2,1)S(1)}, u32[]{:S(2)}, u32[]{:S(2)}) collective-permute-start(bf16[64,256]{1,0:T(8,128)(2,1)S(1)} %get-tuple-element.12), channel_id=1, source_target_pairs={{16,0},{32,16},{48,32},{64,48},{80,64},{96,80},{112,96},{17,1},{33... | collective-permute-start | bytes 98312 | tf_op jit(solution)/shard_map/ppermute | solution.py:338
  14.2 0.9 %convert_reduce_fusion = s32[128]{0:T(128)S(1)} fusion(s32[128]{0:T(128)} %bitcast.30), kind=kLoop, calls=%fused_computation.4 | loop fusion | flops 81792 | bytes 1024 | tf_op jit(solution)/shard_map/reduce_sum | solution.py:347
  15.2 0.7 multiply_add_fusion.target
  15.8 0.7 %broadcast_multiply_fusion = bf16[64,64]{1,0:T(8,128)(2,1)S(1)} fusion(bf16[64,64]{1,0:T(8,128)(2,1)} %param.12), kind=kLoop, calls=%fused_computation.7 | loop fusion | flops 4096 | bytes 16384 | tf_op jit(solution)/shard_map/mul | solution.py:351
  16.5 6.1 %shard_map.91 = (bf16[256,32,128]{2,1,0:T(8,128)(2,1)}, f32[68,32,128]{2,1,0:T(8,128)S(1)}) custom-call(s32[128]{0:T(128)S(1)} %multiply_add_fusion.target, f32[128,32,128]{2,1,0:T(8,128)} %bitcast.29, bf16[64,32,256]{2,1,0:T(8,128)(2,1)} %leaf.1, bf16[64,64]{1,0:T(8,128)(2,1)S(1)} %bitcast.24), custom_call_target="tpu_custom_call" | custom-call | flops 2000000000 | bytes 8388608 | tf_op jit(solution)/shard_map/pallas_call | solution.py:160
  22.7 1.9 %shard_map.93 = bf16[256,32,128]{2,1,0:T(8,128)(2,1)} custom-call(s32[128]{0:T(128)S(1)} %multiply_add_fusion.target, f32[68,32,128]{2,1,0:T(8,128)S(1)} %get-tuple-element.10.rest, bf16[64,64]{1,0:T(8,128)(2,1)S(1)} %bitcast.25, bf16[64,256]{1,0:T(8,128)(2,1)S(1)} %collective-permute-done.above, ...), custom_call_target="tpu_custom_call", output_to_operand_aliasing={{}: (7, {})} | custom-call | flops 200000000 | bytes 2097152 | tf_op jit(solution)/shard_map/pallas_call | solution.py:229
  24.6 0.0 copy-start.3
  24.6 0.0 copy-start.4
  24.6 0.0 copy-start.5
  24.6 0.0 copy-start.1
  24.6 0.0 copy-start.2
  24.6 9.9 %all-to-all-start = ((bf16[128,64,128]{2,1,0:T(8,128)(2,1)}), bf16[128,64,128]{2,1,0:T(8,128)(2,1)S(1)}, u32[]{:S(2)}, u32[]{:S(2)}) async-start(bf16[128,64,128]{2,1,0:T(8,128)(2,1)} %bitcast.26), calls=%async_computation | async-start | bytes 4194304 | tf_op jit(solution)/shard_map/all_to_all | solution.py:356
  34.6 0.1 dot_general.5
  34.7 0.2 fusion
  34.9 0.1 copy.24
  35.0 0.1 pad_maximum_fusion.1
  35.2 29.1 %all-to-all-done = bf16[128,64,128]{2,1,0:T(8,128)(2,1)S(1)} async-done(((bf16[128,64,128]{2,1,0:T(8,128)(2,1)}), bf16[128,64,128]{2,1,0:T(8,128)(2,1)S(1)}, u32[]{:S(2)}, u32[]{:S(2)}) %all-to-all-start) | async-done | bytes 2097184 | tf_op jit(solution)/shard_map/all_to_all | solution.py:356
  64.3 0.1 broadcast_in_dim.2.rate
  64.4 6.6 %shard_map.94 = f32[256,32,128]{2,1,0:T(8,128)} custom-call(s32[256]{0:T(256)S(1)} %copy-done.2, bf16[256,32,128]{2,1,0:T(8,128)(2,1)S(1)} %bitcast.23, f32[64,8,128]{2,1,0:T(8,128)S(1)} %pad_maximum_fusion.ghosts, f32[8,128]{1,0:T(8,128)S(1)} %broadcast_in_dim.2.rate, bf16[256,256]{1,0:T(8,128)(2,1)S(1)} %copy-done.1), custom_call_target="tpu_custom_call" | custom-call | tf_op jit(solution)/shard_map/pallas_call | solution.py:298
  (12 shorter events, 0.1 us)
Async XLA Ops:
  0.0 1.2 %copy-start = (bf16[64,32,256]{2,1,0:T(8,128)(2,1)S(1)}, bf16[64,32,256]{2,1,0:T(8,128)(2,1)}, u32[]{:S(2)}) copy-start(bf16[64,32,256]{2,1,0:T(8,128)(2,1)} %leaf.1) | copy-start | bytes 3145732
  2.1 20.5 %collective-permute-start.3 = (bf16[64,128]{1,0:T(8,128)(2,1)S(1)}, bf16[64,128]{1,0:T(8,128)(2,1)S(1)}, u32[]{:S(2)}, u32[]{:S(2)}) collective-permute-start(bf16[64,128]{1,0:T(8,128)(2,1)S(1)} %get-tuple-element.13), channel_id=1, source_target_pairs={{1,0},{2,1},{3,2},{4,3},{5,4},{6,5},{7,6},{8,7},{9,8},{10,9},{11,1... | collective-permute-start | bytes 49160 | tf_op jit(solution)/shard_map/ppermute | solution.py:342
  7.9 14.7 %collective-permute-start.2 = (bf16[64,128]{1,0:T(8,128)(2,1)S(1)}, bf16[64,128]{1,0:T(8,128)(2,1)S(1)}, u32[]{:S(2)}, u32[]{:S(2)}) collective-permute-start(bf16[64,128]{1,0:T(8,128)(2,1)S(1)} %get-tuple-element.13), channel_id=1, source_target_pairs={{0,1},{1,2},{2,3},{3,4},{4,5},{5,6},{6,7},{7,8},{8,9},{9,10},{10,1... | collective-permute-start | bytes 49160 | tf_op jit(solution)/shard_map/ppermute | solution.py:341
  7.9 14.7 %collective-permute-start = (bf16[64,256]{1,0:T(8,128)(2,1)S(1)}, bf16[64,256]{1,0:T(8,128)(2,1)S(1)}, u32[]{:S(2)}, u32[]{:S(2)}) collective-permute-start(bf16[64,256]{1,0:T(8,128)(2,1)S(1)} %get-tuple-element.11), channel_id=1, source_target_pairs={{0,16},{16,32},{32,48},{48,64},{64,80},{80,96},{96,112},{1,17},{17... | collective-permute-start | bytes 98312 | tf_op jit(solution)/shard_map/ppermute | solution.py:337
  12.3 10.4 %collective-permute-start.1 = (bf16[64,256]{1,0:T(8,128)(2,1)S(1)}, bf16[64,256]{1,0:T(8,128)(2,1)S(1)}, u32[]{:S(2)}, u32[]{:S(2)}) collective-permute-start(bf16[64,256]{1,0:T(8,128)(2,1)S(1)} %get-tuple-element.12), channel_id=1, source_target_pairs={{16,0},{32,16},{48,32},{64,48},{80,64},{96,80},{112,96},{17,1},{33... | collective-permute-start | bytes 98312 | tf_op jit(solution)/shard_map/ppermute | solution.py:338
  24.6 10.0 %copy-start.3 = (f32[64,256]{1,0:T(8,128)S(1)}, f32[64,256]{1,0:T(8,128)}, u32[]{:S(2)}) copy-start(f32[64,256]{1,0:T(8,128)} %param.13) | copy-start | bytes 196612
  24.6 10.1 %copy-start.4 = (f32[64,128,1]{1,0,2:T(8,128)S(1)}, f32[64,128,1]{1,0,2:T(8,128)}, u32[]{:S(2)}) copy-start(f32[64,128,1]{1,0,2:T(8,128)} %constant.13) | copy-start | bytes 98308
  24.6 10.4 %copy-start.5 = (f32[4]{0:T(128)S(1)}, f32[4]{0:T(128)}, u32[]{:S(2)}) copy-start(f32[4]{0:T(128)} %param.15) | copy-start | bytes 52
  24.6 39.8 %copy-start.1 = (bf16[256,256]{1,0:T(8,128)(2,1)S(1)}, bf16[256,256]{1,0:T(8,128)(2,1)}, u32[]{:S(2)}) copy-start(bf16[256,256]{1,0:T(8,128)(2,1)} %constant.11.clone.shift) | copy-start | bytes 393220
  24.6 39.8 %copy-start.2 = (s32[256]{0:T(256)S(1)}, s32[256]{0:T(256)}, u32[]{:S(2)}) copy-start(s32[256]{0:T(256)} %strip.1) | copy-start | bytes 3076
  24.6 39.7 %all-to-all-start = ((bf16[128,64,128]{2,1,0:T(8,128)(2,1)}), bf16[128,64,128]{2,1,0:T(8,128)(2,1)S(1)}, u32[]{:S(2)}, u32[]{:S(2)}) async-start(bf16[128,64,128]{2,1,0:T(8,128)(2,1)} %bitcast.26), calls=%async_computation | async-start | bytes 4194304 | tf_op jit(solution)/shard_map/all_to_all | solution.py:356

commit v3 on v2

v3 whole, which is shorter than its diff:
```python
import functools

import jax
import jax.numpy as jnp
import numpy as np
from jax import lax
from jax.experimental import pallas as pl
from jax.experimental.pallas import tpu as pltpu
from jax.sharding import PartitionSpec as P

PC = 64
FIELDS = 4
STEPS = 2
SPREAD = 0.25
LANES = 128
SUB = 8
SLOTS_EACH = 2
ALL = ("axial", "azim")
F32 = jnp.float32
BF16 = jnp.bfloat16
MIB = 2**20


def to_tiles(x):
    n = x.shape[0]
    return x.reshape(n, FIELDS, -1, LANES).transpose(0, 2, 1, 3).reshape(n, -1, LANES)


def from_tiles(x):
    n = x.shape[0]
    return x.reshape(n, -1, FIELDS, LANES).transpose(0, 2, 1, 3).reshape(n, FIELDS, -1)


def iota(shape, dim):
    return lax.broadcasted_iota(jnp.int32, shape, dim)


def dot(a, b):
    return jnp.dot(a, b, preferred_element_type=F32)


def in_hbm(x):
    return pltpu.with_memory_space_constraint(x, pltpu.HBM)


def where_one(mask):
    return jnp.where(mask, 1.0, 0.0).astype(BF16)


def edges_kernel(leaf_hbm, leaf, first, last, sides, sent, zero, load_sem, zero_sem):
    records, rows, cols = leaf.shape
    size = 16
    loads = []
    for n in range(records // size):
        part = pl.ds(n * size, size)
        loads.append(pltpu.make_async_copy(leaf_hbm.at[part], leaf.at[part], load_sem.at[n]))
        loads[n].start()
    zero[...] = jnp.zeros_like(zero)
    count = zero.shape[0]
    clears = [
        pltpu.make_async_copy(zero, sent.at[pl.ds(i * count, count)], zero_sem) for i in range(sent.shape[0] // count)
    ]
    for c in clears:
        c.start()

    a, b = iota((2 * size, size * rows), 0), iota((2 * size, size * rows), 1)
    ends = where_one(b == a % size * rows + a // size * (rows - 1))
    spot = jnp.where(iota((cols, LANES), 1) // rows % 2 == 0, 0, cols - 1)
    spot = where_one(iota((cols, LANES), 0) == spot)
    mine = iota((size * rows, LANES), 1) % rows == iota((size * rows, LANES), 0) % rows
    gather = where_one(iota((size, size * rows), 1) // rows == iota((size, size * rows), 0))
    for n in range(records // size):
        loads[n].wait()
        part = slice(n * size, (n + 1) * size)
        x = leaf[part].reshape(size * rows, cols)
        both = dot(ends, x).astype(BF16)
        first[part] = both[:size]
        last[part] = both[size:]
        sides[part] = dot(gather, jnp.where(mine, dot(x, spot), 0.0).astype(BF16)).astype(BF16)
    for c in clears:
        c.wait()


def edges(leaf, slots):
    records, rows, cols = leaf.shape
    vmem = pl.BlockSpec(memory_space=pltpu.VMEM)
    hbm = pl.BlockSpec(memory_space=pltpu.HBM)
    shapes = [leaf.shape, (records, cols), (records, cols), (records, LANES)]
    tile = (records // 2, LANES)
    return pl.pallas_call(
        edges_kernel,
        in_specs=[hbm],
        out_specs=[vmem] * 4 + [hbm],
        out_shape=[pltpu.VMEM(s, BF16) for s in shapes] + [pltpu.HBM((slots,) + tile, BF16)],
        scratch_shapes=[
            pltpu.VMEM((32,) + tile, BF16),
            pltpu.SemaphoreType.DMA((records // 16,)),
            pltpu.SemaphoreType.DMA,
        ],
        compiler_params=pltpu.CompilerParams(vmem_limit_bytes=16 * MIB),
        cost_estimate=pl.CostEstimate(flops=10**8, bytes_accessed=MIB, transcendentals=0),
    )(in_hbm(leaf))


def prepare_kernel(owner, stiffness, target, coupling, spread):
    devices, patches = LANES, owner.shape[1]
    mine = owner[...] == iota((devices, patches), 0)
    before = where_one(iota((patches, patches), 0) < iota((patches, patches), 1))
    earlier = dot(where_one(mine), before)
    ranked = jnp.sum(jnp.where(mine, earlier, 0.0), axis=0, keepdims=True)
    target[...] = owner[...] * SLOTS_EACH + ranked.astype(jnp.int32)

    records = stiffness.shape[0]
    half = records // 2
    a, b = iota((records, records), 0), iota((records, records), 1)
    old = a % FIELDS * (records // FIELDS) + a % half // FIELDS * 2 + a // half
    ordered = (dot(where_one(b == old), stiffness[...]) * SPREAD).astype(BF16)
    coupling[...] = ordered

    wide = records * SUB
    lift = where_one(iota((records, wide), 1) // SUB == iota((records, wide), 0))
    lifted = dot(ordered, lift)
    within = iota((half, wide), 1) % SUB
    for p in range(2):
        for r in range(SUB):
            part = jnp.where(within == r, lifted[p * half : (p + 1) * half], 0.0)
            at = (p * SUB + r) * half
            spread[at : at + half] = part.astype(BF16)


def prepare(owner, stiffness):
    vmem = pl.BlockSpec(memory_space=pltpu.VMEM)
    records = stiffness.shape[0]
    return pl.pallas_call(
        prepare_kernel,
        in_specs=[vmem] * 2,
        out_specs=[vmem] * 3,
        out_shape=[
            jax.ShapeDtypeStruct(owner.shape, jnp.int32),
            pltpu.VMEM((records, records), BF16),
            pltpu.VMEM((records * SUB, records * SUB), BF16),
        ],
        compiler_params=pltpu.CompilerParams(vmem_limit_bytes=16 * MIB),
        cost_estimate=pl.CostEstimate(flops=10**8, bytes_accessed=MIB, transcendentals=0),
    )(owner, stiffness)


def laplace_kernel(fields_hbm, leaf, fields, lap, sem):
    load = pltpu.make_async_copy(fields_hbm, fields, sem)
    load.start()
    records, rows, cols = leaf.shape
    group = 256 // rows
    a, b = iota((group * rows, group * rows), 0), iota((group * rows, group * rows), 1)
    beside = where_one((jnp.abs(a - b) == 1) & (a // rows == b // rows))
    a, b = iota((cols, cols), 0), iota((cols, cols), 1)
    along = jnp.where(a == b, -4.0, jnp.where(jnp.abs(a - b) == 1, 1.0, 0.0)).astype(BF16)
    for g in range(records // group):
        x = leaf[g * group : (g + 1) * group].reshape(group * rows, cols)
        y = (dot(beside, x) + dot(x, along)).reshape(group, rows, cols)
        for n in range(rows // SUB):
            part = y[:, n * SUB : (n + 1) * SUB].reshape(group * SUB, cols)
            lap[n, g * group * SUB : (g + 1) * group * SUB] = part.astype(BF16)
    load.wait()


def laplace(fields, leaf):
    records, rows, cols = leaf.shape
    vmem = pl.BlockSpec(memory_space=pltpu.VMEM)
    hbm = pl.BlockSpec(memory_space=pltpu.HBM)
    return pl.pallas_call(
        laplace_kernel,
        in_specs=[hbm, vmem],
        out_specs=[vmem] * 2,
        out_shape=[
            pltpu.VMEM(fields.shape, F32),
            pltpu.VMEM((rows // SUB, records * SUB, cols), BF16),
        ],
        scratch_shapes=[pltpu.SemaphoreType.DMA],
        compiler_params=pltpu.CompilerParams(vmem_limit_bytes=16 * MIB),
        cost_estimate=pl.CostEstimate(flops=5 * 10**8, bytes_accessed=3 * MIB, transcendentals=0),
    )(in_hbm(fields), leaf)


def halves(a, b, low, t):
    a, b = a[:, t * LANES : (t + 1) * LANES], b[:, t * LANES : (t + 1) * LANES]
    return jnp.where(low, a, pltpu.roll(b, PC, 1)), jnp.where(low, pltpu.roll(a, PC, 1), b)


def edge_patches(rows, quarters, span):
    ends = (0, rows - 1)
    return [
        (r, q) for r in range(rows) for q in range(quarters) if r // SUB in span and (r in ends or q in (0, quarters - 1))
    ]


def main_kernel(span, target, fields, lap, spread, sent_in, sent, rest, stage, sem):
    del sent_in
    blocks, _, cols = lap.shape
    half = fields.shape[1]
    rows = blocks * SUB
    quarters = cols // PC
    low = iota((half, LANES), 1) < PC
    listed = edge_patches(rows, quarters, span)
    edge = {rq: i for i, rq in enumerate(listed)}
    for n in span:
        tension = dot(spread[...], lap[n])
        for k in range(SUB):
            r = n * SUB + k
            a = tension[k * half : (k + 1) * half]
            b = tension[(SUB + k) * half : (SUB + k + 1) * half]
            for t in range(cols // LANES):
                for h, sheet in enumerate(halves(a, b, low, t)):
                    q = 2 * t + h
                    patch = r * quarters + q
                    forced = fields[patch] + sheet
                    if (r, q) in edge:
                        rest[edge[r, q]] = forced
                    else:
                        stage[patch] = forced.astype(BF16)
                        pltpu.make_async_copy(stage.at[patch], sent.at[target[0, patch]], sem).start()
    count = len(span) * SUB * quarters - len(edge)
    pltpu.make_async_copy(stage.at[pl.ds(0, count)], sent.at[pl.ds(0, count)], sem).wait()


def main_part(span, target, fields, lap, spread, sent):
    patches, tall, _ = fields.shape
    blocks, _, cols = lap.shape
    vmem = pl.BlockSpec(memory_space=pltpu.VMEM)
    hbm = pl.BlockSpec(memory_space=pltpu.HBM)
    count = len(edge_patches(blocks * SUB, cols // PC, span))
    return pl.pallas_call(
        functools.partial(main_kernel, span),
        in_specs=[pl.BlockSpec(memory_space=pltpu.SMEM), vmem, vmem, vmem, hbm],
        out_specs=[hbm, vmem],
        out_shape=[pltpu.HBM(sent.shape, BF16), pltpu.VMEM((count, tall, LANES), F32)],
        scratch_shapes=[pltpu.VMEM((patches, tall, LANES), BF16), pltpu.SemaphoreType.DMA],
        input_output_aliases={4: 0},
        compiler_params=pltpu.CompilerParams(vmem_limit_bytes=16 * MIB),
        cost_estimate=pl.CostEstimate(flops=10**9, bytes_accessed=4 * MIB, transcendentals=0),
    )(target, fields, lap, spread, sent)


def edge_kernel(target, rest_low, rest_high, coupling, above, below, left, right, sent_in, sent, stage, sem):
    del sent_in
    records, cols = above.shape
    half = records // 2
    quarters = cols // PC
    rows = LANES // 4
    low = iota((half, LANES), 1) < PC

    lane = iota((records, LANES), 1)
    near = jnp.where(lane // rows % 2 == 0, right[...].astype(F32), left[...].astype(F32)).astype(BF16)
    both = dot(coupling[...], near)
    both = jnp.where(low, both[:half], both[half:])
    lane = iota((half, LANES), 1)
    column = jnp.concatenate([jnp.where(lane % rows == r, both, 0.0) for r in range(rows)], axis=0)
    high = column.astype(BF16)
    split = jnp.concatenate([high, (column - high.astype(F32)).astype(BF16)], axis=1)
    a, b = iota((2 * LANES, 2 * LANES), 0), iota((2 * LANES, 2 * LANES), 1)
    p, s = a // PC % 2, a // rows % 2
    split = dot(split, where_one(b == jnp.where(s == 1, p * PC, LANES + p * PC + PC - 1)))

    ends = {}
    for r, row in ((0, above), (rows - 1, below)):
        whole = dot(coupling[...], row[...])
        for t in range(cols // LANES):
            for h, sheet in enumerate(halves(whole[:half], whole[half:], low, t)):
                ends[r, 2 * t + h] = sheet

    listed = edge_patches(rows, quarters, range(rows // SUB))
    for i, (r, q) in enumerate(listed):
        forced = rest_low[i] if i < rest_low.shape[0] else rest_high[i - rest_low.shape[0]]
        if q == 0:
            forced = forced + split[r * half : (r + 1) * half, :LANES]
        if q == quarters - 1:
            forced = forced + split[r * half : (r + 1) * half, LANES:]
        if (r, q) in ends:
            forced = forced + ends[r, q]
        stage[i] = forced.astype(BF16)
        pltpu.make_async_copy(stage.at[i], sent.at[target[0, r * quarters + q]], sem).start()
    count = len(listed)
    pltpu.make_async_copy(stage, sent.at[pl.ds(0, count)], sem).wait()


def edge_part(target, rest_low, rest_high, coupling, above, below, left, right, sent):
    vmem = pl.BlockSpec(memory_space=pltpu.VMEM)
    return pl.pallas_call(
        edge_kernel,
        in_specs=[pl.BlockSpec(memory_space=pltpu.SMEM)] + [vmem] * 7 + [pl.BlockSpec(memory_space=pltpu.HBM)],
        out_specs=pl.BlockSpec(memory_space=pltpu.HBM),
        out_shape=pltpu.HBM(sent.shape, sent.dtype),
        scratch_shapes=[
            pltpu.VMEM((rest_low.shape[0] + rest_high.shape[0],) + rest_low.shape[1:], BF16),
            pltpu.SemaphoreType.DMA,
        ],
        input_output_aliases={8: 0},
        compiler_params=pltpu.CompilerParams(vmem_limit_bytes=16 * MIB),
        cost_estimate=pl.CostEstimate(flops=2 * 10**8, bytes_accessed=2 * MIB, transcendentals=0),
    )(target, rest_low, rest_high, coupling, above, below, left, right, sent)


def sweep_kernel(strip, state, ghosts, rate, shift, out, done, sem):
    count, tall, _ = state.shape
    lane = iota((SUB, LANES), 1)
    row = iota((SUB, LANES), 0)
    first = (lane < PC) & (row < FIELDS)
    last = (lane >= PC) & (row >= FIELDS)
    v = rate[...]
    tiles = tall // SUB
    chunk = 8

    def sweep(x, g, y):
        flat = [y[k * SUB : (k + 1) * SUB, :LANES] for k in range(tiles)]
        across = [y[k * SUB : (k + 1) * SUB, LANES:] for k in range(tiles)]
        ext = [g] + [pltpu.roll(z, FIELDS, 0) for z in across] + [g]
        new = []
        for k in range(tiles):
            vertical = jnp.where(first, ext[k], jnp.where(last, ext[k + 2], ext[k + 1]))
            new.append(x[k] + v * ((flat[k] + across[k]) + vertical))
        return new

    def one(c, _):
        base = pl.multiple_of(c * chunk, chunk)
        x = state[pl.ds(base, chunk)].reshape(chunk * tall, LANES)
        y = dot(x, shift[:LANES])
        xs = []
        gs = []
        for i in range(chunk):
            gs.append(ghosts[strip[base + i]])
            mine = x[i * tall : (i + 1) * tall].astype(F32)
            mine = [mine[k * SUB : (k + 1) * SUB] for k in range(tiles)]
            xs.append(sweep(mine, gs[i], y[i * tall : (i + 1) * tall]))
        for step in range(STEPS - 1):
            flat = jnp.concatenate([z for mine in xs for z in mine], axis=0)
            high = flat.astype(BF16)
            y = dot(jnp.concatenate([high, (flat - high.astype(F32)).astype(BF16)], axis=1), shift[...])
            xs = [sweep(xs[i], gs[i], y[i * tall : (i + 1) * tall]) for i in range(chunk)]
        for i in range(chunk):
            for k in range(tiles):
                done[base + i, k * SUB : (k + 1) * SUB] = xs[i][k]
        pltpu.make_async_copy(done.at[pl.ds(base, chunk)], out.at[pl.ds(base, chunk)], sem).start()
        return 0

    lax.fori_loop(0, count // chunk, one, 0, unroll=count // chunk)
    pltpu.make_async_copy(done, out, sem).wait()


def shift_table():
    table = np.zeros((LANES, 2 * LANES), np.float32)
    for i in range(LANES):
        table[i, i] = -4.0
        for j in (i - 1, i + 1):
            if 0 <= j and j // PC == i // PC:
                table[i, j] = 1.0
        table[i, LANES + (i + PC) % LANES] = 1.0
    return np.concatenate([table, table], axis=0)


def sweeps(strip, state, ghosts, rate):
    vmem = pl.BlockSpec(memory_space=pltpu.VMEM)
    return pl.pallas_call(
        sweep_kernel,
        in_specs=[pl.BlockSpec(memory_space=pltpu.SMEM)] + [vmem] * 4,
        out_specs=pl.BlockSpec(memory_space=pltpu.HBM),
        out_shape=pltpu.HBM(state.shape, F32),
        scratch_shapes=[pltpu.VMEM(state.shape, F32), pltpu.SemaphoreType.DMA],
        compiler_params=pltpu.CompilerParams(vmem_limit_bytes=24 * MIB),
    )(strip, state, ghosts, rate, jnp.asarray(shift_table(), BF16))


def interp_table():
    coarse = PC // 2
    table = np.zeros((2, coarse, 2, PC), np.float32)
    for side in range(2):
        for c in range(PC):
            near = c // 2
            second = max(near - 1, 0) if c % 2 == 0 else min(near + 1, coarse - 1)
            table[side, near, side, c] += 0.75
            table[side, second, side, c] += 0.25
    return table.reshape(2 * coarse, 2 * PC)


def shards(fields, new_owner, leaflet, stiffness, coarse, coarse_of_slot, viscosity):
    devices = lax.axis_size("axial") * lax.axis_size("azim")
    patch_count = fields.shape[0]
    slots = devices * SLOTS_EACH

    leaf, first, last, sides, sent = edges(leaflet, slots)
    size = lax.axis_size("azim")
    around = [(i, (i + 1) % size) for i in range(size)]
    right = lax.ppermute(sides, "azim", [(j, i) for i, j in around])
    target, coupling, spread = prepare(new_owner.reshape(1, patch_count), stiffness)
    sides, right, spread, leaf = lax.optimization_barrier((sides, right, spread, leaf))
    left = lax.ppermute(sides, "azim", around)
    held, lap = laplace(to_tiles(fields), leaf)
    first, last, left, lap = lax.optimization_barrier((first, last, left, lap))
    size = lax.axis_size("axial")
    up = [(i, i + 1) for i in range(size - 1)]
    above = lax.ppermute(last, "axial", up)
    blocks = lap.shape[0]
    sent, rest_low = main_part(range(blocks // 2), target, held, lap, spread, sent)
    first, above, sent = lax.optimization_barrier((first, above, sent))
    below = lax.ppermute(first, "axial", [(j, i) for i, j in up])
    sent, rest_high = main_part(range(blocks // 2, blocks), target, held, lap, spread, sent)
    sent = edge_part(target, rest_low, rest_high, coupling, above, below, left, right, sent)
    arrived = lax.all_to_all(sent.reshape(devices, -1, LANES), ALL, split_axis=0, concat_axis=0, tiled=True)
    state = arrived.reshape(slots, -1, LANES)

    strips = coarse.shape[0]
    ghosts = jnp.dot(
        coarse.reshape(strips * FIELDS, -1), jnp.asarray(interp_table()), precision=lax.Precision.HIGHEST
    ).reshape(strips, FIELDS, LANES)
    ghosts = jnp.concatenate([ghosts, ghosts], axis=1)
    rate = jnp.broadcast_to(jnp.concatenate([viscosity, viscosity])[:, None], (SUB, LANES))
    return from_tiles(sweeps(coarse_of_slot, state, ghosts, rate))


def solution(mesh):
    placed = (
        P(ALL, None, None),
        P(ALL, None),
        P(None, "axial", "azim"),
        P(),
        P(ALL, None),
        P(ALL),
        P(),
    )
    return jax.shard_map(
        shards,
        mesh=mesh,
        in_specs=placed,
        out_specs=P(ALL, None, None),
        check_vma=False,
    )
```

time: 71.4 us -> 71.2 us (level)
  waiting for transfers between devices: 29.1 us -> 34.9 us
  starting transfers between devices: 22 us -> 19.3 us
  other arithmetic: 2.41 us -> 0.12 us
  Pallas kernels: 15.5 us -> 14.4 us
    ppermute x1, waiting for transfers between devices: 0.01 us -> 4.29 us  [shards(): left = lax.ppermute(sides, 'azim', around)]
    all_to_all x1, starting transfers between devices: 9.89 us -> 5.96 us  [shards(): lax.all_to_all(sent.reshape(devices, -1, LANES), ALL, split_axis=0, conca...]
    ppermute x1, waiting for transfers between devices: 0.01 us -> 1.46 us  [shards(): below = lax.ppermute(first, 'axial', [(j, i) for i, j in up])]
    ppermute x1, starting transfers between devices: 4.38 us -> 5.53 us  [shards(): above = lax.ppermute(last, 'axial', up)]
    pallas_call x3 -> x6, Pallas kernels: 13.6 us -> 12.5 us  [the longest x1 4.05 us: sweeps(): pl.pallas_call(sweep_kernel, in_specs=[pl.BlockSpec(memory_space=pltpu.SM...]
    reduce_sum x1 -> x0, other arithmetic: 0.9 us -> none  [shards(): ranked = jnp.sum(earlier.astype(jnp.int32), axis=1)]
    mul x1 -> x0, other arithmetic: 0.72 us -> none  [shards(): stiffness * SPREAD]
  transfers between devices with their start and end apart: 5 -> 5, of which waited for: 1 -> 3; matrix products, arithmetic and copies ran while one was open for 4% -> 1% of each run, Pallas kernels for 9% -> 8%
where the time goes in v3:
time: 71.2 us; the launch traced here: 70.8 us
  waiting for transfers between devices  34.9 us (49%)
  starting transfers between devices  19.3 us (27%)
  Pallas kernels  14.4 us (20%)
  local copies, waits for them, and re-layouts  1.67 us (2%)
    all_to_all x1, waiting for transfers between devices, shards(): lax.all_to_all(sent.reshape(devices, -1, LANES), ALL, split_axis=0, conca...  29.1 us
    all_to_all x1, starting transfers between devices, shards(): lax.all_to_all(sent.reshape(devices, -1, LANES), ALL, split_axis=0, conca...  5.96 us
    ppermute x1, starting transfers between devices, shards(): right = lax.ppermute(sides, 'azim', [(j, i) for i, j in around])  5.83 us
    ppermute x1, starting transfers between devices, shards(): above = lax.ppermute(last, 'axial', up)  5.53 us
    ppermute x1, waiting for transfers between devices, shards(): left = lax.ppermute(sides, 'azim', around)  4.29 us
    pallas_call x1, Pallas kernels, sweeps(): pl.pallas_call(sweep_kernel, in_specs=[pl.BlockSpec(memory_space=pltpu.SM...  4.05 us
    pallas_call x2, Pallas kernels, main_part(): pl.pallas_call(functools.partial(main_kernel, span), in_specs=[pl.BlockSp...  3.69 us
    pallas_call x1, Pallas kernels, edges(): pl.pallas_call(edges_kernel, in_specs=[hbm], out_specs=[vmem] * 4 + [hbm]...  2.82 us
  transfers between devices with their start and end apart: 5, of which 3 were waited for; matrix products, arithmetic and copies ran while one was open for 1% of the time, Pallas kernels for 8%

profile of v3, /device:TPU:1, one launch (start us, length us, event | category | flops | bytes accessed | tf_op | source)
XLA Modules:
  0.0 70.8 jit_solution(10640938251617221075)
XLA Ops:
  0.0 2.8 %shard_map.92 = (bf16[64,32,256]{2,1,0:T(8,128)(2,1)S(1)}, bf16[64,256]{1,0:T(8,128)(2,1)S(1)}, bf16[64,256]{1,0:T(8,128)(2,1)S(1)}, bf16[64,128]{1,0:T(8,128)(2,1)S(1)}, bf16[256,32,128]{2,1,0:T(8,128)(2,1)}) custom-call(bf16[64,32,256]{2,1,0:T(8,128)(2,1)} %leaf_hbm.1), custom_call_target="tpu_custom_call" | custom-call | flops 100000000 | bytes 1048576 | tf_op jit(solution)/shard_map/pallas_call | solution.py:90
  2.8 5.8 %collective-permute-start = (bf16[64,128]{1,0:T(8,128)(2,1)S(1)}, bf16[64,128]{1,0:T(8,128)(2,1)S(1)}, u32[]{:S(2)}, u32[]{:S(2)}) collective-permute-start(bf16[64,128]{1,0:T(8,128)(2,1)S(1)} %get-tuple-element.38), channel_id=1, source_target_pairs={{1,0},{2,1},{3,2},{4,3},{5,4},{6,5},{7,6},{8,7},{9,8},{10,9},{11,1... | collective-permute-start | bytes 49160 | tf_op jit(solution)/shard_map/ppermute | solution.py:391
  8.7 0.7 %copy-done.2 = bf16[64,64]{1,0:T(8,128)(2,1)S(1)} copy-done((bf16[64,64]{1,0:T(8,128)(2,1)S(1)}, bf16[64,64]{1,0:T(8,128)(2,1)}, u32[]{:S(2)}) %copy-start.2) | copy-done | bytes 8216
  9.4 0.7 copy-done.3
  10.0 0.3 shard_map.91
  10.4 0.1 collective-permute-start.1
  10.5 1.6 %shard_map.93 = (f32[128,32,128]{2,1,0:T(8,128)S(1)}, bf16[4,512,256]{2,1,0:T(8,128)(2,1)S(1)}) custom-call(f32[128,32,128]{2,1,0:T(8,128)} %bitcast.21, bf16[64,32,256]{2,1,0:T(8,128)(2,1)S(1)} %get-tuple-element.34.leaf), custom_call_target="tpu_custom_call" | custom-call | flops 500000000 | bytes 3145728 | tf_op jit(solution)/shard_map/pallas_call | solution.py:170
  12.1 4.3 %collective-permute-done.1.left = bf16[64,128]{1,0:T(8,128)(2,1)S(1)} collective-permute-done((bf16[64,128]{1,0:T(8,128)(2,1)S(1)}, bf16[64,128]{1,0:T(8,128)(2,1)S(1)}, u32[]{:S(2)}, u32[]{:S(2)}) %collective-permute-start.1) | collective-permute-done | bytes 16416 | tf_op jit(solution)/shard_map/ppermute | solution.py:394
  16.4 5.5 %collective-permute-start.2 = (bf16[64,256]{1,0:T(8,128)(2,1)S(1)}, bf16[64,256]{1,0:T(8,128)(2,1)S(1)}, u32[]{:S(2)}, u32[]{:S(2)}) collective-permute-start(bf16[64,256]{1,0:T(8,128)(2,1)S(1)} %get-tuple-element.45), channel_id=1, source_target_pairs={{0,16},{16,32},{32,48},{48,64},{64,80},{80,96},{96,112},{1,17},{17... | collective-permute-start | bytes 98312 | tf_op jit(solution)/shard_map/ppermute | solution.py:399
  21.9 1.8 %shard_map.94 = (bf16[256,32,128]{2,1,0:T(8,128)(2,1)}, f32[34,32,128]{2,1,0:T(8,128)S(1)}) custom-call(s32[1,128]{1,0:T(1,128)S(1)} %get-tuple-element.30.target, f32[128,32,128]{2,1,0:T(8,128)S(1)} %get-tuple-element.35.fields, bf16[4,512,256]{2,1,0:T(8,128)(2,1)S(1)} %get-tuple-element.40.lap, ...), custom_call_target="tpu_custom_call", output_to_operand_aliasing={{0}: (4, {})} | custom-call | flops 1000000000 | bytes 4194304 | tf_op jit(solution)/shard_map/pallas_call | solution.py:231
  23.8 1.9 %collective-permute-start.3 = (bf16[64,256]{1,0:T(8,128)(2,1)S(1)}, bf16[64,256]{1,0:T(8,128)(2,1)S(1)}, u32[]{:S(2)}, u32[]{:S(2)}) collective-permute-start(bf16[64,256]{1,0:T(8,128)(2,1)S(1)} %get-tuple-element.51), channel_id=1, source_target_pairs={{16,0},{32,16},{48,32},{64,48},{80,64},{96,80},{112,96},{17,1},{33... | collective-permute-start | bytes 98312 | tf_op jit(solution)/shard_map/ppermute | solution.py:403
  25.7 1.8 %shard_map.95 = (bf16[256,32,128]{2,1,0:T(8,128)(2,1)}, f32[34,32,128]{2,1,0:T(8,128)S(1)}) custom-call(s32[1,128]{1,0:T(1,128)S(1)} %get-tuple-element.30.target, f32[128,32,128]{2,1,0:T(8,128)S(1)} %get-tuple-element.35.fields, bf16[4,512,256]{2,1,0:T(8,128)(2,1)S(1)} %get-tuple-element.40.lap, ...), custom_call_target="tpu_custom_call", output_to_operand_aliasing={{0}: (4, {})} | custom-call | flops 1000000000 | bytes 4194304 | tf_op jit(solution)/shard_map/pallas_call | solution.py:231
  27.5 1.5 %collective-permute-done.3.below = bf16[64,256]{1,0:T(8,128)(2,1)S(1)} collective-permute-done((bf16[64,256]{1,0:T(8,128)(2,1)S(1)}, bf16[64,256]{1,0:T(8,128)(2,1)S(1)}, u32[]{:S(2)}, u32[]{:S(2)}) %collective-permute-start.3) | collective-permute-done | bytes 32800 | tf_op jit(solution)/shard_map/ppermute | solution.py:403
  29.0 1.9 %shard_map.96 = bf16[256,32,128]{2,1,0:T(8,128)(2,1)} custom-call(s32[1,128]{1,0:T(1,128)S(1)} %get-tuple-element.30.target, f32[34,32,128]{2,1,0:T(8,128)S(1)} %get-tuple-element.43.rest_low, f32[34,32,128]{2,1,0:T(8,128)S(1)} %get-tuple-element.48.rest_high, bf16[64,64]{1,0:T(8,128)(2,1)S(1)} %get-tuple-element.49.coupling, ...), custom_call_target="tpu_custom_call", output_to_operand_aliasing={{}: (8, {})} | custom-call | flops 200000000 | bytes 2097152 | tf_op jit(solution)/shard_map/pallas_call | solution.py:287
  30.9 0.0 copy-start.5
  30.9 0.0 copy-start
  30.9 6.0 %all-to-all-start = ((bf16[128,64,128]{2,1,0:T(8,128)(2,1)}), bf16[128,64,128]{2,1,0:T(8,128)(2,1)S(1)}, u32[]{:S(2)}, u32[]{:S(2)}) async-start(bf16[128,64,128]{2,1,0:T(8,128)(2,1)} %bitcast.20), calls=%async_computation | async-start | bytes 4194304 | tf_op jit(solution)/shard_map/all_to_all | solution.py:406
  36.9 0.1 dot_general.5
  37.0 0.2 fusion
  37.3 0.1 copy.20
  37.4 0.1 pad_maximum_fusion.1
  37.5 29.1 %all-to-all-done = bf16[128,64,128]{2,1,0:T(8,128)(2,1)S(1)} async-done(((bf16[128,64,128]{2,1,0:T(8,128)(2,1)}), bf16[128,64,128]{2,1,0:T(8,128)(2,1)S(1)}, u32[]{:S(2)}, u32[]{:S(2)}) %all-to-all-start) | async-done | bytes 2097184 | tf_op jit(solution)/shard_map/all_to_all | solution.py:406
  66.7 0.1 broadcast_in_dim.2.rate
  66.7 4.0 %shard_map.97 = f32[256,32,128]{2,1,0:T(8,128)} custom-call(s32[256]{0:T(256)S(1)} %copy-done.1, bf16[256,32,128]{2,1,0:T(8,128)(2,1)S(1)} %bitcast.18, f32[64,8,128]{2,1,0:T(8,128)S(1)} %pad_maximum_fusion.ghosts, f32[8,128]{1,0:T(8,128)S(1)} %broadcast_in_dim.2.rate, bf16[256,256]{1,0:T(8,128)(2,1)S(1)} %copy-done), custom_call_target="tpu_custom_call" | custom-call | tf_op jit(solution)/shard_map/pallas_call | solution.py:361
  (13 shorter events, 0.1 us)
Async XLA Ops:
  2.8 7.5 %collective-permute-start = (bf16[64,128]{1,0:T(8,128)(2,1)S(1)}, bf16[64,128]{1,0:T(8,128)(2,1)S(1)}, u32[]{:S(2)}, u32[]{:S(2)}) collective-permute-start(bf16[64,128]{1,0:T(8,128)(2,1)S(1)} %get-tuple-element.38), channel_id=1, source_target_pairs={{1,0},{2,1},{3,2},{4,3},{5,4},{6,5},{7,6},{8,7},{9,8},{10,9},{11,1... | collective-permute-start | bytes 49160 | tf_op jit(solution)/shard_map/ppermute | solution.py:391
  8.7 0.7 %copy-start.2 = (bf16[64,64]{1,0:T(8,128)(2,1)S(1)}, bf16[64,64]{1,0:T(8,128)(2,1)}, u32[]{:S(2)}) copy-start(bf16[64,64]{1,0:T(8,128)(2,1)} %stiffness.1) | copy-start | bytes 24580
  9.4 0.7 copy-start.3
  10.4 6.0 %collective-permute-start.1 = (bf16[64,128]{1,0:T(8,128)(2,1)S(1)}, bf16[64,128]{1,0:T(8,128)(2,1)S(1)}, u32[]{:S(2)}, u32[]{:S(2)}) collective-permute-start(bf16[64,128]{1,0:T(8,128)(2,1)S(1)} %get-tuple-element.38), channel_id=1, source_target_pairs={{0,1},{1,2},{2,3},{3,4},{4,5},{5,6},{6,7},{7,8},{8,9},{9,10},{10,1... | collective-permute-start | bytes 49160 | tf_op jit(solution)/shard_map/ppermute | solution.py:394
  16.4 7.4 %collective-permute-start.2 = (bf16[64,256]{1,0:T(8,128)(2,1)S(1)}, bf16[64,256]{1,0:T(8,128)(2,1)S(1)}, u32[]{:S(2)}, u32[]{:S(2)}) collective-permute-start(bf16[64,256]{1,0:T(8,128)(2,1)S(1)} %get-tuple-element.45), channel_id=1, source_target_pairs={{0,16},{16,32},{32,48},{48,64},{64,80},{80,96},{96,112},{1,17},{17... | collective-permute-start | bytes 98312 | tf_op jit(solution)/shard_map/ppermute | solution.py:399
  23.8 5.2 %collective-permute-start.3 = (bf16[64,256]{1,0:T(8,128)(2,1)S(1)}, bf16[64,256]{1,0:T(8,128)(2,1)S(1)}, u32[]{:S(2)}, u32[]{:S(2)}) collective-permute-start(bf16[64,256]{1,0:T(8,128)(2,1)S(1)} %get-tuple-element.51), channel_id=1, source_target_pairs={{16,0},{32,16},{48,32},{64,48},{80,64},{96,80},{112,96},{17,1},{33... | collective-permute-start | bytes 98312 | tf_op jit(solution)/shard_map/ppermute | solution.py:403
  30.9 6.0 %copy-start.4 = (f32[64,256]{1,0:T(8,128)S(1)}, f32[64,256]{1,0:T(8,128)}, u32[]{:S(2)}) copy-start(f32[64,256]{1,0:T(8,128)} %param.13) | copy-start | bytes 196612
  30.9 6.1 %copy-start.5 = (f32[64,128,1]{1,0,2:T(8,128)S(1)}, f32[64,128,1]{1,0,2:T(8,128)}, u32[]{:S(2)}) copy-start(f32[64,128,1]{1,0,2:T(8,128)} %constant.7) | copy-start | bytes 98308
  30.9 6.5 %copy-start.6 = (f32[4]{0:T(128)S(1)}, f32[4]{0:T(128)}, u32[]{:S(2)}) copy-start(f32[4]{0:T(128)} %param.15) | copy-start | bytes 52
  30.9 35.8 %copy-start = (bf16[256,256]{1,0:T(8,128)(2,1)S(1)}, bf16[256,256]{1,0:T(8,128)(2,1)}, u32[]{:S(2)}) copy-start(bf16[256,256]{1,0:T(8,128)(2,1)} %constant.5.clone.shift) | copy-start | bytes 393220
  30.9 35.8 %copy-start.1 = (s32[256]{0:T(256)S(1)}, s32[256]{0:T(256)}, u32[]{:S(2)}) copy-start(s32[256]{0:T(256)} %strip.1) | copy-start | bytes 3076
  30.9 35.7 %all-to-all-start = ((bf16[128,64,128]{2,1,0:T(8,128)(2,1)}), bf16[128,64,128]{2,1,0:T(8,128)(2,1)S(1)}, u32[]{:S(2)}, u32[]{:S(2)}) async-start(bf16[128,64,128]{2,1,0:T(8,128)(2,1)} %bitcast.20), calls=%async_computation | async-start | bytes 4194304 | tf_op jit(solution)/shard_map/all_to_all | solution.py:406

commit v4 on v3

--- a/solution.py
+++ b/solution.py
@@ -1,5 +1,3 @@
-import functools
-
 import jax
 import jax.numpy as jnp
 import numpy as np
@@ -47,24 +45,52 @@
     return jnp.where(mask, 1.0, 0.0).astype(BF16)
 
 
-def edges_kernel(leaf_hbm, leaf, first, last, sides, sent, zero, load_sem, zero_sem):
+def first_kernel(
+    leaf_hbm, owner_hbm, stiff_hbm, leaf, one, two, sides, target, coupling, spread, owner, stiffness, load_sem, small_sem
+):
     records, rows, cols = leaf.shape
+    small = [
+        pltpu.make_async_copy(owner_hbm, owner, small_sem.at[0]),
+        pltpu.make_async_copy(stiff_hbm, stiffness, small_sem.at[1]),
+    ]
+    for c in small:
+        c.start()
     size = 16
     loads = []
     for n in range(records // size):
         part = pl.ds(n * size, size)
         loads.append(pltpu.make_async_copy(leaf_hbm.at[part], leaf.at[part], load_sem.at[n]))
         loads[n].start()
-    zero[...] = jnp.zeros_like(zero)
-    count = zero.shape[0]
-    clears = [
-        pltpu.make_async_copy(zero, sent.at[pl.ds(i * count, count)], zero_sem) for i in range(sent.shape[0] // count)
-    ]
-    for c in clears:
-        c.start()
-
+
+    small[0].wait()
+    devices, patches = LANES, owner.shape[1]
+    mine = owner[...] == iota((devices, patches), 0)
+    before = where_one(iota((patches, patches), 0) < iota((patches, patches), 1))
+    earlier = dot(where_one(mine), before)
+    ranked = jnp.sum(jnp.where(mine, earlier, 0.0), axis=0, keepdims=True)
+    target[...] = owner[...] * SLOTS_EACH + ranked.astype(jnp.int32)
+
+    small[1].wait()
+    half = records // 2
+    a, b = iota((records, records), 0), iota((records, records), 1)
+    old = a % FIELDS * (records // FIELDS) + a % half // FIELDS * 2 + a // half
+    ordered = (dot(where_one(b == old), stiffness[...]) * SPREAD).astype(BF16)
+    coupling[...] = ordered
+
+    wide = records * SUB
+    lift = where_one(iota((records, wide), 1) // SUB == iota((records, wide), 0))
+    lifted = dot(ordered, lift)
+    within = iota((half, wide), 1) % SUB
+    for p in range(2):
+        for r in range(SUB):
+            part = jnp.where(within == r, lifted[p * half : (p + 1) * half], 0.0)
+            at = (p * SUB + r) * half
+            spread[at : at + half] = part.astype(BF16)
+
+    odd = lax.axis_index("axial") % 2
     a, b = iota((2 * size, size * rows), 0), iota((2 * size, size * rows), 1)
-    ends = where_one(b == a % size * rows + a // size * (rows - 1))
+    pick = jnp.where((a // size + odd) % 2 == 0, rows - 1, 0)
+    ends = where_one(b == a % size * rows + pick)
     spot = jnp.where(iota((cols, LANES), 1) // rows % 2 == 0, 0, cols - 1)
     spot = where_one(iota((cols, LANES), 0) == spot)
     mine = iota((size * rows, LANES), 1) % rows == iota((size * rows, LANES), 0) % rows
@@ -74,80 +100,47 @@
         part = slice(n * size, (n + 1) * size)
         x = leaf[part].reshape(size * rows, cols)
         both = dot(ends, x).astype(BF16)
-        first[part] = both[:size]
-        last[part] = both[size:]
+        one[part] = both[:size]
+        two[part] = both[size:]
         sides[part] = dot(gather, jnp.where(mine, dot(x, spot), 0.0).astype(BF16)).astype(BF16)
-    for c in clears:
-        c.wait()
-
-
-def edges(leaf, slots):
+
+
+def first_part(leaf, owner, stiffness):
     records, rows, cols = leaf.shape
     vmem = pl.BlockSpec(memory_space=pltpu.VMEM)
     hbm = pl.BlockSpec(memory_space=pltpu.HBM)
     shapes = [leaf.shape, (records, cols), (records, cols), (records, LANES)]
-    tile = (records // 2, LANES)
     return pl.pallas_call(
-        edges_kernel,
-        in_specs=[hbm],
-        out_specs=[vmem] * 4 + [hbm],
-        out_shape=[pltpu.VMEM(s, BF16) for s in shapes] + [pltpu.HBM((slots,) + tile, BF16)],
-        scratch_shapes=[
-            pltpu.VMEM((32,) + tile, BF16),
-            pltpu.SemaphoreType.DMA((records // 16,)),
-            pltpu.SemaphoreType.DMA,
-        ],
-        compiler_params=pltpu.CompilerParams(vmem_limit_bytes=16 * MIB),
-        cost_estimate=pl.CostEstimate(flops=10**8, bytes_accessed=MIB, transcendentals=0),
-    )(in_hbm(leaf))
-
-
-def prepare_kernel(owner, stiffness, target, coupling, spread):
-    devices, patches = LANES, owner.shape[1]
-    mine = owner[...] == iota((devices, patches), 0)
-    before = where_one(iota((patches, patches), 0) < iota((patches, patches), 1))
-    earlier = dot(where_one(mine), before)
-    ranked = jnp.sum(jnp.where(mine, earlier, 0.0), axis=0, keepdims=True)
-    target[...] = owner[...] * SLOTS_EACH + ranked.astype(jnp.int32)
-
-    records = stiffness.shape[0]
-    half = records // 2
-    a, b = iota((records, records), 0), iota((records, records), 1)
-    old = a % FIELDS * (records // FIELDS) + a % half // FIELDS * 2 + a // half
-    ordered = (dot(where_one(b == old), stiffness[...]) * SPREAD).astype(BF16)
-    coupling[...] = ordered
-
-    wide = records * SUB
-    lift = where_one(iota((records, wide), 1) // SUB == iota((records, wide), 0))
-    lifted = dot(ordered, lift)
-    within = iota((half, wide), 1) % SUB
-    for p in range(2):
-        for r in range(SUB):
-            part = jnp.where(within == r, lifted[p * half : (p + 1) * half], 0.0)
-            at = (p * SUB + r) * half
-            spread[at : at + half] = part.astype(BF16)
-
-
-def prepare(owner, stiffness):
-    vmem = pl.BlockSpec(memory_space=pltpu.VMEM)
-    records = stiffness.shape[0]
-    return pl.pallas_call(
-        prepare_kernel,
-        in_specs=[vmem] * 2,
-        out_specs=[vmem] * 3,
-        out_shape=[
+        first_kernel,
+        in_specs=[hbm] * 3,
+        out_specs=[vmem] * 7,
+        out_shape=[pltpu.VMEM(s, BF16) for s in shapes]
+        + [
             jax.ShapeDtypeStruct(owner.shape, jnp.int32),
             pltpu.VMEM((records, records), BF16),
             pltpu.VMEM((records * SUB, records * SUB), BF16),
         ],
+        scratch_shapes=[
+            pltpu.VMEM(owner.shape, jnp.int32),
+            pltpu.VMEM(stiffness.shape, BF16),
+            pltpu.SemaphoreType.DMA((records // 16,)),
+            pltpu.SemaphoreType.DMA((2,)),
+        ],
         compiler_params=pltpu.CompilerParams(vmem_limit_bytes=16 * MIB),
         cost_estimate=pl.CostEstimate(flops=10**8, bytes_accessed=MIB, transcendentals=0),
-    )(owner, stiffness)
-
-
-def laplace_kernel(fields_hbm, leaf, fields, lap, sem):
+    )(in_hbm(leaf), in_hbm(owner), in_hbm(stiffness))
+
+
+def laplace_kernel(fields_hbm, leaf, fields, lap, sent, zero, sem, zero_sem):
     load = pltpu.make_async_copy(fields_hbm, fields, sem)
     load.start()
+    zero[...] = jnp.zeros_like(zero)
+    count = zero.shape[0]
+    clears = [
+        pltpu.make_async_copy(zero, sent.at[pl.ds(i * count, count)], zero_sem) for i in range(sent.shape[0] // count)
+    ]
+    for c in clears:
+        c.start()
     records, rows, cols = leaf.shape
     group = 256 // rows
     a, b = iota((group * rows, group * rows), 0), iota((group * rows, group * rows), 1)
@@ -160,49 +153,61 @@
         for n in range(rows // SUB):
             part = y[:, n * SUB : (n + 1) * SUB].reshape(group * SUB, cols)
             lap[n, g * group * SUB : (g + 1) * group * SUB] = part.astype(BF16)
+    for c in clears:
+        c.wait()
     load.wait()
 
 
-def laplace(fields, leaf):
+def laplace(fields, leaf, slots):
     records, rows, cols = leaf.shape
     vmem = pl.BlockSpec(memory_space=pltpu.VMEM)
     hbm = pl.BlockSpec(memory_space=pltpu.HBM)
     return pl.pallas_call(
         laplace_kernel,
         in_specs=[hbm, vmem],
-        out_specs=[vmem] * 2,
+        out_specs=[vmem, vmem, hbm],
         out_shape=[
             pltpu.VMEM(fields.shape, F32),
             pltpu.VMEM((rows // SUB, records * SUB, cols), BF16),
+            pltpu.HBM((slots,) + fields.shape[1:], BF16),
         ],
-        scratch_shapes=[pltpu.SemaphoreType.DMA],
+        scratch_shapes=[
+            pltpu.VMEM((32,) + fields.shape[1:], BF16),
+            pltpu.SemaphoreType.DMA,
+            pltpu.SemaphoreType.DMA,
+        ],
         compiler_params=pltpu.CompilerParams(vmem_limit_bytes=16 * MIB),
         cost_estimate=pl.CostEstimate(flops=5 * 10**8, bytes_accessed=3 * MIB, transcendentals=0),
     )(in_hbm(fields), leaf)
 
 
+def exchange(x, axis, offset):
+    size = lax.axis_size(axis)
+    pairs = [(i % size, (i + 1) % size) for i in range(offset, size + offset, 2)]
+    return lax.ppermute(x, axis, pairs + [(j, i) for i, j in pairs])
+
+
 def halves(a, b, low, t):
     a, b = a[:, t * LANES : (t + 1) * LANES], b[:, t * LANES : (t + 1) * LANES]
     return jnp.where(low, a, pltpu.roll(b, PC, 1)), jnp.where(low, pltpu.roll(a, PC, 1), b)
 
 
-def edge_patches(rows, quarters, span):
-    ends = (0, rows - 1)
+def edge_patches(rows, quarters):
     return [
-        (r, q) for r in range(rows) for q in range(quarters) if r // SUB in span and (r in ends or q in (0, quarters - 1))
+        (r, q) for r in range(rows) for q in range(quarters) if r in (0, rows - 1) or q in (0, quarters - 1)
     ]
 
 
-def main_kernel(span, target, fields, lap, spread, sent_in, sent, rest, stage, sem):
+def main_kernel(target, fields, lap, spread, sent_in, sent, rest, stage, sem):
     del sent_in
     blocks, _, cols = lap.shape
     half = fields.shape[1]
     rows = blocks * SUB
     quarters = cols // PC
     low = iota((half, LANES), 1) < PC
-    listed = edge_patches(rows, quarters, span)
+    listed = edge_patches(rows, quarters)
     edge = {rq: i for i, rq in enumerate(listed)}
-    for n in span:
+    for n in range(blocks):
         tension = dot(spread[...], lap[n])
         for k in range(SUB):
             r = n * SUB + k
@@ -218,18 +223,18 @@
                     else:
                         stage[patch] = forced.astype(BF16)
                         pltpu.make_async_copy(stage.at[patch], sent.at[target[0, patch]], sem).start()
-    count = len(span) * SUB * quarters - len(edge)
+    count = rows * quarters - len(edge)
     pltpu.make_async_copy(stage.at[pl.ds(0, count)], sent.at[pl.ds(0, count)], sem).wait()
 
 
-def main_part(span, target, fields, lap, spread, sent):
+def main_part(target, fields, lap, spread, sent):
     patches, tall, _ = fields.shape
     blocks, _, cols = lap.shape
     vmem = pl.BlockSpec(memory_space=pltpu.VMEM)
     hbm = pl.BlockSpec(memory_space=pltpu.HBM)
-    count = len(edge_patches(blocks * SUB, cols // PC, span))
+    count = len(edge_patches(blocks * SUB, cols // PC))
     return pl.pallas_call(
-        functools.partial(main_kernel, span),
+        main_kernel,
         in_specs=[pl.BlockSpec(memory_space=pltpu.SMEM), vmem, vmem, vmem, hbm],
         out_specs=[hbm, vmem],
         out_shape=[pltpu.HBM(sent.shape, BF16), pltpu.VMEM((count, tall, LANES), F32)],
@@ -240,16 +245,17 @@
     )(target, fields, lap, spread, sent)
 
 
-def edge_kernel(target, rest_low, rest_high, coupling, above, below, left, right, sent_in, sent, stage, sem):
+def edge_kernel(target, rest, coupling, row_one, row_two, side_one, side_two, sent_in, sent, stage, sem):
     del sent_in
-    records, cols = above.shape
+    records, cols = row_one.shape
     half = records // 2
     quarters = cols // PC
     rows = LANES // 4
     low = iota((half, LANES), 1) < PC
 
     lane = iota((records, LANES), 1)
-    near = jnp.where(lane // rows % 2 == 0, right[...].astype(F32), left[...].astype(F32)).astype(BF16)
+    odd = lax.axis_index("azim") % 2
+    near = jnp.where((lane // rows + odd) % 2 == 0, side_one[...].astype(F32), side_two[...].astype(F32)).astype(BF16)
     both = dot(coupling[...], near)
     both = jnp.where(low, both[:half], both[half:])
     lane = iota((half, LANES), 1)
@@ -260,16 +266,20 @@
     p, s = a // PC % 2, a // rows % 2
     split = dot(split, where_one(b == jnp.where(s == 1, p * PC, LANES + p * PC + PC - 1)))
 
+    place, size = lax.axis_index("axial"), lax.axis_size("axial")
+    odd = place % 2 == 1
+    one, two = row_one[...].astype(F32), row_two[...].astype(F32)
+    two = jnp.where((place == 0) | (place == size - 1), 0.0, two)
     ends = {}
-    for r, row in ((0, above), (rows - 1, below)):
-        whole = dot(coupling[...], row[...])
+    for r, row in ((0, jnp.where(odd, one, two)), (rows - 1, jnp.where(odd, two, one))):
+        whole = dot(coupling[...], row.astype(BF16))
         for t in range(cols // LANES):
             for h, sheet in enumerate(halves(whole[:half], whole[half:], low, t)):
                 ends[r, 2 * t + h] = sheet
 
-    listed = edge_patches(rows, quarters, range(rows // SUB))
+    listed = edge_patches(rows, quarters)
     for i, (r, q) in enumerate(listed):
-        forced = rest_low[i] if i < rest_low.shape[0] else rest_high[i - rest_low.shape[0]]
+        forced = rest[i]
         if q == 0:
             forced = forced + split[r * half : (r + 1) * half, :LANES]
         if q == quarters - 1:
@@ -282,21 +292,18 @@
     pltpu.make_async_copy(stage, sent.at[pl.ds(0, count)], sem).wait()
 
 
-def edge_part(target, rest_low, rest_high, coupling, above, below, left, right, sent):
+def edge_part(target, rest, coupling, row_one, row_two, side_one, side_two, sent):
     vmem = pl.BlockSpec(memory_space=pltpu.VMEM)
     return pl.pallas_call(
         edge_kernel,
-        in_specs=[pl.BlockSpec(memory_space=pltpu.SMEM)] + [vmem] * 7 + [pl.BlockSpec(memory_space=pltpu.HBM)],
+        in_specs=[pl.BlockSpec(memory_space=pltpu.SMEM)] + [vmem] * 6 + [pl.BlockSpec(memory_space=pltpu.HBM)],
         out_specs=pl.BlockSpec(memory_space=pltpu.HBM),
         out_shape=pltpu.HBM(sent.shape, sent.dtype),
-        scratch_shapes=[
-            pltpu.VMEM((rest_low.shape[0] + rest_high.shape[0],) + rest_low.shape[1:], BF16),
-            pltpu.SemaphoreType.DMA,
-        ],
-        input_output_aliases={8: 0},
+        scratch_shapes=[pltpu.VMEM(rest.shape, BF16), pltpu.SemaphoreType.DMA],
+        input_output_aliases={7: 0},
         compiler_params=pltpu.CompilerParams(vmem_limit_bytes=16 * MIB),
         cost_estimate=pl.CostEstimate(flops=2 * 10**8, bytes_accessed=2 * MIB, transcendentals=0),
-    )(target, rest_low, rest_high, coupling, above, below, left, right, sent)
+    )(target, rest, coupling, row_one, row_two, side_one, side_two, sent)
 
 
 def sweep_kernel(strip, state, ghosts, rate, shift, out, done, sem):
@@ -385,24 +392,16 @@
     patch_count = fields.shape[0]
     slots = devices * SLOTS_EACH
 
-    leaf, first, last, sides, sent = edges(leaflet, slots)
-    size = lax.axis_size("azim")
-    around = [(i, (i + 1) % size) for i in range(size)]
-    right = lax.ppermute(sides, "azim", [(j, i) for i, j in around])
-    target, coupling, spread = prepare(new_owner.reshape(1, patch_count), stiffness)
-    sides, right, spread, leaf = lax.optimization_barrier((sides, right, spread, leaf))
-    left = lax.ppermute(sides, "azim", around)
-    held, lap = laplace(to_tiles(fields), leaf)
-    first, last, left, lap = lax.optimization_barrier((first, last, left, lap))
-    size = lax.axis_size("axial")
-    up = [(i, i + 1) for i in range(size - 1)]
-    above = lax.ppermute(last, "axial", up)
-    blocks = lap.shape[0]
-    sent, rest_low = main_part(range(blocks // 2), target, held, lap, spread, sent)
-    first, above, sent = lax.optimization_barrier((first, above, sent))
-    below = lax.ppermute(first, "axial", [(j, i) for i, j in up])
-    sent, rest_high = main_part(range(blocks // 2, blocks), target, held, lap, spread, sent)
-    sent = edge_part(target, rest_low, rest_high, coupling, above, below, left, right, sent)
+    leaf, row_one, row_two, sides, target, coupling, spread = first_part(
+        leaflet, new_owner.reshape(1, patch_count), stiffness
+    )
+    side_one = exchange(sides, "azim", 0)
+    side_two = exchange(sides, "azim", 1)
+    row_one = exchange(row_one, "axial", 0)
+    row_two = exchange(row_two, "axial", 1)
+    held, lap, sent = laplace(to_tiles(fields), leaf, slots)
+    sent, rest = main_part(target, held, lap, spread, sent)
+    sent = edge_part(target, rest, coupling, row_one, row_two, side_one, side_two, sent)
     arrived = lax.all_to_all(sent.reshape(devices, -1, LANES), ALL, split_axis=0, concat_axis=0, tiled=True)
     state = arrived.reshape(slots, -1, LANES)
 

time: 71.2 us -> 58.8 us (0.83)
  waiting for transfers between devices: 34.9 us -> 29.3 us
  starting transfers between devices: 19.3 us -> 15.3 us
  local copies, waits for them, and re-layouts: 1.67 us -> 0.3 us
  Pallas kernels: 14.4 us -> 13.2 us
    ppermute x4, waiting for transfers between devices: 5.75 us -> 0.01 us  [exchange(): return lax.ppermute(x, axis, pairs + [(j, i) for i, j in pairs])]
    ppermute x4, starting transfers between devices: 13.3 us -> 9.06 us  [exchange(): return lax.ppermute(x, axis, pairs + [(j, i) for i, j in pairs])]
    unnamed x14 -> x10, local copies, waits for them, and re-layouts: 1.4 us -> 0.03 us
    pallas_call x5 -> x3, Pallas kernels: 8.43 us -> 7.2 us  [the longest x1 3.12 us: first_part(): pl.pallas_call(first_kernel, in_specs=[hbm] * 3, out_specs=[vmem] * 7, ou...]
  transfers between devices with their start and end apart: 5 -> 5, of which waited for: 3 -> 1; matrix products, arithmetic and copies ran while one was open for 1% -> 1% of each run, Pallas kernels for 8% -> 7%
where the time goes in v4:
time: 58.8 us; the launch traced here: 58.6 us
  waiting for transfers between devices  29.3 us (50%)
  starting transfers between devices  15.3 us (26%)
  Pallas kernels  13.2 us (22%)
    all_to_all x1, waiting for transfers between devices, shards(): lax.all_to_all(sent.reshape(devices, -1, LANES), ALL, split_axis=0, conca...  29.3 us
    ppermute x4, starting transfers between devices, exchange(): return lax.ppermute(x, axis, pairs + [(j, i) for i, j in pairs])  9.06 us
    all_to_all x1, starting transfers between devices, shards(): lax.all_to_all(sent.reshape(devices, -1, LANES), ALL, split_axis=0, conca...  6.22 us
    pallas_call x1, Pallas kernels, sweeps(): pl.pallas_call(sweep_kernel, in_specs=[pl.BlockSpec(memory_space=pltpu.SM...  4.06 us
    pallas_call x1, Pallas kernels, first_part(): pl.pallas_call(first_kernel, in_specs=[hbm] * 3, out_specs=[vmem] * 7, ou...  3.12 us
    pallas_call x1, Pallas kernels, main_part(): pl.pallas_call(main_kernel, in_specs=[pl.BlockSpec(memory_space=pltpu.SME...  2.15 us
    pallas_call x1, Pallas kernels, laplace(): pl.pallas_call(laplace_kernel, in_specs=[hbm, vmem], out_specs=[vmem, vme...  1.93 us
    pallas_call x1, Pallas kernels, edge_part(): pl.pallas_call(edge_kernel, in_specs=[pl.BlockSpec(memory_space=pltpu.SME...  1.9 us
  transfers between devices with their start and end apart: 5, of which 1 were waited for; matrix products, arithmetic and copies ran while one was open for 1% of the time, Pallas kernels for 7%

profile of v4, /device:TPU:1, one launch (start us, length us, event | category | flops | bytes accessed | tf_op | source)
XLA Modules:
  0.0 58.6 jit_solution(1283724898331274743)
XLA Ops:
  0.0 3.1 %shard_map.91 = (bf16[64,32,256]{2,1,0:T(8,128)(2,1)S(1)}, bf16[64,256]{1,0:T(8,128)(2,1)S(1)}, bf16[64,256]{1,0:T(8,128)(2,1)S(1)}, bf16[64,128]{1,0:T(8,128)(2...) custom-call(bf16[64,32,256]{2,1,0:T(8,128)(2,1)} %leaf_hbm.1, ...), custom_call_target="tpu_custom_call" | custom-call | flops 100000000 | bytes 1048576 | tf_op jit(solution)/shard_map/pallas_call | solution.py:113
  3.1 2.2 %collective-permute-start.2 = (bf16[64,128]{1,0:T(8,128)(2,1)S(1)}, bf16[64,128]{1,0:T(8,128)(2,1)S(1)}, u32[]{:S(2)}, u32[]{:S(2)}) collective-permute-start(bf16[64,128]{1,0:T(8,128)(2,1)S(1)} %get-tuple-element.27), channel_id=1, source_target_pairs={{0,1},{2,3},{4,5},{6,7},{8,9},{10,11},{12,13},{14,15},{1,0},{3,2},... | collective-permute-start | bytes 49160 | tf_op jit(solution)/shard_map/ppermute | solution.py:187
  5.3 4.1 %collective-permute-start.3 = (bf16[64,128]{1,0:T(8,128)(2,1)S(1)}, bf16[64,128]{1,0:T(8,128)(2,1)S(1)}, u32[]{:S(2)}, u32[]{:S(2)}) collective-permute-start(bf16[64,128]{1,0:T(8,128)(2,1)S(1)} %get-tuple-element.27), channel_id=1, source_target_pairs={{1,2},{3,4},{5,6},{7,8},{9,10},{11,12},{13,14},{15,0},{2,1},{4,3},... | collective-permute-start | bytes 49160 | tf_op jit(solution)/shard_map/ppermute | solution.py:187
  9.4 1.2 %collective-permute-start = (bf16[64,256]{1,0:T(8,128)(2,1)S(1)}, bf16[64,256]{1,0:T(8,128)(2,1)S(1)}, u32[]{:S(2)}, u32[]{:S(2)}) collective-permute-start(bf16[64,256]{1,0:T(8,128)(2,1)S(1)} %get-tuple-element.25), channel_id=1, source_target_pairs={{0,16},{32,48},{64,80},{96,112},{16,0},{48,32},{80,64},{112,96},{1... | collective-permute-start | bytes 98312 | tf_op jit(solution)/shard_map/ppermute | solution.py:187
  10.7 1.5 %collective-permute-start.1 = (bf16[64,256]{1,0:T(8,128)(2,1)S(1)}, bf16[64,256]{1,0:T(8,128)(2,1)S(1)}, u32[]{:S(2)}, u32[]{:S(2)}) collective-permute-start(bf16[64,256]{1,0:T(8,128)(2,1)S(1)} %get-tuple-element.26), channel_id=1, source_target_pairs={{16,32},{48,64},{80,96},{112,0},{32,16},{64,48},{96,80},{0,112},{1... | collective-permute-start | bytes 98312 | tf_op jit(solution)/shard_map/ppermute | solution.py:187
  12.2 1.9 %shard_map.92 = (f32[128,32,128]{2,1,0:T(8,128)S(1)}, bf16[4,512,256]{2,1,0:T(8,128)(2,1)S(1)}, bf16[256,32,128]{2,1,0:T(8,128)(2,1)}) custom-call(f32[128,32,128]{2,1,0:T(8,128)} %bitcast.20, bf16[64,32,256]{2,1,0:T(8,128)(2,1)S(1)} %get-tuple-element.18.leaf), custom_call_target="tpu_custom_call" | custom-call | flops 500000000 | bytes 3145728 | tf_op jit(solution)/shard_map/pallas_call | solution.py:165
  14.1 2.2 %shard_map.93 = (bf16[256,32,128]{2,1,0:T(8,128)(2,1)}, f32[68,32,128]{2,1,0:T(8,128)S(1)}) custom-call(s32[1,128]{1,0:T(1,128)S(1)} %get-tuple-element.17.target, f32[128,32,128]{2,1,0:T(8,128)S(1)} %get-tuple-element.19.fields, bf16[4,512,256]{2,1,0:T(8,128)(2,1)S(1)} %get-tuple-element.20.lap, ...), custom_call_target="tpu_custom_call", output_to_operand_aliasing={{0}: (4, {})} | custom-call | flops 1000000000 | bytes 4194304 | tf_op jit(solution)/shard_map/pallas_call | solution.py:236
  16.3 0.0 collective-permute-done.2.side_one
  16.3 0.0 collective-permute-done.3.side_two
  16.3 0.0 collective-permute-done.row_one
  16.3 1.9 %shard_map.94 = bf16[256,32,128]{2,1,0:T(8,128)(2,1)} custom-call(s32[1,128]{1,0:T(1,128)S(1)} %get-tuple-element.17.target, f32[68,32,128]{2,1,0:T(8,128)S(1)} %get-tuple-element.23.rest, bf16[64,64]{1,0:T(8,128)(2,1)S(1)} %get-tuple-element.24.coupling, bf16[64,256]{1,0:T(8,128)(2,1)S(1)} %collective-permute-done.row_one, ...), custom_call_target="tpu_custom_call", output_to_operand_aliasing={{}: (7, {})} | custom-call | flops 200000000 | bytes 2097152 | tf_op jit(solution)/shard_map/pallas_call | solution.py:297
  18.2 0.0 copy-start.2
  18.2 0.0 copy-start.3
  18.3 0.0 copy-start.4
  18.3 0.0 copy-start
  18.3 0.0 copy-start.1
  18.3 6.2 %all-to-all-start = ((bf16[128,64,128]{2,1,0:T(8,128)(2,1)}), bf16[128,64,128]{2,1,0:T(8,128)(2,1)S(1)}, u32[]{:S(2)}, u32[]{:S(2)}) async-start(bf16[128,64,128]{2,1,0:T(8,128)(2,1)} %bitcast.19), calls=%async_computation | async-start | bytes 4194304 | tf_op jit(solution)/shard_map/all_to_all | solution.py:405
  24.5 0.1 dot_general.5
  24.7 0.3 fusion
  24.9 0.1 copy.19
  25.0 0.1 pad_maximum_fusion.1
  25.1 29.3 %all-to-all-done = bf16[128,64,128]{2,1,0:T(8,128)(2,1)S(1)} async-done(((bf16[128,64,128]{2,1,0:T(8,128)(2,1)}), bf16[128,64,128]{2,1,0:T(8,128)(2,1)S(1)}, u32[]{:S(2)}, u32[]{:S(2)}) %all-to-all-start) | async-done | bytes 2097184 | tf_op jit(solution)/shard_map/all_to_all | solution.py:405
  54.4 0.1 broadcast_in_dim.2.rate
  54.5 4.1 %shard_map.95 = f32[256,32,128]{2,1,0:T(8,128)} custom-call(s32[256]{0:T(256)S(1)} %copy-done.1, bf16[256,32,128]{2,1,0:T(8,128)(2,1)S(1)} %bitcast.18, f32[64,8,128]{2,1,0:T(8,128)S(1)} %pad_maximum_fusion.ghosts, f32[8,128]{1,0:T(8,128)S(1)} %broadcast_in_dim.2.rate, bf16[256,256]{1,0:T(8,128)(2,1)S(1)} %copy-done), custom_call_target="tpu_custom_call" | custom-call | tf_op jit(solution)/shard_map/pallas_call | solution.py:368
  (7 shorter events, 0.1 us)
Async XLA Ops:
  3.1 13.2 %collective-permute-start.2 = (bf16[64,128]{1,0:T(8,128)(2,1)S(1)}, bf16[64,128]{1,0:T(8,128)(2,1)S(1)}, u32[]{:S(2)}, u32[]{:S(2)}) collective-permute-start(bf16[64,128]{1,0:T(8,128)(2,1)S(1)} %get-tuple-element.27), channel_id=1, source_target_pairs={{0,1},{2,3},{4,5},{6,7},{8,9},{10,11},{12,13},{14,15},{1,0},{3,2},... | collective-permute-start | bytes 49160 | tf_op jit(solution)/shard_map/ppermute | solution.py:187
  5.3 11.0 %collective-permute-start.3 = (bf16[64,128]{1,0:T(8,128)(2,1)S(1)}, bf16[64,128]{1,0:T(8,128)(2,1)S(1)}, u32[]{:S(2)}, u32[]{:S(2)}) collective-permute-start(bf16[64,128]{1,0:T(8,128)(2,1)S(1)} %get-tuple-element.27), channel_id=1, source_target_pairs={{1,2},{3,4},{5,6},{7,8},{9,10},{11,12},{13,14},{15,0},{2,1},{4,3},... | collective-permute-start | bytes 49160 | tf_op jit(solution)/shard_map/ppermute | solution.py:187
  9.4 6.9 %collective-permute-start = (bf16[64,256]{1,0:T(8,128)(2,1)S(1)}, bf16[64,256]{1,0:T(8,128)(2,1)S(1)}, u32[]{:S(2)}, u32[]{:S(2)}) collective-permute-start(bf16[64,256]{1,0:T(8,128)(2,1)S(1)} %get-tuple-element.25), channel_id=1, source_target_pairs={{0,16},{32,48},{64,80},{96,112},{16,0},{48,32},{80,64},{112,96},{1... | collective-permute-start | bytes 98312 | tf_op jit(solution)/shard_map/ppermute | solution.py:187
  10.7 5.7 %collective-permute-start.1 = (bf16[64,256]{1,0:T(8,128)(2,1)S(1)}, bf16[64,256]{1,0:T(8,128)(2,1)S(1)}, u32[]{:S(2)}, u32[]{:S(2)}) collective-permute-start(bf16[64,256]{1,0:T(8,128)(2,1)S(1)} %get-tuple-element.26), channel_id=1, source_target_pairs={{16,32},{48,64},{80,96},{112,0},{32,16},{64,48},{96,80},{0,112},{1... | collective-permute-start | bytes 98312 | tf_op jit(solution)/shard_map/ppermute | solution.py:187
  18.2 6.3 %copy-start.2 = (f32[64,256]{1,0:T(8,128)S(1)}, f32[64,256]{1,0:T(8,128)}, u32[]{:S(2)}) copy-start(f32[64,256]{1,0:T(8,128)} %param.13) | copy-start | bytes 196612
  18.2 6.4 %copy-start.3 = (f32[64,128,1]{1,0,2:T(8,128)S(1)}, f32[64,128,1]{1,0,2:T(8,128)}, u32[]{:S(2)}) copy-start(f32[64,128,1]{1,0,2:T(8,128)} %constant.7) | copy-start | bytes 98308
  18.3 6.8 %copy-start.4 = (f32[4]{0:T(128)S(1)}, f32[4]{0:T(128)}, u32[]{:S(2)}) copy-start(f32[4]{0:T(128)} %param.15) | copy-start | bytes 52
  18.3 36.2 %copy-start = (bf16[256,256]{1,0:T(8,128)(2,1)S(1)}, bf16[256,256]{1,0:T(8,128)(2,1)}, u32[]{:S(2)}) copy-start(bf16[256,256]{1,0:T(8,128)(2,1)} %constant.5.clone.shift) | copy-start | bytes 393220
  18.3 36.2 %copy-start.1 = (s32[256]{0:T(256)S(1)}, s32[256]{0:T(256)}, u32[]{:S(2)}) copy-start(s32[256]{0:T(256)} %strip.1) | copy-start | bytes 3076
  18.3 36.1 %all-to-all-start = ((bf16[128,64,128]{2,1,0:T(8,128)(2,1)}), bf16[128,64,128]{2,1,0:T(8,128)(2,1)S(1)}, u32[]{:S(2)}, u32[]{:S(2)}) async-start(bf16[128,64,128]{2,1,0:T(8,128)(2,1)} %bitcast.19), calls=%async_computation | async-start | bytes 4194304 | tf_op jit(solution)/shard_map/all_to_all | solution.py:405

commit v5 on v4

--- a/solution.py
+++ b/solution.py
@@ -45,47 +45,14 @@
     return jnp.where(mask, 1.0, 0.0).astype(BF16)
 
 
-def first_kernel(
-    leaf_hbm, owner_hbm, stiff_hbm, leaf, one, two, sides, target, coupling, spread, owner, stiffness, load_sem, small_sem
-):
+def first_kernel(leaf_hbm, leaf, one, two, sides, load_sem):
     records, rows, cols = leaf.shape
-    small = [
-        pltpu.make_async_copy(owner_hbm, owner, small_sem.at[0]),
-        pltpu.make_async_copy(stiff_hbm, stiffness, small_sem.at[1]),
-    ]
-    for c in small:
-        c.start()
     size = 16
     loads = []
     for n in range(records // size):
         part = pl.ds(n * size, size)
         loads.append(pltpu.make_async_copy(leaf_hbm.at[part], leaf.at[part], load_sem.at[n]))
         loads[n].start()
-
-    small[0].wait()
-    devices, patches = LANES, owner.shape[1]
-    mine = owner[...] == iota((devices, patches), 0)
-    before = where_one(iota((patches, patches), 0) < iota((patches, patches), 1))
-    earlier = dot(where_one(mine), before)
-    ranked = jnp.sum(jnp.where(mine, earlier, 0.0), axis=0, keepdims=True)
-    target[...] = owner[...] * SLOTS_EACH + ranked.astype(jnp.int32)
-
-    small[1].wait()
-    half = records // 2
-    a, b = iota((records, records), 0), iota((records, records), 1)
-    old = a % FIELDS * (records // FIELDS) + a % half // FIELDS * 2 + a // half
-    ordered = (dot(where_one(b == old), stiffness[...]) * SPREAD).astype(BF16)
-    coupling[...] = ordered
-
-    wide = records * SUB
-    lift = where_one(iota((records, wide), 1) // SUB == iota((records, wide), 0))
-    lifted = dot(ordered, lift)
-    within = iota((half, wide), 1) % SUB
-    for p in range(2):
-        for r in range(SUB):
-            part = jnp.where(within == r, lifted[p * half : (p + 1) * half], 0.0)
-            at = (p * SUB + r) * half
-            spread[at : at + half] = part.astype(BF16)
 
     odd = lax.axis_index("axial") % 2
     a, b = iota((2 * size, size * rows), 0), iota((2 * size, size * rows), 1)
@@ -105,43 +72,105 @@
         sides[part] = dot(gather, jnp.where(mine, dot(x, spot), 0.0).astype(BF16)).astype(BF16)
 
 
-def first_part(leaf, owner, stiffness):
+def first_part(leaf):
     records, rows, cols = leaf.shape
     vmem = pl.BlockSpec(memory_space=pltpu.VMEM)
-    hbm = pl.BlockSpec(memory_space=pltpu.HBM)
     shapes = [leaf.shape, (records, cols), (records, cols), (records, LANES)]
     return pl.pallas_call(
         first_kernel,
-        in_specs=[hbm] * 3,
-        out_specs=[vmem] * 7,
-        out_shape=[pltpu.VMEM(s, BF16) for s in shapes]
-        + [
-            jax.ShapeDtypeStruct(owner.shape, jnp.int32),
-            pltpu.VMEM((records, records), BF16),
-            pltpu.VMEM((records * SUB, records * SUB), BF16),
-        ],
-        scratch_shapes=[
-            pltpu.VMEM(owner.shape, jnp.int32),
-            pltpu.VMEM(stiffness.shape, BF16),
-            pltpu.SemaphoreType.DMA((records // 16,)),
-            pltpu.SemaphoreType.DMA((2,)),
-        ],
+        in_specs=[pl.BlockSpec(memory_space=pltpu.HBM)],
+        out_specs=[vmem] * 4,
+        out_shape=[pltpu.VMEM(s, BF16) for s in shapes],
+        scratch_shapes=[pltpu.SemaphoreType.DMA((records // 16,))],
         compiler_params=pltpu.CompilerParams(vmem_limit_bytes=16 * MIB),
         cost_estimate=pl.CostEstimate(flops=10**8, bytes_accessed=MIB, transcendentals=0),
-    )(in_hbm(leaf), in_hbm(owner), in_hbm(stiffness))
-
-
-def laplace_kernel(fields_hbm, leaf, fields, lap, sent, zero, sem, zero_sem):
-    load = pltpu.make_async_copy(fields_hbm, fields, sem)
-    load.start()
-    zero[...] = jnp.zeros_like(zero)
-    count = zero.shape[0]
-    clears = [
-        pltpu.make_async_copy(zero, sent.at[pl.ds(i * count, count)], zero_sem) for i in range(sent.shape[0] // count)
+    )(in_hbm(leaf))
+
+
+def exchange(x, axis, offset):
+    size = lax.axis_size(axis)
+    pairs = [(i % size, (i + 1) % size) for i in range(offset, size + offset, 2)]
+    return lax.ppermute(x, axis, pairs + [(j, i) for i, j in pairs])
+
+
+def halves(a, b, low, t):
+    a, b = a[:, t * LANES : (t + 1) * LANES], b[:, t * LANES : (t + 1) * LANES]
+    return jnp.where(low, a, pltpu.roll(b, PC, 1)), jnp.where(low, pltpu.roll(a, PC, 1), b)
+
+
+def edge_patches(rows, quarters):
+    return [
+        (r, q) for r in range(rows) for q in range(quarters) if r in (0, rows - 1) or q in (0, quarters - 1)
     ]
-    for c in clears:
+
+
+def main_kernel(
+    fields_hbm,
+    leaf,
+    owner_hbm,
+    stiff_hbm,
+    image,
+    rest,
+    target,
+    coupling,
+    fields,
+    lap,
+    spread,
+    owner,
+    stiffness,
+    slot,
+    load_sem,
+    small_sem,
+):
+    small = [
+        pltpu.make_async_copy(owner_hbm, owner, small_sem.at[0]),
+        pltpu.make_async_copy(stiff_hbm, stiffness, small_sem.at[1]),
+    ]
+    for c in small:
         c.start()
     records, rows, cols = leaf.shape
+    blocks = rows // SUB
+    size = fields.shape[0] // blocks
+    loads = []
+    for n in range(blocks):
+        part = pl.ds(n * size, size)
+        loads.append(pltpu.make_async_copy(fields_hbm.at[part], fields.at[part], load_sem.at[n]))
+        loads[n].start()
+
+    small[0].wait()
+    devices, patches = LANES, owner.shape[1]
+    mine = owner[...] == iota((devices, patches), 0)
+    before = where_one(iota((patches, patches), 0) < iota((patches, patches), 1))
+    earlier = dot(where_one(mine), before)
+    ranked = jnp.sum(jnp.where(mine, earlier, 0.0), axis=0, keepdims=True)
+    target[...] = owner[...] * SLOTS_EACH + ranked.astype(jnp.int32)
+
+    turn = pltpu.make_async_copy(target, slot, small_sem.at[0])
+    turn.start()
+
+    small[1].wait()
+    half = records // 2
+    a, b = iota((records, records), 0), iota((records, records), 1)
+    old = a % FIELDS * (records // FIELDS) + a % half // FIELDS * 2 + a // half
+    ordered = (dot(where_one(b == old), stiffness[...]) * SPREAD).astype(BF16)
+    coupling[...] = ordered
+
+    wide = records * SUB
+    lift = where_one(iota((records, wide), 1) // SUB == iota((records, wide), 0))
+    lifted = dot(ordered, lift)
+    within = iota((half, wide), 1) % SUB
+    for p in range(2):
+        for r in range(SUB):
+            part = jnp.where(within == r, lifted[p * half : (p + 1) * half], 0.0)
+            at = (p * SUB + r) * half
+            spread[at : at + half] = part.astype(BF16)
+
+    def clear(i, _):
+        image[pl.ds(i * SUB, SUB)] = jnp.zeros((SUB,) + image.shape[1:], BF16)
+        return 0
+
+    lax.fori_loop(0, image.shape[0] // SUB, clear, 0)
+
     group = 256 // rows
     a, b = iota((group * rows, group * rows), 0), iota((group * rows, group * rows), 1)
     beside = where_one((jnp.abs(a - b) == 1) & (a // rows == b // rows))
@@ -153,62 +182,14 @@
         for n in range(rows // SUB):
             part = y[:, n * SUB : (n + 1) * SUB].reshape(group * SUB, cols)
             lap[n, g * group * SUB : (g + 1) * group * SUB] = part.astype(BF16)
-    for c in clears:
-        c.wait()
-    load.wait()
-
-
-def laplace(fields, leaf, slots):
-    records, rows, cols = leaf.shape
-    vmem = pl.BlockSpec(memory_space=pltpu.VMEM)
-    hbm = pl.BlockSpec(memory_space=pltpu.HBM)
-    return pl.pallas_call(
-        laplace_kernel,
-        in_specs=[hbm, vmem],
-        out_specs=[vmem, vmem, hbm],
-        out_shape=[
-            pltpu.VMEM(fields.shape, F32),
-            pltpu.VMEM((rows // SUB, records * SUB, cols), BF16),
-            pltpu.HBM((slots,) + fields.shape[1:], BF16),
-        ],
-        scratch_shapes=[
-            pltpu.VMEM((32,) + fields.shape[1:], BF16),
-            pltpu.SemaphoreType.DMA,
-            pltpu.SemaphoreType.DMA,
-        ],
-        compiler_params=pltpu.CompilerParams(vmem_limit_bytes=16 * MIB),
-        cost_estimate=pl.CostEstimate(flops=5 * 10**8, bytes_accessed=3 * MIB, transcendentals=0),
-    )(in_hbm(fields), leaf)
-
-
-def exchange(x, axis, offset):
-    size = lax.axis_size(axis)
-    pairs = [(i % size, (i + 1) % size) for i in range(offset, size + offset, 2)]
-    return lax.ppermute(x, axis, pairs + [(j, i) for i, j in pairs])
-
-
-def halves(a, b, low, t):
-    a, b = a[:, t * LANES : (t + 1) * LANES], b[:, t * LANES : (t + 1) * LANES]
-    return jnp.where(low, a, pltpu.roll(b, PC, 1)), jnp.where(low, pltpu.roll(a, PC, 1), b)
-
-
-def edge_patches(rows, quarters):
-    return [
-        (r, q) for r in range(rows) for q in range(quarters) if r in (0, rows - 1) or q in (0, quarters - 1)
-    ]
-
-
-def main_kernel(target, fields, lap, spread, sent_in, sent, rest, stage, sem):
-    del sent_in
-    blocks, _, cols = lap.shape
-    half = fields.shape[1]
-    rows = blocks * SUB
+
+    turn.wait()
     quarters = cols // PC
     low = iota((half, LANES), 1) < PC
-    listed = edge_patches(rows, quarters)
-    edge = {rq: i for i, rq in enumerate(listed)}
+    edge = {rq: i for i, rq in enumerate(edge_patches(rows, quarters))}
     for n in range(blocks):
         tension = dot(spread[...], lap[n])
+        loads[n].wait()
         for k in range(SUB):
             r = n * SUB + k
             a = tension[k * half : (k + 1) * half]
@@ -221,32 +202,42 @@
                     if (r, q) in edge:
                         rest[edge[r, q]] = forced
                     else:
-                        stage[patch] = forced.astype(BF16)
-                        pltpu.make_async_copy(stage.at[patch], sent.at[target[0, patch]], sem).start()
-    count = rows * quarters - len(edge)
-    pltpu.make_async_copy(stage.at[pl.ds(0, count)], sent.at[pl.ds(0, count)], sem).wait()
-
-
-def main_part(target, fields, lap, spread, sent):
-    patches, tall, _ = fields.shape
-    blocks, _, cols = lap.shape
+                        image[slot[0, patch]] = forced.astype(BF16)
+
+
+def main_part(fields, leaf, owner, stiffness, slots):
+    records, rows, cols = leaf.shape
+    _, tall, _ = fields.shape
     vmem = pl.BlockSpec(memory_space=pltpu.VMEM)
     hbm = pl.BlockSpec(memory_space=pltpu.HBM)
-    count = len(edge_patches(blocks * SUB, cols // PC))
+    count = len(edge_patches(rows, cols // PC))
     return pl.pallas_call(
         main_kernel,
-        in_specs=[pl.BlockSpec(memory_space=pltpu.SMEM), vmem, vmem, vmem, hbm],
-        out_specs=[hbm, vmem],
-        out_shape=[pltpu.HBM(sent.shape, BF16), pltpu.VMEM((count, tall, LANES), F32)],
-        scratch_shapes=[pltpu.VMEM((patches, tall, LANES), BF16), pltpu.SemaphoreType.DMA],
-        input_output_aliases={4: 0},
+        in_specs=[hbm, vmem, hbm, hbm],
+        out_specs=[vmem] * 4,
+        out_shape=[
+            pltpu.VMEM((slots, tall, LANES), BF16),
+            pltpu.VMEM((count, tall, LANES), F32),
+            jax.ShapeDtypeStruct(owner.shape, jnp.int32),
+            pltpu.VMEM((records, records), BF16),
+        ],
+        scratch_shapes=[
+            pltpu.VMEM(fields.shape, F32),
+            pltpu.VMEM((rows // SUB, records * SUB, cols), BF16),
+            pltpu.VMEM((records * SUB, records * SUB), BF16),
+            pltpu.VMEM(owner.shape, jnp.int32),
+            pltpu.VMEM(stiffness.shape, BF16),
+            pltpu.SMEM(owner.shape, jnp.int32),
+            pltpu.SemaphoreType.DMA((rows // SUB,)),
+            pltpu.SemaphoreType.DMA((2,)),
+        ],
         compiler_params=pltpu.CompilerParams(vmem_limit_bytes=16 * MIB),
-        cost_estimate=pl.CostEstimate(flops=10**9, bytes_accessed=4 * MIB, transcendentals=0),
-    )(target, fields, lap, spread, sent)
-
-
-def edge_kernel(target, rest, coupling, row_one, row_two, side_one, side_two, sent_in, sent, stage, sem):
-    del sent_in
+        cost_estimate=pl.CostEstimate(flops=2 * 10**9, bytes_accessed=8 * MIB, transcendentals=0),
+    )(in_hbm(fields), leaf, in_hbm(owner), in_hbm(stiffness))
+
+
+def edge_kernel(target, rest, coupling, row_two, row_one, side_two, side_one, image_in, image, sent, sem):
+    del image_in
     records, cols = row_one.shape
     half = records // 2
     quarters = cols // PC
@@ -286,24 +277,25 @@
             forced = forced + split[r * half : (r + 1) * half, LANES:]
         if (r, q) in ends:
             forced = forced + ends[r, q]
-        stage[i] = forced.astype(BF16)
-        pltpu.make_async_copy(stage.at[i], sent.at[target[0, r * quarters + q]], sem).start()
-    count = len(listed)
-    pltpu.make_async_copy(stage, sent.at[pl.ds(0, count)], sem).wait()
-
-
-def edge_part(target, rest, coupling, row_one, row_two, side_one, side_two, sent):
+        image[target[0, r * quarters + q]] = forced.astype(BF16)
+    whole = pltpu.make_async_copy(image, sent, sem)
+    whole.start()
+    whole.wait()
+
+
+def edge_part(target, rest, coupling, row_two, row_one, side_two, side_one, image):
     vmem = pl.BlockSpec(memory_space=pltpu.VMEM)
-    return pl.pallas_call(
+    _, sent = pl.pallas_call(
         edge_kernel,
-        in_specs=[pl.BlockSpec(memory_space=pltpu.SMEM)] + [vmem] * 6 + [pl.BlockSpec(memory_space=pltpu.HBM)],
-        out_specs=pl.BlockSpec(memory_space=pltpu.HBM),
-        out_shape=pltpu.HBM(sent.shape, sent.dtype),
-        scratch_shapes=[pltpu.VMEM(rest.shape, BF16), pltpu.SemaphoreType.DMA],
+        in_specs=[pl.BlockSpec(memory_space=pltpu.SMEM)] + [vmem] * 7,
+        out_specs=[vmem, pl.BlockSpec(memory_space=pltpu.HBM)],
+        out_shape=[pltpu.VMEM(image.shape, BF16), pltpu.HBM(image.shape, BF16)],
+        scratch_shapes=[pltpu.SemaphoreType.DMA],
         input_output_aliases={7: 0},
         compiler_params=pltpu.CompilerParams(vmem_limit_bytes=16 * MIB),
         cost_estimate=pl.CostEstimate(flops=2 * 10**8, bytes_accessed=2 * MIB, transcendentals=0),
-    )(target, rest, coupling, row_one, row_two, side_one, side_two, sent)
+    )(target, rest, coupling, row_two, row_one, side_two, side_one, image)
+    return sent
 
 
 def sweep_kernel(strip, state, ghosts, rate, shift, out, done, sem):
@@ -392,16 +384,13 @@
     patch_count = fields.shape[0]
     slots = devices * SLOTS_EACH
 
-    leaf, row_one, row_two, sides, target, coupling, spread = first_part(
-        leaflet, new_owner.reshape(1, patch_count), stiffness
-    )
+    leaf, row_one, row_two, sides = first_part(leaflet)
+    side_two = exchange(sides, "azim", 1)
     side_one = exchange(sides, "azim", 0)
-    side_two = exchange(sides, "azim", 1)
+    row_two = exchange(row_two, "axial", 1)
     row_one = exchange(row_one, "axial", 0)
-    row_two = exchange(row_two, "axial", 1)
-    held, lap, sent = laplace(to_tiles(fields), leaf, slots)
-    sent, rest = main_part(target, held, lap, spread, sent)
-    sent = edge_part(target, rest, coupling, row_one, row_two, side_one, side_two, sent)
+    image, rest, target, coupling = main_part(to_tiles(fields), leaf, new_owner.reshape(1, patch_count), stiffness, slots)
+    sent = edge_part(target, rest, coupling, row_two, row_one, side_two, side_one, image)
     arrived = lax.all_to_all(sent.reshape(devices, -1, LANES), ALL, split_axis=0, concat_axis=0, tiled=True)
     state = arrived.reshape(slots, -1, LANES)
 

time: 58.8 us -> 59.2 us (level)
    ppermute x4, starting transfers between devices: 9.06 us -> 9.99 us  [exchange(): return lax.ppermute(x, axis, pairs + [(j, i) for i, j in pairs])]
    all_to_all x1, starting transfers between devices: 6.22 us -> 5.3 us  [shards(): lax.all_to_all(sent.reshape(devices, -1, LANES), ALL, split_axis=0, conca...]
    pallas_call x3 -> x2, Pallas kernels: 7.2 us -> 7.23 us  [the longest x1 4.53 us: main_part(): pl.pallas_call(main_kernel, in_specs=[hbm, vmem, hbm, hbm], out_specs=[vm...]
  transfers between devices with their start and end apart: 5 -> 5, of which waited for: 1 -> 1; matrix products, arithmetic and copies ran while one was open for 1% -> 1% of each run, Pallas kernels for 7% -> 8%
where the time goes in v5:
time: 59.2 us; the launch traced here: 59 us
  waiting for transfers between devices  29.1 us (49%)
  starting transfers between devices  15.3 us (26%)
  Pallas kernels  13.7 us (23%)
    all_to_all x1, waiting for transfers between devices, shards(): lax.all_to_all(sent.reshape(devices, -1, LANES), ALL, split_axis=0, conca...  29.1 us
    ppermute x4, starting transfers between devices, exchange(): return lax.ppermute(x, axis, pairs + [(j, i) for i, j in pairs])  9.99 us
    all_to_all x1, starting transfers between devices, shards(): lax.all_to_all(sent.reshape(devices, -1, LANES), ALL, split_axis=0, conca...  5.3 us
    pallas_call x1, Pallas kernels, main_part(): pl.pallas_call(main_kernel, in_specs=[hbm, vmem, hbm, hbm], out_specs=[vm...  4.53 us
    pallas_call x1, Pallas kernels, sweeps(): pl.pallas_call(sweep_kernel, in_specs=[pl.BlockSpec(memory_space=pltpu.SM...  4.05 us
    pallas_call x1, Pallas kernels, first_part(): pl.pallas_call(first_kernel, in_specs=[pl.BlockSpec(memory_space=pltpu.HB...  2.7 us
    pallas_call x1, Pallas kernels, edge_part(): pl.pallas_call(edge_kernel, in_specs=[pl.BlockSpec(memory_space=pltpu.SME...  2.43 us
  transfers between devices with their start and end apart: 5, of which 1 were waited for; matrix products, arithmetic and copies ran while one was open for 1% of the time, Pallas kernels for 8%

profile of v5, /device:TPU:1, one launch (start us, length us, event | category | flops | bytes accessed | tf_op | source)
XLA Modules:
  0.0 59.0 jit_solution(3706571963666874366)
XLA Ops:
  0.0 2.7 %shard_map.91 = (bf16[64,32,256]{2,1,0:T(8,128)(2,1)S(1)}, bf16[64,256]{1,0:T(8,128)(2,1)S(1)}, bf16[64,256]{1,0:T(8,128)(2,1)S(1)}, bf16[64,128]{1,0:T(8,128)(2,1)S(1)}) custom-call(bf16[64,32,256]{2,1,0:T(8,128)(2,1)} %leaf_hbm.1), custom_call_target="tpu_custom_call" | custom-call | flops 100000000 | bytes 1048576 | tf_op jit(solution)/shard_map/pallas_call | solution.py:79
  2.7 5.8 %collective-permute-start.2 = (bf16[64,128]{1,0:T(8,128)(2,1)S(1)}, bf16[64,128]{1,0:T(8,128)(2,1)S(1)}, u32[]{:S(2)}, u32[]{:S(2)}) collective-permute-start(bf16[64,128]{1,0:T(8,128)(2,1)S(1)} %get-tuple-element.20), channel_id=1, source_target_pairs={{1,2},{3,4},{5,6},{7,8},{9,10},{11,12},{13,14},{15,0},{2,1},{4,3},... | collective-permute-start | bytes 49160 | tf_op jit(solution)/shard_map/ppermute | solution.py:93
  8.5 0.0 collective-permute-start.3
  8.5 2.5 %collective-permute-start = (bf16[64,256]{1,0:T(8,128)(2,1)S(1)}, bf16[64,256]{1,0:T(8,128)(2,1)S(1)}, u32[]{:S(2)}, u32[]{:S(2)}) collective-permute-start(bf16[64,256]{1,0:T(8,128)(2,1)S(1)} %get-tuple-element.18), channel_id=1, source_target_pairs={{16,32},{48,64},{80,96},{112,0},{32,16},{64,48},{96,80},{0,112},{1... | collective-permute-start | bytes 98312 | tf_op jit(solution)/shard_map/ppermute | solution.py:93
  11.0 1.7 %collective-permute-start.1 = (bf16[64,256]{1,0:T(8,128)(2,1)S(1)}, bf16[64,256]{1,0:T(8,128)(2,1)S(1)}, u32[]{:S(2)}, u32[]{:S(2)}) collective-permute-start(bf16[64,256]{1,0:T(8,128)(2,1)S(1)} %get-tuple-element.19), channel_id=1, source_target_pairs={{0,16},{32,48},{64,80},{96,112},{16,0},{48,32},{80,64},{112,96},{1... | collective-permute-start | bytes 98312 | tf_op jit(solution)/shard_map/ppermute | solution.py:93
  12.7 4.5 %shard_map.92 = (bf16[256,32,128]{2,1,0:T(8,128)(2,1)S(1)}, f32[68,32,128]{2,1,0:T(8,128)S(1)}, s32[1,128]{1,0:T(1,128)S(1)}, bf16[64,64]{1,0:T(8,128)(2,1)S(1)}) custom-call(f32[128,32,128]{2,1,0:T(8,128)} %bitcast.21, bf16[64,32,256]{2,1,0:T(8,128)(2,1)S(1)} %get-tuple-element.14.leaf, s32[1,128]{1,0:T(1,128)} %bitcast.22, bf16[64,64]{1,0:T(8,128)(2,1)} %stiff_hbm.1), custom_call_target="tpu_custom_call" | custom-call | flops 2000000000 | bytes 8388608 | tf_op jit(solution)/shard_map/pallas_call | solution.py:214
  17.2 0.0 collective-permute-done.2.side_two
  17.2 0.0 collective-permute-done.3.side_one
  17.3 0.0 collective-permute-done.row_two
  17.3 0.0 collective-permute-done.1.row_one
  17.3 2.4 %shard_map.93 = (bf16[256,32,128]{2,1,0:T(8,128)(2,1)S(1)}, bf16[256,32,128]{2,1,0:T(8,128)(2,1)}) custom-call(s32[1,128]{1,0:T(1,128)S(1)} %get-tuple-element.15.target, f32[68,32,128]{2,1,0:T(8,128)S(1)} %get-tuple-element.16.rest, bf16[64,64]{1,0:T(8,128)(2,1)S(1)} %get-tuple-element.17.coupling, ...), custom_call_target="tpu_custom_call", output_to_operand_aliasing={{0}: (7, {})} | custom-call | flops 200000000 | bytes 2097152 | tf_op jit(solution)/shard_map/pallas_call | solution.py:288
  19.7 0.0 copy-start.2
  19.7 0.0 copy-start.3
  19.7 0.0 copy-start.4
  19.8 0.0 copy-start
  19.8 0.0 copy-start.1
  19.8 5.3 %all-to-all-start = ((bf16[128,64,128]{2,1,0:T(8,128)(2,1)}), bf16[128,64,128]{2,1,0:T(8,128)(2,1)S(1)}, u32[]{:S(2)}, u32[]{:S(2)}) async-start(bf16[128,64,128]{2,1,0:T(8,128)(2,1)} %bitcast.19), calls=%async_computation | async-start | bytes 4194304 | tf_op jit(solution)/shard_map/all_to_all | solution.py:394
  25.1 0.1 dot_general.5
  25.2 0.2 fusion
  25.5 0.1 copy.18
  25.6 0.1 pad_maximum_fusion.1
  25.7 29.1 %all-to-all-done = bf16[128,64,128]{2,1,0:T(8,128)(2,1)S(1)} async-done(((bf16[128,64,128]{2,1,0:T(8,128)(2,1)}), bf16[128,64,128]{2,1,0:T(8,128)(2,1)S(1)}, u32[]{:S(2)}, u32[]{:S(2)}) %all-to-all-start) | async-done | bytes 2097184 | tf_op jit(solution)/shard_map/all_to_all | solution.py:394
  54.9 0.1 broadcast_in_dim.2.rate
  54.9 4.1 %shard_map.94 = f32[256,32,128]{2,1,0:T(8,128)} custom-call(s32[256]{0:T(256)S(1)} %copy-done.1, bf16[256,32,128]{2,1,0:T(8,128)(2,1)S(1)} %bitcast.18, f32[64,8,128]{2,1,0:T(8,128)S(1)} %pad_maximum_fusion.ghosts, f32[8,128]{1,0:T(8,128)S(1)} %broadcast_in_dim.2.rate, bf16[256,256]{1,0:T(8,128)(2,1)S(1)} %copy-done), custom_call_target="tpu_custom_call" | custom-call | tf_op jit(solution)/shard_map/pallas_call | solution.py:360
  (6 shorter events, 0.1 us)
Async XLA Ops:
  2.7 14.5 %collective-permute-start.2 = (bf16[64,128]{1,0:T(8,128)(2,1)S(1)}, bf16[64,128]{1,0:T(8,128)(2,1)S(1)}, u32[]{:S(2)}, u32[]{:S(2)}) collective-permute-start(bf16[64,128]{1,0:T(8,128)(2,1)S(1)} %get-tuple-element.20), channel_id=1, source_target_pairs={{1,2},{3,4},{5,6},{7,8},{9,10},{11,12},{13,14},{15,0},{2,1},{4,3},... | collective-permute-start | bytes 49160 | tf_op jit(solution)/shard_map/ppermute | solution.py:93
  8.5 8.7 %collective-permute-start.3 = (bf16[64,128]{1,0:T(8,128)(2,1)S(1)}, bf16[64,128]{1,0:T(8,128)(2,1)S(1)}, u32[]{:S(2)}, u32[]{:S(2)}) collective-permute-start(bf16[64,128]{1,0:T(8,128)(2,1)S(1)} %get-tuple-element.20), channel_id=1, source_target_pairs={{0,1},{2,3},{4,5},{6,7},{8,9},{10,11},{12,13},{14,15},{1,0},{3,2},... | collective-permute-start | bytes 49160 | tf_op jit(solution)/shard_map/ppermute | solution.py:93
  8.5 8.7 %collective-permute-start = (bf16[64,256]{1,0:T(8,128)(2,1)S(1)}, bf16[64,256]{1,0:T(8,128)(2,1)S(1)}, u32[]{:S(2)}, u32[]{:S(2)}) collective-permute-start(bf16[64,256]{1,0:T(8,128)(2,1)S(1)} %get-tuple-element.18), channel_id=1, source_target_pairs={{16,32},{48,64},{80,96},{112,0},{32,16},{64,48},{96,80},{0,112},{1... | collective-permute-start | bytes 98312 | tf_op jit(solution)/shard_map/ppermute | solution.py:93
  11.0 6.2 %collective-permute-start.1 = (bf16[64,256]{1,0:T(8,128)(2,1)S(1)}, bf16[64,256]{1,0:T(8,128)(2,1)S(1)}, u32[]{:S(2)}, u32[]{:S(2)}) collective-permute-start(bf16[64,256]{1,0:T(8,128)(2,1)S(1)} %get-tuple-element.19), channel_id=1, source_target_pairs={{0,16},{32,48},{64,80},{96,112},{16,0},{48,32},{80,64},{112,96},{1... | collective-permute-start | bytes 98312 | tf_op jit(solution)/shard_map/ppermute | solution.py:93
  19.7 5.4 %copy-start.2 = (f32[64,256]{1,0:T(8,128)S(1)}, f32[64,256]{1,0:T(8,128)}, u32[]{:S(2)}) copy-start(f32[64,256]{1,0:T(8,128)} %param.13) | copy-start | bytes 196612
  19.7 5.5 %copy-start.3 = (f32[64,128,1]{1,0,2:T(8,128)S(1)}, f32[64,128,1]{1,0,2:T(8,128)}, u32[]{:S(2)}) copy-start(f32[64,128,1]{1,0,2:T(8,128)} %constant.7) | copy-start | bytes 98308
  19.7 5.8 %copy-start.4 = (f32[4]{0:T(128)S(1)}, f32[4]{0:T(128)}, u32[]{:S(2)}) copy-start(f32[4]{0:T(128)} %param.15) | copy-start | bytes 52
  19.8 35.2 %copy-start = (bf16[256,256]{1,0:T(8,128)(2,1)S(1)}, bf16[256,256]{1,0:T(8,128)(2,1)}, u32[]{:S(2)}) copy-start(bf16[256,256]{1,0:T(8,128)(2,1)} %constant.5.clone.shift) | copy-start | bytes 393220
  19.8 35.2 %copy-start.1 = (s32[256]{0:T(256)S(1)}, s32[256]{0:T(256)}, u32[]{:S(2)}) copy-start(s32[256]{0:T(256)} %strip.1) | copy-start | bytes 3076
  19.8 35.1 %all-to-all-start = ((bf16[128,64,128]{2,1,0:T(8,128)(2,1)}), bf16[128,64,128]{2,1,0:T(8,128)(2,1)S(1)}, u32[]{:S(2)}, u32[]{:S(2)}) async-start(bf16[128,64,128]{2,1,0:T(8,128)(2,1)} %bitcast.19), calls=%async_computation | async-start | bytes 4194304 | tf_op jit(solution)/shard_map/all_to_all | solution.py:394

commit v6 on v4

--- a/solution.py
+++ b/solution.py
@@ -41,99 +41,54 @@
     return pltpu.with_memory_space_constraint(x, pltpu.HBM)
 
 
+def in_vmem(x):
+    return pltpu.with_memory_space_constraint(x, pltpu.VMEM)
+
+
 def where_one(mask):
     return jnp.where(mask, 1.0, 0.0).astype(BF16)
 
 
-def first_kernel(
-    leaf_hbm, owner_hbm, stiff_hbm, leaf, one, two, sides, target, coupling, spread, owner, stiffness, load_sem, small_sem
+def first_kernel(leaf, one, two, sides):
+    records, rows, cols = leaf.shape
+    half = rows // 2
+    odd = lax.axis_index("axial") % 2
+    spot = jnp.where(iota((cols, LANES), 1) // rows % 2 == 0, 0, cols - 1)
+    wide = dot(leaf[...].reshape(-1, cols), where_one(iota((cols, LANES), 0) == spot))
+    r = iota((records * rows, LANES), 0) % rows
+    wide = jnp.where(iota((records * rows, LANES), 1) % rows == r, wide, 0.0).astype(BF16)
+    gather = iota((records, records * rows), 1) // rows == iota((records, records * rows), 0)
+    sides[...] = dot(where_one(gather), wide).astype(BF16)
+    pick = iota((records, records * half), 1) - iota((records, records * half), 0) * half
+    first = dot(where_one(pick == 0), leaf[:, :half].reshape(-1, cols))
+    last = dot(where_one(pick == half - 1), leaf[:, half:].reshape(-1, cols))
+    one[...] = jnp.where(odd == 0, last, first).astype(BF16)
+    two[...] = jnp.where(odd == 0, first, last).astype(BF16)
+
+
+def first_part(leaf):
+    records, rows, cols = leaf.shape
+    vmem = pl.BlockSpec(memory_space=pltpu.VMEM)
+    shapes = [(records, cols), (records, cols), (records, LANES)]
+    return pl.pallas_call(
+        first_kernel,
+        in_specs=[vmem],
+        out_specs=[vmem] * 3,
+        out_shape=[pltpu.VMEM(s, BF16) for s in shapes],
+        compiler_params=pltpu.CompilerParams(vmem_limit_bytes=16 * MIB),
+        cost_estimate=pl.CostEstimate(flops=10**8, bytes_accessed=MIB, transcendentals=0),
+    )(leaf)
+
+
+def laplace_kernel(
+    leaf, owner_hbm, stiff_hbm, lap, sent, target, coupling, spread, zero, owner, stiffness, zero_sem, small_sem
 ):
-    records, rows, cols = leaf.shape
     small = [
         pltpu.make_async_copy(owner_hbm, owner, small_sem.at[0]),
         pltpu.make_async_copy(stiff_hbm, stiffness, small_sem.at[1]),
     ]
     for c in small:
         c.start()
-    size = 16
-    loads = []
-    for n in range(records // size):
-        part = pl.ds(n * size, size)
-        loads.append(pltpu.make_async_copy(leaf_hbm.at[part], leaf.at[part], load_sem.at[n]))
-        loads[n].start()
-
-    small[0].wait()
-    devices, patches = LANES, owner.shape[1]
-    mine = owner[...] == iota((devices, patches), 0)
-    before = where_one(iota((patches, patches), 0) < iota((patches, patches), 1))
-    earlier = dot(where_one(mine), before)
-    ranked = jnp.sum(jnp.where(mine, earlier, 0.0), axis=0, keepdims=True)
-    target[...] = owner[...] * SLOTS_EACH + ranked.astype(jnp.int32)
-
-    small[1].wait()
-    half = records // 2
-    a, b = iota((records, records), 0), iota((records, records), 1)
-    old = a % FIELDS * (records // FIELDS) + a % half // FIELDS * 2 + a // half
-    ordered = (dot(where_one(b == old), stiffness[...]) * SPREAD).astype(BF16)
-    coupling[...] = ordered
-
-    wide = records * SUB
-    lift = where_one(iota((records, wide), 1) // SUB == iota((records, wide), 0))
-    lifted = dot(ordered, lift)
-    within = iota((half, wide), 1) % SUB
-    for p in range(2):
-        for r in range(SUB):
-            part = jnp.where(within == r, lifted[p * half : (p + 1) * half], 0.0)
-            at = (p * SUB + r) * half
-            spread[at : at + half] = part.astype(BF16)
-
-    odd = lax.axis_index("axial") % 2
-    a, b = iota((2 * size, size * rows), 0), iota((2 * size, size * rows), 1)
-    pick = jnp.where((a // size + odd) % 2 == 0, rows - 1, 0)
-    ends = where_one(b == a % size * rows + pick)
-    spot = jnp.where(iota((cols, LANES), 1) // rows % 2 == 0, 0, cols - 1)
-    spot = where_one(iota((cols, LANES), 0) == spot)
-    mine = iota((size * rows, LANES), 1) % rows == iota((size * rows, LANES), 0) % rows
-    gather = where_one(iota((size, size * rows), 1) // rows == iota((size, size * rows), 0))
-    for n in range(records // size):
-        loads[n].wait()
-        part = slice(n * size, (n + 1) * size)
-        x = leaf[part].reshape(size * rows, cols)
-        both = dot(ends, x).astype(BF16)
-        one[part] = both[:size]
-        two[part] = both[size:]
-        sides[part] = dot(gather, jnp.where(mine, dot(x, spot), 0.0).astype(BF16)).astype(BF16)
-
-
-def first_part(leaf, owner, stiffness):
-    records, rows, cols = leaf.shape
-    vmem = pl.BlockSpec(memory_space=pltpu.VMEM)
-    hbm = pl.BlockSpec(memory_space=pltpu.HBM)
-    shapes = [leaf.shape, (records, cols), (records, cols), (records, LANES)]
-    return pl.pallas_call(
-        first_kernel,
-        in_specs=[hbm] * 3,
-        out_specs=[vmem] * 7,
-        out_shape=[pltpu.VMEM(s, BF16) for s in shapes]
-        + [
-            jax.ShapeDtypeStruct(owner.shape, jnp.int32),
-            pltpu.VMEM((records, records), BF16),
-            pltpu.VMEM((records * SUB, records * SUB), BF16),
-        ],
-        scratch_shapes=[
-            pltpu.VMEM(owner.shape, jnp.int32),
-            pltpu.VMEM(stiffness.shape, BF16),
-            pltpu.SemaphoreType.DMA((records // 16,)),
-            pltpu.SemaphoreType.DMA((2,)),
-        ],
-        compiler_params=pltpu.CompilerParams(vmem_limit_bytes=16 * MIB),
-        cost_estimate=pl.CostEstimate(flops=10**8, bytes_accessed=MIB, transcendentals=0),
-    )(in_hbm(leaf), in_hbm(owner), in_hbm(stiffness))
-
-
-def laplace_kernel(fields_hbm, leaf, fields, lap, sent, zero, sem, zero_sem):
-    load = pltpu.make_async_copy(fields_hbm, fields, sem)
-    load.start()
     zero[...] = jnp.zeros_like(zero)
     count = zero.shape[0]
     clears = [
@@ -142,6 +97,7 @@
     for c in clears:
         c.start()
     records, rows, cols = leaf.shape
+
     group = 256 // rows
     a, b = iota((group * rows, group * rows), 0), iota((group * rows, group * rows), 1)
     beside = where_one((jnp.abs(a - b) == 1) & (a // rows == b // rows))
@@ -153,32 +109,60 @@
         for n in range(rows // SUB):
             part = y[:, n * SUB : (n + 1) * SUB].reshape(group * SUB, cols)
             lap[n, g * group * SUB : (g + 1) * group * SUB] = part.astype(BF16)
+    small[0].wait()
+    devices, patches = LANES, owner.shape[1]
+    mine = owner[...] == iota((devices, patches), 0)
+    before = where_one(iota((patches, patches), 0) < iota((patches, patches), 1))
+    earlier = dot(where_one(mine), before)
+    ranked = jnp.sum(jnp.where(mine, earlier, 0.0), axis=0, keepdims=True)
+    target[...] = owner[...] * SLOTS_EACH + ranked.astype(jnp.int32)
+
+    small[1].wait()
+    half = records // 2
+    a, b = iota((records, records), 0), iota((records, records), 1)
+    old = a % FIELDS * (records // FIELDS) + a % half // FIELDS * 2 + a // half
+    ordered = (dot(where_one(b == old), stiffness[...]) * SPREAD).astype(BF16)
+    coupling[...] = ordered
+
+    wide = records * SUB
+    lift = where_one(iota((records, wide), 1) // SUB == iota((records, wide), 0))
+    lifted = dot(ordered, lift)
+    within = iota((half, wide), 1) % SUB
+    for p in range(2):
+        for r in range(SUB):
+            part = jnp.where(within == r, lifted[p * half : (p + 1) * half], 0.0)
+            at = (p * SUB + r) * half
+            spread[at : at + half] = part.astype(BF16)
     for c in clears:
         c.wait()
-    load.wait()
-
-
-def laplace(fields, leaf, slots):
+
+
+def laplace(leaf, owner, stiffness, slots):
     records, rows, cols = leaf.shape
     vmem = pl.BlockSpec(memory_space=pltpu.VMEM)
     hbm = pl.BlockSpec(memory_space=pltpu.HBM)
+    tile = (records // 2, LANES)
     return pl.pallas_call(
         laplace_kernel,
-        in_specs=[hbm, vmem],
-        out_specs=[vmem, vmem, hbm],
+        in_specs=[vmem, hbm, hbm],
+        out_specs=[vmem, hbm, vmem, vmem, vmem],
         out_shape=[
-            pltpu.VMEM(fields.shape, F32),
             pltpu.VMEM((rows // SUB, records * SUB, cols), BF16),
-            pltpu.HBM((slots,) + fields.shape[1:], BF16),
+            pltpu.HBM((slots,) + tile, BF16),
+            jax.ShapeDtypeStruct(owner.shape, jnp.int32),
+            pltpu.VMEM((records, records), BF16),
+            pltpu.VMEM((records * SUB, records * SUB), BF16),
         ],
         scratch_shapes=[
-            pltpu.VMEM((32,) + fields.shape[1:], BF16),
+            pltpu.VMEM((32,) + tile, BF16),
+            pltpu.VMEM(owner.shape, jnp.int32),
+            pltpu.VMEM(stiffness.shape, BF16),
             pltpu.SemaphoreType.DMA,
-            pltpu.SemaphoreType.DMA,
+            pltpu.SemaphoreType.DMA((2,)),
         ],
         compiler_params=pltpu.CompilerParams(vmem_limit_bytes=16 * MIB),
         cost_estimate=pl.CostEstimate(flops=5 * 10**8, bytes_accessed=3 * MIB, transcendentals=0),
-    )(in_hbm(fields), leaf)
+    )(leaf, in_hbm(owner), in_hbm(stiffness))
 
 
 def exchange(x, axis, offset):
@@ -245,7 +229,7 @@
     )(target, fields, lap, spread, sent)
 
 
-def edge_kernel(target, rest, coupling, row_one, row_two, side_one, side_two, sent_in, sent, stage, sem):
+def edge_kernel(target, rest, coupling, row_two, row_one, side_two, side_one, sent_in, sent, stage, sem):
     del sent_in
     records, cols = row_one.shape
     half = records // 2
@@ -292,7 +276,7 @@
     pltpu.make_async_copy(stage, sent.at[pl.ds(0, count)], sem).wait()
 
 
-def edge_part(target, rest, coupling, row_one, row_two, side_one, side_two, sent):
+def edge_part(target, rest, coupling, row_two, row_one, side_two, side_one, sent):
     vmem = pl.BlockSpec(memory_space=pltpu.VMEM)
     return pl.pallas_call(
         edge_kernel,
@@ -303,7 +287,7 @@
         input_output_aliases={7: 0},
         compiler_params=pltpu.CompilerParams(vmem_limit_bytes=16 * MIB),
         cost_estimate=pl.CostEstimate(flops=2 * 10**8, bytes_accessed=2 * MIB, transcendentals=0),
-    )(target, rest, coupling, row_one, row_two, side_one, side_two, sent)
+    )(target, rest, coupling, row_two, row_one, side_two, side_one, sent)
 
 
 def sweep_kernel(strip, state, ghosts, rate, shift, out, done, sem):
@@ -323,7 +307,7 @@
         new = []
         for k in range(tiles):
             vertical = jnp.where(first, ext[k], jnp.where(last, ext[k + 2], ext[k + 1]))
-            new.append(x[k] + v * ((flat[k] + across[k]) + vertical))
+            new.append(x[k] + v * (flat[k] + vertical))
         return new
 
     def one(c, _):
@@ -359,6 +343,7 @@
         for j in (i - 1, i + 1):
             if 0 <= j and j // PC == i // PC:
                 table[i, j] = 1.0
+        table[i, (i + PC) % LANES] = 1.0
         table[i, LANES + (i + PC) % LANES] = 1.0
     return np.concatenate([table, table], axis=0)
 
@@ -392,16 +377,16 @@
     patch_count = fields.shape[0]
     slots = devices * SLOTS_EACH
 
-    leaf, row_one, row_two, sides, target, coupling, spread = first_part(
-        leaflet, new_owner.reshape(1, patch_count), stiffness
-    )
+    leaf = in_vmem(leaflet)
+    row_one, row_two, sides = first_part(leaf)
+    side_two = exchange(sides, "azim", 1)
     side_one = exchange(sides, "azim", 0)
-    side_two = exchange(sides, "azim", 1)
+    row_two = exchange(row_two, "axial", 1)
     row_one = exchange(row_one, "axial", 0)
-    row_two = exchange(row_two, "axial", 1)
-    held, lap, sent = laplace(to_tiles(fields), leaf, slots)
+    lap, sent, target, coupling, spread = laplace(leaf, new_owner.reshape(1, patch_count), stiffness, slots)
+    held = in_vmem(to_tiles(fields))
     sent, rest = main_part(target, held, lap, spread, sent)
-    sent = edge_part(target, rest, coupling, row_one, row_two, side_one, side_two, sent)
+    sent = edge_part(target, rest, coupling, row_two, row_one, side_two, side_one, sent)
     arrived = lax.all_to_all(sent.reshape(devices, -1, LANES), ALL, split_axis=0, concat_axis=0, tiled=True)
     state = arrived.reshape(slots, -1, LANES)
 

time: 58.8 us -> 57.8 us (0.983)
  Pallas kernels: 13.2 us -> 10.9 us
  local copies, waits for them, and re-layouts: 0.3 us -> 1.68 us
    pallas_call x2, Pallas kernels: 5.05 us -> 3.03 us  [the longest x1 1.94 us: laplace(): pl.pallas_call(laplace_kernel, in_specs=[vmem, hbm, hbm], out_specs=[vmem...]
    unnamed x10 -> x14, local copies, waits for them, and re-layouts: 0.03 us -> 1.41 us
    ppermute x4, starting transfers between devices: 9.06 us -> 9.99 us  [exchange(): return lax.ppermute(x, axis, pairs + [(j, i) for i, j in pairs])]
    all_to_all x1, starting transfers between devices: 6.22 us -> 5.3 us  [shards(): lax.all_to_all(sent.reshape(devices, -1, LANES), ALL, split_axis=0, conca...]
where the time goes in v6:
time: 57.8 us; the launch traced here: 57.6 us
  waiting for transfers between devices  29.1 us (50%)
  starting transfers between devices  15.3 us (26%)
  Pallas kernels  10.9 us (19%)
  local copies, waits for them, and re-layouts  1.68 us (3%)
    all_to_all x1, waiting for transfers between devices, shards(): lax.all_to_all(sent.reshape(devices, -1, LANES), ALL, split_axis=0, conca...  29.1 us
    ppermute x4, starting transfers between devices, exchange(): return lax.ppermute(x, axis, pairs + [(j, i) for i, j in pairs])  9.99 us
    all_to_all x1, starting transfers between devices, shards(): lax.all_to_all(sent.reshape(devices, -1, LANES), ALL, split_axis=0, conca...  5.3 us
    pallas_call x1, Pallas kernels, sweeps(): pl.pallas_call(sweep_kernel, in_specs=[pl.BlockSpec(memory_space=pltpu.SM...  3.84 us
    pallas_call x1, Pallas kernels, main_part(): pl.pallas_call(main_kernel, in_specs=[pl.BlockSpec(memory_space=pltpu.SME...  2.13 us
    pallas_call x1, Pallas kernels, laplace(): pl.pallas_call(laplace_kernel, in_specs=[vmem, hbm, hbm], out_specs=[vmem...  1.94 us
    pallas_call x1, Pallas kernels, edge_part(): pl.pallas_call(edge_kernel, in_specs=[pl.BlockSpec(memory_space=pltpu.SME...  1.9 us
    unnamed x14, local copies, waits for them, and re-layouts  1.41 us
  transfers between devices with their start and end apart: 5, of which 1 were waited for; matrix products, arithmetic and copies ran while one was open for 1% of the time, Pallas kernels for 7%

profile of v6, /device:TPU:1, one launch (start us, length us, event | category | flops | bytes accessed | tf_op | source)
XLA Modules:
  0.0 57.6 jit_solution(3278949668377731835)
XLA Ops:
  0.0 1.4 %copy-done.1 = bf16[64,32,256]{2,1,0:T(8,128)(2,1)S(1)} copy-done((bf16[64,32,256]{2,1,0:T(8,128)(2,1)S(1)}, bf16[64,32,256]{2,1,0:T(8,128)(2,1)}, u32[]{:S(2)}) %copy-start.1) | copy-done | bytes 1048600
  1.4 1.1 %shard_map.93 = (bf16[64,256]{1,0:T(8,128)(2,1)S(1)}, bf16[64,256]{1,0:T(8,128)(2,1)S(1)}, bf16[64,128]{1,0:T(8,128)(2,1)S(1)}) custom-call(bf16[64,32,256]{2,1,0:T(8,128)(2,1)S(1)} %copy-done.1), custom_call_target="tpu_custom_call" | custom-call | flops 100000000 | bytes 1048576 | tf_op jit(solution)/shard_map/pallas_call | solution.py:73
  2.5 5.8 %collective-permute-start.2 = (bf16[64,128]{1,0:T(8,128)(2,1)S(1)}, bf16[64,128]{1,0:T(8,128)(2,1)S(1)}, u32[]{:S(2)}, u32[]{:S(2)}) collective-permute-start(bf16[64,128]{1,0:T(8,128)(2,1)S(1)} %get-tuple-element.23), channel_id=1, source_target_pairs={{1,2},{3,4},{5,6},{7,8},{9,10},{11,12},{13,14},{15,0},{2,1},{4,3},... | collective-permute-start | bytes 49160 | tf_op jit(solution)/shard_map/ppermute | solution.py:171
  8.3 0.0 collective-permute-start.3
  8.3 2.5 %collective-permute-start = (bf16[64,256]{1,0:T(8,128)(2,1)S(1)}, bf16[64,256]{1,0:T(8,128)(2,1)S(1)}, u32[]{:S(2)}, u32[]{:S(2)}) collective-permute-start(bf16[64,256]{1,0:T(8,128)(2,1)S(1)} %get-tuple-element.21), channel_id=1, source_target_pairs={{16,32},{48,64},{80,96},{112,0},{32,16},{64,48},{96,80},{0,112},{1... | collective-permute-start | bytes 98312 | tf_op jit(solution)/shard_map/ppermute | solution.py:171
  10.8 1.7 %collective-permute-start.1 = (bf16[64,256]{1,0:T(8,128)(2,1)S(1)}, bf16[64,256]{1,0:T(8,128)(2,1)S(1)}, u32[]{:S(2)}, u32[]{:S(2)}) collective-permute-start(bf16[64,256]{1,0:T(8,128)(2,1)S(1)} %get-tuple-element.22), channel_id=1, source_target_pairs={{0,16},{32,48},{64,80},{96,112},{16,0},{48,32},{80,64},{112,96},{1... | collective-permute-start | bytes 98312 | tf_op jit(solution)/shard_map/ppermute | solution.py:171
  12.5 1.9 %shard_map.91 = (bf16[4,512,256]{2,1,0:T(8,128)(2,1)S(1)}, bf16[256,32,128]{2,1,0:T(8,128)(2,1)}, s32[1,128]{1,0:T(1,128)S(1)}, bf16[64,64]{1,0:T(8,128)(2,1)S(1)}, bf16[512,512]{1,0:T(8,128)(2,1)S(1)}) custom-call(bf16[64,32,256]{2,1,0:T(8,128)(2,1)S(1)} %copy-done.1, s32[1,128]{1,0:T(1,128)} %bitcast.22, bf16[64,64]{1,0:T(8,128)(2,1)} %stiff_hbm.1), custom_call_target="tpu_custom_call" | custom-call | flops 500000000 | bytes 3145728 | tf_op jit(solution)/shard_map/pallas_call | solution.py:145
  14.4 2.1 %shard_map.92 = (bf16[256,32,128]{2,1,0:T(8,128)(2,1)}, f32[68,32,128]{2,1,0:T(8,128)S(1)}) custom-call(s32[1,128]{1,0:T(1,128)S(1)} %get-tuple-element.15.target, f32[128,32,128]{2,1,0:T(8,128)S(1)} %bitcast.19, bf16[4,512,256]{2,1,0:T(8,128)(2,1)S(1)} %get-tuple-element.16.lap, ...), custom_call_target="tpu_custom_call", output_to_operand_aliasing={{0}: (4, {})} | custom-call | flops 1000000000 | bytes 4194304 | tf_op jit(solution)/shard_map/pallas_call | solution.py:220
  16.6 0.0 collective-permute-done.2.side_two
  16.6 0.0 collective-permute-done.3.side_one
  16.6 1.9 %shard_map.94 = bf16[256,32,128]{2,1,0:T(8,128)(2,1)} custom-call(s32[1,128]{1,0:T(1,128)S(1)} %get-tuple-element.15.target, f32[68,32,128]{2,1,0:T(8,128)S(1)} %get-tuple-element.19.rest, bf16[64,64]{1,0:T(8,128)(2,1)S(1)} %get-tuple-element.20.coupling, bf16[64,256]{1,0:T(8,128)(2,1)S(1)} %collective-permute-done.row_two, ...), custom_call_target="tpu_custom_call", output_to_operand_aliasing={{}: (7, {})} | custom-call | flops 200000000 | bytes 2097152 | tf_op jit(solution)/shard_map/pallas_call | solution.py:281
  18.5 0.0 copy-start.4
  18.5 0.0 copy-start.5
  18.5 0.0 copy-start.6
  18.6 0.0 copy-start.2
  18.6 0.0 copy-start.3
  18.6 5.3 %all-to-all-start = ((bf16[128,64,128]{2,1,0:T(8,128)(2,1)}), bf16[128,64,128]{2,1,0:T(8,128)(2,1)S(1)}, u32[]{:S(2)}, u32[]{:S(2)}) async-start(bf16[128,64,128]{2,1,0:T(8,128)(2,1)} %bitcast.20), calls=%async_computation | async-start | bytes 4194304 | tf_op jit(solution)/shard_map/all_to_all | solution.py:390
  23.9 0.1 dot_general.5
  24.0 0.2 fusion
  24.3 0.1 copy.19
  24.4 0.1 pad_maximum_fusion.1
  24.5 29.1 %all-to-all-done = bf16[128,64,128]{2,1,0:T(8,128)(2,1)S(1)} async-done(((bf16[128,64,128]{2,1,0:T(8,128)(2,1)}), bf16[128,64,128]{2,1,0:T(8,128)(2,1)S(1)}, u32[]{:S(2)}, u32[]{:S(2)}) %all-to-all-start) | async-done | bytes 2097184 | tf_op jit(solution)/shard_map/all_to_all | solution.py:390
  53.6 0.1 broadcast_in_dim.2.rate
  53.7 3.8 %shard_map.95 = f32[256,32,128]{2,1,0:T(8,128)} custom-call(s32[256]{0:T(256)S(1)} %copy-done.3, bf16[256,32,128]{2,1,0:T(8,128)(2,1)S(1)} %bitcast.18, f32[64,8,128]{2,1,0:T(8,128)S(1)} %pad_maximum_fusion.ghosts, f32[8,128]{1,0:T(8,128)S(1)} %broadcast_in_dim.2.rate, bf16[256,256]{1,0:T(8,128)(2,1)S(1)} %copy-done.2), custom_call_target="tpu_custom_call" | custom-call | tf_op jit(solution)/shard_map/pallas_call | solution.py:353
  (11 shorter events, 0.1 us)
Async XLA Ops:
  0.0 14.4 %copy-start = (f32[128,4,1024]{2,1,0:T(4,128)S(1)}, f32[128,4,1024]{2,1,0:T(4,128)}, u32[]{:S(2)}) copy-start(f32[128,4,1024]{2,1,0:T(4,128)} %param.9) | copy-start | bytes 6291460
  0.0 1.4 %copy-start.1 = (bf16[64,32,256]{2,1,0:T(8,128)(2,1)S(1)}, bf16[64,32,256]{2,1,0:T(8,128)(2,1)}, u32[]{:S(2)}) copy-start(bf16[64,32,256]{2,1,0:T(8,128)(2,1)} %leaf.3) | copy-start | bytes 3145732
  2.5 14.1 %collective-permute-start.2 = (bf16[64,128]{1,0:T(8,128)(2,1)S(1)}, bf16[64,128]{1,0:T(8,128)(2,1)S(1)}, u32[]{:S(2)}, u32[]{:S(2)}) collective-permute-start(bf16[64,128]{1,0:T(8,128)(2,1)S(1)} %get-tuple-element.23), channel_id=1, source_target_pairs={{1,2},{3,4},{5,6},{7,8},{9,10},{11,12},{13,14},{15,0},{2,1},{4,3},... | collective-permute-start | bytes 49160 | tf_op jit(solution)/shard_map/ppermute | solution.py:171
  8.3 8.3 %collective-permute-start.3 = (bf16[64,128]{1,0:T(8,128)(2,1)S(1)}, bf16[64,128]{1,0:T(8,128)(2,1)S(1)}, u32[]{:S(2)}, u32[]{:S(2)}) collective-permute-start(bf16[64,128]{1,0:T(8,128)(2,1)S(1)} %get-tuple-element.23), channel_id=1, source_target_pairs={{0,1},{2,3},{4,5},{6,7},{8,9},{10,11},{12,13},{14,15},{1,0},{3,2},... | collective-permute-start | bytes 49160 | tf_op jit(solution)/shard_map/ppermute | solution.py:171
  8.3 8.3 %collective-permute-start = (bf16[64,256]{1,0:T(8,128)(2,1)S(1)}, bf16[64,256]{1,0:T(8,128)(2,1)S(1)}, u32[]{:S(2)}, u32[]{:S(2)}) collective-permute-start(bf16[64,256]{1,0:T(8,128)(2,1)S(1)} %get-tuple-element.21), channel_id=1, source_target_pairs={{16,32},{48,64},{80,96},{112,0},{32,16},{64,48},{96,80},{0,112},{1... | collective-permute-start | bytes 98312 | tf_op jit(solution)/shard_map/ppermute | solution.py:171
  10.8 5.8 %collective-permute-start.1 = (bf16[64,256]{1,0:T(8,128)(2,1)S(1)}, bf16[64,256]{1,0:T(8,128)(2,1)S(1)}, u32[]{:S(2)}, u32[]{:S(2)}) collective-permute-start(bf16[64,256]{1,0:T(8,128)(2,1)S(1)} %get-tuple-element.22), channel_id=1, source_target_pairs={{0,16},{32,48},{64,80},{96,112},{16,0},{48,32},{80,64},{112,96},{1... | collective-permute-start | bytes 98312 | tf_op jit(solution)/shard_map/ppermute | solution.py:171
  18.5 5.4 %copy-start.4 = (f32[64,256]{1,0:T(8,128)S(1)}, f32[64,256]{1,0:T(8,128)}, u32[]{:S(2)}) copy-start(f32[64,256]{1,0:T(8,128)} %param.13) | copy-start | bytes 196612
  18.5 5.5 %copy-start.5 = (f32[64,128,1]{1,0,2:T(8,128)S(1)}, f32[64,128,1]{1,0,2:T(8,128)}, u32[]{:S(2)}) copy-start(f32[64,128,1]{1,0,2:T(8,128)} %constant.7) | copy-start | bytes 98308
  18.5 5.8 %copy-start.6 = (f32[4]{0:T(128)S(1)}, f32[4]{0:T(128)}, u32[]{:S(2)}) copy-start(f32[4]{0:T(128)} %param.15) | copy-start | bytes 52
  18.6 35.2 %copy-start.2 = (bf16[256,256]{1,0:T(8,128)(2,1)S(1)}, bf16[256,256]{1,0:T(8,128)(2,1)}, u32[]{:S(2)}) copy-start(bf16[256,256]{1,0:T(8,128)(2,1)} %constant.5.clone.shift) | copy-start | bytes 393220
  18.6 35.2 %copy-start.3 = (s32[256]{0:T(256)S(1)}, s32[256]{0:T(256)}, u32[]{:S(2)}) copy-start(s32[256]{0:T(256)} %strip.1) | copy-start | bytes 3076
  18.6 35.1 %all-to-all-start = ((bf16[128,64,128]{2,1,0:T(8,128)(2,1)}), bf16[128,64,128]{2,1,0:T(8,128)(2,1)S(1)}, u32[]{:S(2)}, u32[]{:S(2)}) async-start(bf16[128,64,128]{2,1,0:T(8,128)(2,1)} %bitcast.20), calls=%async_computation | async-start | bytes 4194304 | tf_op jit(solution)/shard_map/all_to_all | solution.py:390

commit v7 on v6

--- a/solution.py
+++ b/solution.py
@@ -81,20 +81,13 @@
 
 
 def laplace_kernel(
-    leaf, owner_hbm, stiff_hbm, lap, sent, target, coupling, spread, zero, owner, stiffness, zero_sem, small_sem
+    leaf, owner_hbm, stiff_hbm, lap, target, coupling, spread, owner, stiffness, small_sem
 ):
     small = [
         pltpu.make_async_copy(owner_hbm, owner, small_sem.at[0]),
         pltpu.make_async_copy(stiff_hbm, stiffness, small_sem.at[1]),
     ]
     for c in small:
-        c.start()
-    zero[...] = jnp.zeros_like(zero)
-    count = zero.shape[0]
-    clears = [
-        pltpu.make_async_copy(zero, sent.at[pl.ds(i * count, count)], zero_sem) for i in range(sent.shape[0] // count)
-    ]
-    for c in clears:
         c.start()
     records, rows, cols = leaf.shape
 
@@ -133,31 +126,25 @@
             part = jnp.where(within == r, lifted[p * half : (p + 1) * half], 0.0)
             at = (p * SUB + r) * half
             spread[at : at + half] = part.astype(BF16)
-    for c in clears:
-        c.wait()
-
-
-def laplace(leaf, owner, stiffness, slots):
+
+
+def laplace(leaf, owner, stiffness):
     records, rows, cols = leaf.shape
     vmem = pl.BlockSpec(memory_space=pltpu.VMEM)
     hbm = pl.BlockSpec(memory_space=pltpu.HBM)
-    tile = (records // 2, LANES)
     return pl.pallas_call(
         laplace_kernel,
         in_specs=[vmem, hbm, hbm],
-        out_specs=[vmem, hbm, vmem, vmem, vmem],
+        out_specs=[vmem] * 4,
         out_shape=[
             pltpu.VMEM((rows // SUB, records * SUB, cols), BF16),
-            pltpu.HBM((slots,) + tile, BF16),
             jax.ShapeDtypeStruct(owner.shape, jnp.int32),
             pltpu.VMEM((records, records), BF16),
             pltpu.VMEM((records * SUB, records * SUB), BF16),
         ],
         scratch_shapes=[
-            pltpu.VMEM((32,) + tile, BF16),
             pltpu.VMEM(owner.shape, jnp.int32),
             pltpu.VMEM(stiffness.shape, BF16),
-            pltpu.SemaphoreType.DMA,
             pltpu.SemaphoreType.DMA((2,)),
         ],
         compiler_params=pltpu.CompilerParams(vmem_limit_bytes=16 * MIB),
@@ -182,15 +169,14 @@
     ]
 
 
-def main_kernel(target, fields, lap, spread, sent_in, sent, rest, stage, sem):
-    del sent_in
+def main_kernel(target, fields, lap, spread, image, rest):
     blocks, _, cols = lap.shape
     half = fields.shape[1]
     rows = blocks * SUB
     quarters = cols // PC
     low = iota((half, LANES), 1) < PC
-    listed = edge_patches(rows, quarters)
-    edge = {rq: i for i, rq in enumerate(listed)}
+    edge = {rq: i for i, rq in enumerate(edge_patches(rows, quarters))}
+    image[...] = jnp.zeros_like(image)
     for n in range(blocks):
         tension = dot(spread[...], lap[n])
         for k in range(SUB):
@@ -205,32 +191,26 @@
                     if (r, q) in edge:
                         rest[edge[r, q]] = forced
                     else:
-                        stage[patch] = forced.astype(BF16)
-                        pltpu.make_async_copy(stage.at[patch], sent.at[target[0, patch]], sem).start()
-    count = rows * quarters - len(edge)
-    pltpu.make_async_copy(stage.at[pl.ds(0, count)], sent.at[pl.ds(0, count)], sem).wait()
-
-
-def main_part(target, fields, lap, spread, sent):
-    patches, tall, _ = fields.shape
+                        image[target[0, patch]] = forced.astype(BF16)
+
+
+def main_part(target, fields, lap, spread, slots):
+    _, tall, _ = fields.shape
     blocks, _, cols = lap.shape
     vmem = pl.BlockSpec(memory_space=pltpu.VMEM)
-    hbm = pl.BlockSpec(memory_space=pltpu.HBM)
     count = len(edge_patches(blocks * SUB, cols // PC))
     return pl.pallas_call(
         main_kernel,
-        in_specs=[pl.BlockSpec(memory_space=pltpu.SMEM), vmem, vmem, vmem, hbm],
-        out_specs=[hbm, vmem],
-        out_shape=[pltpu.HBM(sent.shape, BF16), pltpu.VMEM((count, tall, LANES), F32)],
-        scratch_shapes=[pltpu.VMEM((patches, tall, LANES), BF16), pltpu.SemaphoreType.DMA],
-        input_output_aliases={4: 0},
+        in_specs=[pl.BlockSpec(memory_space=pltpu.SMEM), vmem, vmem, vmem],
+        out_specs=[vmem, vmem],
+        out_shape=[pltpu.VMEM((slots, tall, LANES), BF16), pltpu.VMEM((count, tall, LANES), F32)],
         compiler_params=pltpu.CompilerParams(vmem_limit_bytes=16 * MIB),
         cost_estimate=pl.CostEstimate(flops=10**9, bytes_accessed=4 * MIB, transcendentals=0),
-    )(target, fields, lap, spread, sent)
-
-
-def edge_kernel(target, rest, coupling, row_two, row_one, side_two, side_one, sent_in, sent, stage, sem):
-    del sent_in
+    )(target, fields, lap, spread)
+
+
+def edge_kernel(target, rest, coupling, row_two, row_one, side_two, side_one, image_in, image, sent, sem):
+    del image_in
     records, cols = row_one.shape
     half = records // 2
     quarters = cols // PC
@@ -270,24 +250,25 @@
             forced = forced + split[r * half : (r + 1) * half, LANES:]
         if (r, q) in ends:
             forced = forced + ends[r, q]
-        stage[i] = forced.astype(BF16)
-        pltpu.make_async_copy(stage.at[i], sent.at[target[0, r * quarters + q]], sem).start()
-    count = len(listed)
-    pltpu.make_async_copy(stage, sent.at[pl.ds(0, count)], sem).wait()
-
-
-def edge_part(target, rest, coupling, row_two, row_one, side_two, side_one, sent):
-    vmem = pl.BlockSpec(memory_space=pltpu.VMEM)
-    return pl.pallas_call(
+        image[target[0, r * quarters + q]] = forced.astype(BF16)
+    whole = pltpu.make_async_copy(image, sent, sem)
+    whole.start()
+    whole.wait()
+
+
+def edge_part(target, rest, coupling, row_two, row_one, side_two, side_one, image):
+    vmem = pl.BlockSpec(memory_space=pltpu.VMEM)
+    _, sent = pl.pallas_call(
         edge_kernel,
-        in_specs=[pl.BlockSpec(memory_space=pltpu.SMEM)] + [vmem] * 6 + [pl.BlockSpec(memory_space=pltpu.HBM)],
-        out_specs=pl.BlockSpec(memory_space=pltpu.HBM),
-        out_shape=pltpu.HBM(sent.shape, sent.dtype),
-        scratch_shapes=[pltpu.VMEM(rest.shape, BF16), pltpu.SemaphoreType.DMA],
+        in_specs=[pl.BlockSpec(memory_space=pltpu.SMEM)] + [vmem] * 7,
+        out_specs=[vmem, pl.BlockSpec(memory_space=pltpu.HBM)],
+        out_shape=[pltpu.VMEM(image.shape, BF16), pltpu.HBM(image.shape, BF16)],
+        scratch_shapes=[pltpu.SemaphoreType.DMA],
         input_output_aliases={7: 0},
         compiler_params=pltpu.CompilerParams(vmem_limit_bytes=16 * MIB),
         cost_estimate=pl.CostEstimate(flops=2 * 10**8, bytes_accessed=2 * MIB, transcendentals=0),
-    )(target, rest, coupling, row_two, row_one, side_two, side_one, sent)
+    )(target, rest, coupling, row_two, row_one, side_two, side_one, image)
+    return sent
 
 
 def sweep_kernel(strip, state, ghosts, rate, shift, out, done, sem):
@@ -383,10 +364,10 @@
     side_one = exchange(sides, "azim", 0)
     row_two = exchange(row_two, "axial", 1)
     row_one = exchange(row_one, "axial", 0)
-    lap, sent, target, coupling, spread = laplace(leaf, new_owner.reshape(1, patch_count), stiffness, slots)
+    lap, target, coupling, spread = laplace(leaf, new_owner.reshape(1, patch_count), stiffness)
     held = in_vmem(to_tiles(fields))
-    sent, rest = main_part(target, held, lap, spread, sent)
-    sent = edge_part(target, rest, coupling, row_two, row_one, side_two, side_one, sent)
+    image, rest = main_part(target, held, lap, spread, slots)
+    sent = edge_part(target, rest, coupling, row_two, row_one, side_two, side_one, image)
     arrived = lax.all_to_all(sent.reshape(devices, -1, LANES), ALL, split_axis=0, concat_axis=0, tiled=True)
     state = arrived.reshape(slots, -1, LANES)
 

time: 57.8 us -> 57.1 us (0.988)
  Pallas kernels: 10.9 us -> 10.3 us
    pallas_call x1, Pallas kernels: 1.94 us -> 1.23 us  [laplace(): pl.pallas_call(laplace_kernel, in_specs=[vmem, hbm, hbm], out_specs=[vmem...]
  transfers between devices with their start and end apart: 5 -> 5, of which waited for: 1 -> 1; matrix products, arithmetic and copies ran while one was open for 1% -> 1% of each run, Pallas kernels for 7% -> 5%
where the time goes in v7:
time: 57.1 us; the launch traced here: 56.8 us
  waiting for transfers between devices  29.1 us (51%)
  starting transfers between devices  15.3 us (27%)
  Pallas kernels  10.3 us (18%)
  local copies, waits for them, and re-layouts  1.53 us (3%)
    all_to_all x1, waiting for transfers between devices, shards(): lax.all_to_all(sent.reshape(devices, -1, LANES), ALL, split_axis=0, conca...  29.1 us
    ppermute x4, starting transfers between devices, exchange(): return lax.ppermute(x, axis, pairs + [(j, i) for i, j in pairs])  9.99 us
    all_to_all x1, starting transfers between devices, shards(): lax.all_to_all(sent.reshape(devices, -1, LANES), ALL, split_axis=0, conca...  5.31 us
    pallas_call x1, Pallas kernels, sweeps(): pl.pallas_call(sweep_kernel, in_specs=[pl.BlockSpec(memory_space=pltpu.SM...  3.84 us
    pallas_call x1, Pallas kernels, edge_part(): pl.pallas_call(edge_kernel, in_specs=[pl.BlockSpec(memory_space=pltpu.SME...  2.43 us
    pallas_call x1, Pallas kernels, main_part(): pl.pallas_call(main_kernel, in_specs=[pl.BlockSpec(memory_space=pltpu.SME...  1.74 us
    unnamed x14, local copies, waits for them, and re-layouts  1.26 us
    pallas_call x1, Pallas kernels, laplace(): pl.pallas_call(laplace_kernel, in_specs=[vmem, hbm, hbm], out_specs=[vmem...  1.23 us
  transfers between devices with their start and end apart: 5, of which 1 were waited for; matrix products, arithmetic and copies ran while one was open for 1% of the time, Pallas kernels for 5%

profile of v7, /device:TPU:1, one launch (start us, length us, event | category | flops | bytes accessed | tf_op | source)
XLA Modules:
  0.0 56.8 jit_solution(10483906205433220041)
XLA Ops:
  0.0 1.2 %copy-done = bf16[64,32,256]{2,1,0:T(8,128)(2,1)S(1)} copy-done((bf16[64,32,256]{2,1,0:T(8,128)(2,1)S(1)}, bf16[64,32,256]{2,1,0:T(8,128)(2,1)}, u32[]{:S(2)}) %copy-start) | copy-done | bytes 1048600
  1.2 1.1 %shard_map.93 = (bf16[64,256]{1,0:T(8,128)(2,1)S(1)}, bf16[64,256]{1,0:T(8,128)(2,1)S(1)}, bf16[64,128]{1,0:T(8,128)(2,1)S(1)}) custom-call(bf16[64,32,256]{2,1,0:T(8,128)(2,1)S(1)} %copy-done), custom_call_target="tpu_custom_call" | custom-call | flops 100000000 | bytes 1048576 | tf_op jit(solution)/shard_map/pallas_call | solution.py:73
  2.3 5.8 %collective-permute-start.2 = (bf16[64,128]{1,0:T(8,128)(2,1)S(1)}, bf16[64,128]{1,0:T(8,128)(2,1)S(1)}, u32[]{:S(2)}, u32[]{:S(2)}) collective-permute-start(bf16[64,128]{1,0:T(8,128)(2,1)S(1)} %get-tuple-element.22), channel_id=1, source_target_pairs={{1,2},{3,4},{5,6},{7,8},{9,10},{11,12},{13,14},{15,0},{2,1},{4,3},... | collective-permute-start | bytes 49160 | tf_op jit(solution)/shard_map/ppermute | solution.py:158
  8.2 2.5 %collective-permute-start = (bf16[64,256]{1,0:T(8,128)(2,1)S(1)}, bf16[64,256]{1,0:T(8,128)(2,1)S(1)}, u32[]{:S(2)}, u32[]{:S(2)}) collective-permute-start(bf16[64,256]{1,0:T(8,128)(2,1)S(1)} %get-tuple-element.20), channel_id=1, source_target_pairs={{16,32},{48,64},{80,96},{112,0},{32,16},{64,48},{96,80},{0,112},{1... | collective-permute-start | bytes 98312 | tf_op jit(solution)/shard_map/ppermute | solution.py:158
  10.6 1.7 %collective-permute-start.1 = (bf16[64,256]{1,0:T(8,128)(2,1)S(1)}, bf16[64,256]{1,0:T(8,128)(2,1)S(1)}, u32[]{:S(2)}, u32[]{:S(2)}) collective-permute-start(bf16[64,256]{1,0:T(8,128)(2,1)S(1)} %get-tuple-element.21), channel_id=1, source_target_pairs={{0,16},{32,48},{64,80},{96,112},{16,0},{48,32},{80,64},{112,96},{1... | collective-permute-start | bytes 98312 | tf_op jit(solution)/shard_map/ppermute | solution.py:158
  12.3 1.2 %shard_map.91 = (bf16[4,512,256]{2,1,0:T(8,128)(2,1)S(1)}, s32[1,128]{1,0:T(1,128)S(1)}, bf16[64,64]{1,0:T(8,128)(2,1)S(1)}, bf16[512,512]{1,0:T(8,128)(2,1)S(1)}) custom-call(bf16[64,32,256]{2,1,0:T(8,128)(2,1)S(1)} %copy-done, s32[1,128]{1,0:T(1,128)} %bitcast.22, bf16[64,64]{1,0:T(8,128)(2,1)} %stiff_hbm.1), custom_call_target="tpu_custom_call" | custom-call | flops 500000000 | bytes 3145728 | tf_op jit(solution)/shard_map/pallas_call | solution.py:135
  13.6 1.7 %shard_map.92 = (bf16[256,32,128]{2,1,0:T(8,128)(2,1)S(1)}, f32[68,32,128]{2,1,0:T(8,128)S(1)}) custom-call(s32[1,128]{1,0:T(1,128)S(1)} %get-tuple-element.15.target, f32[128,32,128]{2,1,0:T(8,128)S(1)} %bitcast.19, bf16[4,512,256]{2,1,0:T(8,128)(2,1)S(1)} %get-tuple-element.16.lap, bf16[512,512]{1,0:T(8,128)(2,1)S(1)} %get-tuple-element.17.spread), custom_call_target="tpu_custom_call" | custom-call | flops 1000000000 | bytes 4194304 | tf_op jit(solution)/shard_map/pallas_call | solution.py:202
  15.3 0.0 collective-permute-done.2.side_two
  15.3 0.0 collective-permute-done.3.side_one
  15.3 0.0 collective-permute-done.1.row_one
  15.4 2.4 %shard_map.94 = (bf16[256,32,128]{2,1,0:T(8,128)(2,1)S(1)}, bf16[256,32,128]{2,1,0:T(8,128)(2,1)}) custom-call(s32[1,128]{1,0:T(1,128)S(1)} %get-tuple-element.15.target, f32[68,32,128]{2,1,0:T(8,128)S(1)} %get-tuple-element.18.rest, bf16[64,64]{1,0:T(8,128)(2,1)S(1)} %get-tuple-element.19.coupling, ...), custom_call_target="tpu_custom_call", output_to_operand_aliasing={{0}: (7, {})} | custom-call | flops 200000000 | bytes 2097152 | tf_op jit(solution)/shard_map/pallas_call | solution.py:261
  17.8 0.0 copy-start.4
  17.8 0.0 copy-start.5
  17.8 0.0 copy-start.6
  17.8 0.0 copy-start.1
  17.8 0.0 copy-start.2
  17.9 5.3 %all-to-all-start = ((bf16[128,64,128]{2,1,0:T(8,128)(2,1)}), bf16[128,64,128]{2,1,0:T(8,128)(2,1)S(1)}, u32[]{:S(2)}, u32[]{:S(2)}) async-start(bf16[128,64,128]{2,1,0:T(8,128)(2,1)} %bitcast.20), calls=%async_computation | async-start | bytes 4194304 | tf_op jit(solution)/shard_map/all_to_all | solution.py:371
  23.2 0.1 dot_general.5
  23.3 0.3 fusion
  23.6 0.1 copy.18
  23.7 0.1 pad_maximum_fusion.1
  23.8 29.1 %all-to-all-done = bf16[128,64,128]{2,1,0:T(8,128)(2,1)S(1)} async-done(((bf16[128,64,128]{2,1,0:T(8,128)(2,1)}), bf16[128,64,128]{2,1,0:T(8,128)(2,1)S(1)}, u32[]{:S(2)}, u32[]{:S(2)}) %all-to-all-start) | async-done | bytes 2097184 | tf_op jit(solution)/shard_map/all_to_all | solution.py:371
  52.9 0.1 broadcast_in_dim.2.rate
  53.0 3.8 %shard_map.95 = f32[256,32,128]{2,1,0:T(8,128)} custom-call(s32[256]{0:T(256)S(1)} %copy-done.2, bf16[256,32,128]{2,1,0:T(8,128)(2,1)S(1)} %bitcast.18, f32[64,8,128]{2,1,0:T(8,128)S(1)} %pad_maximum_fusion.ghosts, f32[8,128]{1,0:T(8,128)S(1)} %broadcast_in_dim.2.rate, bf16[256,256]{1,0:T(8,128)(2,1)S(1)} %copy-done.1), custom_call_target="tpu_custom_call" | custom-call | tf_op jit(solution)/shard_map/pallas_call | solution.py:334
  (11 shorter events, 0.1 us)
Async XLA Ops:
  0.0 1.2 %copy-start = (bf16[64,32,256]{2,1,0:T(8,128)(2,1)S(1)}, bf16[64,32,256]{2,1,0:T(8,128)(2,1)}, u32[]{:S(2)}) copy-start(bf16[64,32,256]{2,1,0:T(8,128)(2,1)} %leaf.3) | copy-start | bytes 3145732
  1.2 12.3 %copy-start.3 = (f32[128,4,1024]{2,1,0:T(4,128)S(1)}, f32[128,4,1024]{2,1,0:T(4,128)}, u32[]{:S(2)}) copy-start(f32[128,4,1024]{2,1,0:T(4,128)} %param.9) | copy-start | bytes 6291460
  2.3 13.0 %collective-permute-start.2 = (bf16[64,128]{1,0:T(8,128)(2,1)S(1)}, bf16[64,128]{1,0:T(8,128)(2,1)S(1)}, u32[]{:S(2)}, u32[]{:S(2)}) collective-permute-start(bf16[64,128]{1,0:T(8,128)(2,1)S(1)} %get-tuple-element.22), channel_id=1, source_target_pairs={{1,2},{3,4},{5,6},{7,8},{9,10},{11,12},{13,14},{15,0},{2,1},{4,3},... | collective-permute-start | bytes 49160 | tf_op jit(solution)/shard_map/ppermute | solution.py:158
  8.2 7.2 %collective-permute-start.3 = (bf16[64,128]{1,0:T(8,128)(2,1)S(1)}, bf16[64,128]{1,0:T(8,128)(2,1)S(1)}, u32[]{:S(2)}, u32[]{:S(2)}) collective-permute-start(bf16[64,128]{1,0:T(8,128)(2,1)S(1)} %get-tuple-element.22), channel_id=1, source_target_pairs={{0,1},{2,3},{4,5},{6,7},{8,9},{10,11},{12,13},{14,15},{1,0},{3,2},... | collective-permute-start | bytes 49160 | tf_op jit(solution)/shard_map/ppermute | solution.py:158
  8.2 7.2 %collective-permute-start = (bf16[64,256]{1,0:T(8,128)(2,1)S(1)}, bf16[64,256]{1,0:T(8,128)(2,1)S(1)}, u32[]{:S(2)}, u32[]{:S(2)}) collective-permute-start(bf16[64,256]{1,0:T(8,128)(2,1)S(1)} %get-tuple-element.20), channel_id=1, source_target_pairs={{16,32},{48,64},{80,96},{112,0},{32,16},{64,48},{96,80},{0,112},{1... | collective-permute-start | bytes 98312 | tf_op jit(solution)/shard_map/ppermute | solution.py:158
  10.6 4.7 %collective-permute-start.1 = (bf16[64,256]{1,0:T(8,128)(2,1)S(1)}, bf16[64,256]{1,0:T(8,128)(2,1)S(1)}, u32[]{:S(2)}, u32[]{:S(2)}) collective-permute-start(bf16[64,256]{1,0:T(8,128)(2,1)S(1)} %get-tuple-element.21), channel_id=1, source_target_pairs={{0,16},{32,48},{64,80},{96,112},{16,0},{48,32},{80,64},{112,96},{1... | collective-permute-start | bytes 98312 | tf_op jit(solution)/shard_map/ppermute | solution.py:158
  17.8 5.4 %copy-start.4 = (f32[64,256]{1,0:T(8,128)S(1)}, f32[64,256]{1,0:T(8,128)}, u32[]{:S(2)}) copy-start(f32[64,256]{1,0:T(8,128)} %param.13) | copy-start | bytes 196612
  17.8 5.5 %copy-start.5 = (f32[64,128,1]{1,0,2:T(8,128)S(1)}, f32[64,128,1]{1,0,2:T(8,128)}, u32[]{:S(2)}) copy-start(f32[64,128,1]{1,0,2:T(8,128)} %constant.7) | copy-start | bytes 98308
  17.8 5.8 %copy-start.6 = (f32[4]{0:T(128)S(1)}, f32[4]{0:T(128)}, u32[]{:S(2)}) copy-start(f32[4]{0:T(128)} %param.15) | copy-start | bytes 52
  17.8 35.2 %copy-start.1 = (bf16[256,256]{1,0:T(8,128)(2,1)S(1)}, bf16[256,256]{1,0:T(8,128)(2,1)}, u32[]{:S(2)}) copy-start(bf16[256,256]{1,0:T(8,128)(2,1)} %constant.5.clone.shift) | copy-start | bytes 393220
  17.8 35.2 %copy-start.2 = (s32[256]{0:T(256)S(1)}, s32[256]{0:T(256)}, u32[]{:S(2)}) copy-start(s32[256]{0:T(256)} %strip.1) | copy-start | bytes 3076
  17.9 35.1 %all-to-all-start = ((bf16[128,64,128]{2,1,0:T(8,128)(2,1)}), bf16[128,64,128]{2,1,0:T(8,128)(2,1)S(1)}, u32[]{:S(2)}, u32[]{:S(2)}) async-start(bf16[128,64,128]{2,1,0:T(8,128)(2,1)} %bitcast.20), calls=%async_computation | async-start | bytes 4194304 | tf_op jit(solution)/shard_map/all_to_all | solution.py:371

commit v8 on v7

--- a/solution.py
+++ b/solution.py
@@ -49,16 +49,20 @@
     return jnp.where(mask, 1.0, 0.0).astype(BF16)
 
 
-def first_kernel(leaf, one, two, sides):
+def sides_kernel(leaf, sides):
     records, rows, cols = leaf.shape
-    half = rows // 2
-    odd = lax.axis_index("axial") % 2
     spot = jnp.where(iota((cols, LANES), 1) // rows % 2 == 0, 0, cols - 1)
     wide = dot(leaf[...].reshape(-1, cols), where_one(iota((cols, LANES), 0) == spot))
     r = iota((records * rows, LANES), 0) % rows
     wide = jnp.where(iota((records * rows, LANES), 1) % rows == r, wide, 0.0).astype(BF16)
     gather = iota((records, records * rows), 1) // rows == iota((records, records * rows), 0)
     sides[...] = dot(where_one(gather), wide).astype(BF16)
+
+
+def rows_kernel(leaf, one, two):
+    records, rows, cols = leaf.shape
+    half = rows // 2
+    odd = lax.axis_index("axial") % 2
     pick = iota((records, records * half), 1) - iota((records, records * half), 0) * half
     first = dot(where_one(pick == 0), leaf[:, :half].reshape(-1, cols))
     last = dot(where_one(pick == half - 1), leaf[:, half:].reshape(-1, cols))
@@ -66,14 +70,12 @@
     two[...] = jnp.where(odd == 0, first, last).astype(BF16)
 
 
-def first_part(leaf):
-    records, rows, cols = leaf.shape
+def edge_call(kernel, leaf, shapes):
     vmem = pl.BlockSpec(memory_space=pltpu.VMEM)
-    shapes = [(records, cols), (records, cols), (records, LANES)]
     return pl.pallas_call(
-        first_kernel,
+        kernel,
         in_specs=[vmem],
-        out_specs=[vmem] * 3,
+        out_specs=[vmem] * len(shapes),
         out_shape=[pltpu.VMEM(s, BF16) for s in shapes],
         compiler_params=pltpu.CompilerParams(vmem_limit_bytes=16 * MIB),
         cost_estimate=pl.CostEstimate(flops=10**8, bytes_accessed=MIB, transcendentals=0),
@@ -359,7 +361,10 @@
     slots = devices * SLOTS_EACH
 
     leaf = in_vmem(leaflet)
-    row_one, row_two, sides = first_part(leaf)
+    records, _, cols = leaf.shape
+    (sides,) = edge_call(sides_kernel, leaf, [(records, LANES)])
+    sides, leaf = lax.optimization_barrier((sides, leaf))
+    row_one, row_two = edge_call(rows_kernel, leaf, [(records, cols)] * 2)
     side_two = exchange(sides, "azim", 1)
     side_one = exchange(sides, "azim", 0)
     row_two = exchange(row_two, "axial", 1)

time: 57.1 us -> 57.1 us (level)
  transfers between devices with their start and end apart: 5 -> 5, of which waited for: 1 -> 1; matrix products, arithmetic and copies ran while one was open for 1% -> 1% of each run, Pallas kernels for 5% -> 6%
where the time goes in v8:
time: 57.1 us; the launch traced here: 56.8 us
  waiting for transfers between devices  29.1 us (51%)
  starting transfers between devices  15.4 us (27%)
  Pallas kernels  10.2 us (18%)
  local copies, waits for them, and re-layouts  1.53 us (3%)
    all_to_all x1, waiting for transfers between devices, shards(): lax.all_to_all(sent.reshape(devices, -1, LANES), ALL, split_axis=0, conca...  29.1 us
    ppermute x4, starting transfers between devices, exchange(): return lax.ppermute(x, axis, pairs + [(j, i) for i, j in pairs])  10.1 us
    all_to_all x1, starting transfers between devices, shards(): lax.all_to_all(sent.reshape(devices, -1, LANES), ALL, split_axis=0, conca...  5.31 us
    pallas_call x1, Pallas kernels, sweeps(): pl.pallas_call(sweep_kernel, in_specs=[pl.BlockSpec(memory_space=pltpu.SM...  3.84 us
    pallas_call x1, Pallas kernels, edge_part(): pl.pallas_call(edge_kernel, in_specs=[pl.BlockSpec(memory_space=pltpu.SME...  2.43 us
    pallas_call x1, Pallas kernels, main_part(): pl.pallas_call(main_kernel, in_specs=[pl.BlockSpec(memory_space=pltpu.SME...  1.73 us
    unnamed x14, local copies, waits for them, and re-layouts  1.26 us
    pallas_call x1, Pallas kernels, laplace(): pl.pallas_call(laplace_kernel, in_specs=[vmem, hbm, hbm], out_specs=[vmem...  1.23 us
  transfers between devices with their start and end apart: 5, of which 1 were waited for; matrix products, arithmetic and copies ran while one was open for 1% of the time, Pallas kernels for 6%

profile of v8, /device:TPU:1, one launch (start us, length us, event | category | flops | bytes accessed | tf_op | source)
XLA Modules:
  0.0 56.8 jit_solution(2104921809055227867)
XLA Ops:
  0.0 1.2 %copy-done = bf16[64,32,256]{2,1,0:T(8,128)(2,1)S(1)} copy-done((bf16[64,32,256]{2,1,0:T(8,128)(2,1)S(1)}, bf16[64,32,256]{2,1,0:T(8,128)(2,1)}, u32[]{:S(2)}) %copy-start) | copy-done | bytes 1048600
  1.2 0.7 %shard_map.91 = bf16[64,128]{1,0:T(8,128)(2,1)S(1)} custom-call(bf16[64,32,256]{2,1,0:T(8,128)(2,1)S(1)} %copy-done), custom_call_target="tpu_custom_call" | custom-call | flops 100000000 | bytes 1048576 | tf_op jit(solution)/shard_map/pallas_call | solution.py:75
  1.9 5.8 %collective-permute-start.2 = (bf16[64,128]{1,0:T(8,128)(2,1)S(1)}, bf16[64,128]{1,0:T(8,128)(2,1)S(1)}, u32[]{:S(2)}, u32[]{:S(2)}) collective-permute-start(bf16[64,128]{1,0:T(8,128)(2,1)S(1)} %shard_map.91), channel_id=1, source_target_pairs={{1,2},{3,4},{5,6},{7,8},{9,10},{11,12},{13,14},{15,0},{2,1},{4,3},... | collective-permute-start | bytes 49160 | tf_op jit(solution)/shard_map/ppermute | solution.py:160
  7.8 0.0 collective-permute-start.3
  7.8 0.3 shard_map.94
  8.1 2.5 %collective-permute-start = (bf16[64,256]{1,0:T(8,128)(2,1)S(1)}, bf16[64,256]{1,0:T(8,128)(2,1)S(1)}, u32[]{:S(2)}, u32[]{:S(2)}) collective-permute-start(bf16[64,256]{1,0:T(8,128)(2,1)S(1)} %get-tuple-element.22), channel_id=1, source_target_pairs={{16,32},{48,64},{80,96},{112,0},{32,16},{64,48},{96,80},{0,112},{1... | collective-permute-start | bytes 98312 | tf_op jit(solution)/shard_map/ppermute | solution.py:160
  10.6 1.7 %collective-permute-start.1 = (bf16[64,256]{1,0:T(8,128)(2,1)S(1)}, bf16[64,256]{1,0:T(8,128)(2,1)S(1)}, u32[]{:S(2)}, u32[]{:S(2)}) collective-permute-start(bf16[64,256]{1,0:T(8,128)(2,1)S(1)} %get-tuple-element.23), channel_id=1, source_target_pairs={{0,16},{32,48},{64,80},{96,112},{16,0},{48,32},{80,64},{112,96},{1... | collective-permute-start | bytes 98312 | tf_op jit(solution)/shard_map/ppermute | solution.py:160
  12.3 1.2 %shard_map.92 = (bf16[4,512,256]{2,1,0:T(8,128)(2,1)S(1)}, s32[1,128]{1,0:T(1,128)S(1)}, bf16[64,64]{1,0:T(8,128)(2,1)S(1)}, bf16[512,512]{1,0:T(8,128)(2,1)S(1)}) custom-call(bf16[64,32,256]{2,1,0:T(8,128)(2,1)S(1)} %copy-done, s32[1,128]{1,0:T(1,128)} %bitcast.22, bf16[64,64]{1,0:T(8,128)(2,1)} %stiff_hbm.1), custom_call_target="tpu_custom_call" | custom-call | flops 500000000 | bytes 3145728 | tf_op jit(solution)/shard_map/pallas_call | solution.py:137
  13.6 1.7 %shard_map.93 = (bf16[256,32,128]{2,1,0:T(8,128)(2,1)S(1)}, f32[68,32,128]{2,1,0:T(8,128)S(1)}) custom-call(s32[1,128]{1,0:T(1,128)S(1)} %get-tuple-element.17.target, f32[128,32,128]{2,1,0:T(8,128)S(1)} %bitcast.19, bf16[4,512,256]{2,1,0:T(8,128)(2,1)S(1)} %get-tuple-element.18.lap, bf16[512,512]{1,0:T(8,128)(2,1)S(1)} %get-tuple-element.19.spread), custom_call_target="tpu_custom_call" | custom-call | flops 1000000000 | bytes 4194304 | tf_op jit(solution)/shard_map/pallas_call | solution.py:204
  15.3 0.0 collective-permute-done.2.side_two
  15.3 2.4 %shard_map.95 = (bf16[256,32,128]{2,1,0:T(8,128)(2,1)S(1)}, bf16[256,32,128]{2,1,0:T(8,128)(2,1)}) custom-call(s32[1,128]{1,0:T(1,128)S(1)} %get-tuple-element.17.target, f32[68,32,128]{2,1,0:T(8,128)S(1)} %get-tuple-element.20.rest, bf16[64,64]{1,0:T(8,128)(2,1)S(1)} %get-tuple-element.21.coupling, ...), custom_call_target="tpu_custom_call", output_to_operand_aliasing={{0}: (7, {})} | custom-call | flops 200000000 | bytes 2097152 | tf_op jit(solution)/shard_map/pallas_call | solution.py:263
  17.8 0.0 copy-start.4
  17.8 0.0 copy-start.5
  17.8 0.0 copy-start.6
  17.8 0.0 copy-start.1
  17.8 0.0 copy-start.2
  17.9 5.3 %all-to-all-start = ((bf16[128,64,128]{2,1,0:T(8,128)(2,1)}), bf16[128,64,128]{2,1,0:T(8,128)(2,1)S(1)}, u32[]{:S(2)}, u32[]{:S(2)}) async-start(bf16[128,64,128]{2,1,0:T(8,128)(2,1)} %bitcast.20), calls=%async_computation | async-start | bytes 4194304 | tf_op jit(solution)/shard_map/all_to_all | solution.py:376
  23.2 0.1 dot_general.5
  23.3 0.3 fusion
  23.6 0.1 copy.18
  23.7 0.1 pad_maximum_fusion.1
  23.8 29.1 %all-to-all-done = bf16[128,64,128]{2,1,0:T(8,128)(2,1)S(1)} async-done(((bf16[128,64,128]{2,1,0:T(8,128)(2,1)}), bf16[128,64,128]{2,1,0:T(8,128)(2,1)S(1)}, u32[]{:S(2)}, u32[]{:S(2)}) %all-to-all-start) | async-done | bytes 2097184 | tf_op jit(solution)/shard_map/all_to_all | solution.py:376
  52.9 0.1 broadcast_in_dim.2.rate
  53.0 3.8 %shard_map.96 = f32[256,32,128]{2,1,0:T(8,128)} custom-call(s32[256]{0:T(256)S(1)} %copy-done.2, bf16[256,32,128]{2,1,0:T(8,128)(2,1)S(1)} %bitcast.18, f32[64,8,128]{2,1,0:T(8,128)S(1)} %pad_maximum_fusion.ghosts, f32[8,128]{1,0:T(8,128)S(1)} %broadcast_in_dim.2.rate, bf16[256,256]{1,0:T(8,128)(2,1)S(1)} %copy-done.1), custom_call_target="tpu_custom_call" | custom-call | tf_op jit(solution)/shard_map/pallas_call | solution.py:336
  (12 shorter events, 0.1 us)
Async XLA Ops:
  0.0 1.2 %copy-start = (bf16[64,32,256]{2,1,0:T(8,128)(2,1)S(1)}, bf16[64,32,256]{2,1,0:T(8,128)(2,1)}, u32[]{:S(2)}) copy-start(bf16[64,32,256]{2,1,0:T(8,128)(2,1)} %leaf.3) | copy-start | bytes 3145732
  1.2 12.3 %copy-start.3 = (f32[128,4,1024]{2,1,0:T(4,128)S(1)}, f32[128,4,1024]{2,1,0:T(4,128)}, u32[]{:S(2)}) copy-start(f32[128,4,1024]{2,1,0:T(4,128)} %param.9) | copy-start | bytes 6291460
  1.9 13.4 %collective-permute-start.2 = (bf16[64,128]{1,0:T(8,128)(2,1)S(1)}, bf16[64,128]{1,0:T(8,128)(2,1)S(1)}, u32[]{:S(2)}, u32[]{:S(2)}) collective-permute-start(bf16[64,128]{1,0:T(8,128)(2,1)S(1)} %shard_map.91), channel_id=1, source_target_pairs={{1,2},{3,4},{5,6},{7,8},{9,10},{11,12},{13,14},{15,0},{2,1},{4,3},... | collective-permute-start | bytes 49160 | tf_op jit(solution)/shard_map/ppermute | solution.py:160
  7.8 7.5 %collective-permute-start.3 = (bf16[64,128]{1,0:T(8,128)(2,1)S(1)}, bf16[64,128]{1,0:T(8,128)(2,1)S(1)}, u32[]{:S(2)}, u32[]{:S(2)}) collective-permute-start(bf16[64,128]{1,0:T(8,128)(2,1)S(1)} %shard_map.91), channel_id=1, source_target_pairs={{0,1},{2,3},{4,5},{6,7},{8,9},{10,11},{12,13},{14,15},{1,0},{3,2},... | collective-permute-start | bytes 49160 | tf_op jit(solution)/shard_map/ppermute | solution.py:160
  8.1 7.2 %collective-permute-start = (bf16[64,256]{1,0:T(8,128)(2,1)S(1)}, bf16[64,256]{1,0:T(8,128)(2,1)S(1)}, u32[]{:S(2)}, u32[]{:S(2)}) collective-permute-start(bf16[64,256]{1,0:T(8,128)(2,1)S(1)} %get-tuple-element.22), channel_id=1, source_target_pairs={{16,32},{48,64},{80,96},{112,0},{32,16},{64,48},{96,80},{0,112},{1... | collective-permute-start | bytes 98312 | tf_op jit(solution)/shard_map/ppermute | solution.py:160
  10.6 4.7 %collective-permute-start.1 = (bf16[64,256]{1,0:T(8,128)(2,1)S(1)}, bf16[64,256]{1,0:T(8,128)(2,1)S(1)}, u32[]{:S(2)}, u32[]{:S(2)}) collective-permute-start(bf16[64,256]{1,0:T(8,128)(2,1)S(1)} %get-tuple-element.23), channel_id=1, source_target_pairs={{0,16},{32,48},{64,80},{96,112},{16,0},{48,32},{80,64},{112,96},{1... | collective-permute-start | bytes 98312 | tf_op jit(solution)/shard_map/ppermute | solution.py:160
  17.8 5.4 %copy-start.4 = (f32[64,256]{1,0:T(8,128)S(1)}, f32[64,256]{1,0:T(8,128)}, u32[]{:S(2)}) copy-start(f32[64,256]{1,0:T(8,128)} %param.13) | copy-start | bytes 196612
  17.8 5.5 %copy-start.5 = (f32[64,128,1]{1,0,2:T(8,128)S(1)}, f32[64,128,1]{1,0,2:T(8,128)}, u32[]{:S(2)}) copy-start(f32[64,128,1]{1,0,2:T(8,128)} %constant.7) | copy-start | bytes 98308
  17.8 5.8 %copy-start.6 = (f32[4]{0:T(128)S(1)}, f32[4]{0:T(128)}, u32[]{:S(2)}) copy-start(f32[4]{0:T(128)} %param.15) | copy-start | bytes 52
  17.8 35.2 %copy-start.1 = (bf16[256,256]{1,0:T(8,128)(2,1)S(1)}, bf16[256,256]{1,0:T(8,128)(2,1)}, u32[]{:S(2)}) copy-start(bf16[256,256]{1,0:T(8,128)(2,1)} %constant.5.clone.shift) | copy-start | bytes 393220
  17.8 35.2 %copy-start.2 = (s32[256]{0:T(256)S(1)}, s32[256]{0:T(256)}, u32[]{:S(2)}) copy-start(s32[256]{0:T(256)} %strip.1) | copy-start | bytes 3076
  17.9 35.1 %all-to-all-start = ((bf16[128,64,128]{2,1,0:T(8,128)(2,1)}), bf16[128,64,128]{2,1,0:T(8,128)(2,1)S(1)}, u32[]{:S(2)}, u32[]{:S(2)}) async-start(bf16[128,64,128]{2,1,0:T(8,128)(2,1)} %bitcast.20), calls=%async_computation | async-start | bytes 4194304 | tf_op jit(solution)/shard_map/all_to_all | solution.py:376

commit v9 on v7

--- a/solution.py
+++ b/solution.py
@@ -304,8 +304,7 @@
             xs.append(sweep(mine, gs[i], y[i * tall : (i + 1) * tall]))
         for step in range(STEPS - 1):
             flat = jnp.concatenate([z for mine in xs for z in mine], axis=0)
-            high = flat.astype(BF16)
-            y = dot(jnp.concatenate([high, (flat - high.astype(F32)).astype(BF16)], axis=1), shift[...])
+            y = dot(flat.astype(BF16), shift[:LANES])
             xs = [sweep(xs[i], gs[i], y[i * tall : (i + 1) * tall]) for i in range(chunk)]
         for i in range(chunk):
             for k in range(tiles):

time: 57.1 us -> 57 us (level)
  no operation moved by 1% of the time
where the time goes in v9:
time: 57 us; the launch traced here: 56.7 us
  waiting for transfers between devices  29.1 us (51%)
  starting transfers between devices  15.3 us (27%)
  Pallas kernels  10.2 us (18%)
  local copies, waits for them, and re-layouts  1.53 us (3%)
    all_to_all x1, waiting for transfers between devices, shards(): lax.all_to_all(sent.reshape(devices, -1, LANES), ALL, split_axis=0, conca...  29.1 us
    ppermute x4, starting transfers between devices, exchange(): return lax.ppermute(x, axis, pairs + [(j, i) for i, j in pairs])  9.99 us
    all_to_all x1, starting transfers between devices, shards(): lax.all_to_all(sent.reshape(devices, -1, LANES), ALL, split_axis=0, conca...  5.31 us
    pallas_call x1, Pallas kernels, sweeps(): pl.pallas_call(sweep_kernel, in_specs=[pl.BlockSpec(memory_space=pltpu.SM...  3.72 us
    pallas_call x1, Pallas kernels, edge_part(): pl.pallas_call(edge_kernel, in_specs=[pl.BlockSpec(memory_space=pltpu.SME...  2.43 us
    pallas_call x1, Pallas kernels, main_part(): pl.pallas_call(main_kernel, in_specs=[pl.BlockSpec(memory_space=pltpu.SME...  1.74 us
    unnamed x14, local copies, waits for them, and re-layouts  1.26 us
    pallas_call x1, Pallas kernels, laplace(): pl.pallas_call(laplace_kernel, in_specs=[vmem, hbm, hbm], out_specs=[vmem...  1.23 us
  transfers between devices with their start and end apart: 5, of which 1 were waited for; matrix products, arithmetic and copies ran while one was open for 1% of the time, Pallas kernels for 5%

profile of v9, /device:TPU:1, one launch (start us, length us, event | category | flops | bytes accessed | tf_op | source)
XLA Modules:
  0.0 56.7 jit_solution(12958172136259256598)
XLA Ops:
  0.0 1.2 %copy-done = bf16[64,32,256]{2,1,0:T(8,128)(2,1)S(1)} copy-done((bf16[64,32,256]{2,1,0:T(8,128)(2,1)S(1)}, bf16[64,32,256]{2,1,0:T(8,128)(2,1)}, u32[]{:S(2)}) %copy-start) | copy-done | bytes 1048600
  1.2 1.1 %shard_map.93 = (bf16[64,256]{1,0:T(8,128)(2,1)S(1)}, bf16[64,256]{1,0:T(8,128)(2,1)S(1)}, bf16[64,128]{1,0:T(8,128)(2,1)S(1)}) custom-call(bf16[64,32,256]{2,1,0:T(8,128)(2,1)S(1)} %copy-done), custom_call_target="tpu_custom_call" | custom-call | flops 100000000 | bytes 1048576 | tf_op jit(solution)/shard_map/pallas_call | solution.py:73
  2.3 5.8 %collective-permute-start.2 = (bf16[64,128]{1,0:T(8,128)(2,1)S(1)}, bf16[64,128]{1,0:T(8,128)(2,1)S(1)}, u32[]{:S(2)}, u32[]{:S(2)}) collective-permute-start(bf16[64,128]{1,0:T(8,128)(2,1)S(1)} %get-tuple-element.22), channel_id=1, source_target_pairs={{1,2},{3,4},{5,6},{7,8},{9,10},{11,12},{13,14},{15,0},{2,1},{4,3},... | collective-permute-start | bytes 49160 | tf_op jit(solution)/shard_map/ppermute | solution.py:158
  8.2 0.0 collective-permute-start.3
  8.2 2.5 %collective-permute-start = (bf16[64,256]{1,0:T(8,128)(2,1)S(1)}, bf16[64,256]{1,0:T(8,128)(2,1)S(1)}, u32[]{:S(2)}, u32[]{:S(2)}) collective-permute-start(bf16[64,256]{1,0:T(8,128)(2,1)S(1)} %get-tuple-element.20), channel_id=1, source_target_pairs={{16,32},{48,64},{80,96},{112,0},{32,16},{64,48},{96,80},{0,112},{1... | collective-permute-start | bytes 98312 | tf_op jit(solution)/shard_map/ppermute | solution.py:158
  10.6 1.7 %collective-permute-start.1 = (bf16[64,256]{1,0:T(8,128)(2,1)S(1)}, bf16[64,256]{1,0:T(8,128)(2,1)S(1)}, u32[]{:S(2)}, u32[]{:S(2)}) collective-permute-start(bf16[64,256]{1,0:T(8,128)(2,1)S(1)} %get-tuple-element.21), channel_id=1, source_target_pairs={{0,16},{32,48},{64,80},{96,112},{16,0},{48,32},{80,64},{112,96},{1... | collective-permute-start | bytes 98312 | tf_op jit(solution)/shard_map/ppermute | solution.py:158
  12.3 1.2 %shard_map.91 = (bf16[4,512,256]{2,1,0:T(8,128)(2,1)S(1)}, s32[1,128]{1,0:T(1,128)S(1)}, bf16[64,64]{1,0:T(8,128)(2,1)S(1)}, bf16[512,512]{1,0:T(8,128)(2,1)S(1)}) custom-call(bf16[64,32,256]{2,1,0:T(8,128)(2,1)S(1)} %copy-done, s32[1,128]{1,0:T(1,128)} %bitcast.22, bf16[64,64]{1,0:T(8,128)(2,1)} %stiff_hbm.1), custom_call_target="tpu_custom_call" | custom-call | flops 500000000 | bytes 3145728 | tf_op jit(solution)/shard_map/pallas_call | solution.py:135
  13.6 1.7 %shard_map.92 = (bf16[256,32,128]{2,1,0:T(8,128)(2,1)S(1)}, f32[68,32,128]{2,1,0:T(8,128)S(1)}) custom-call(s32[1,128]{1,0:T(1,128)S(1)} %get-tuple-element.15.target, f32[128,32,128]{2,1,0:T(8,128)S(1)} %bitcast.19, bf16[4,512,256]{2,1,0:T(8,128)(2,1)S(1)} %get-tuple-element.16.lap, bf16[512,512]{1,0:T(8,128)(2,1)S(1)} %get-tuple-element.17.spread), custom_call_target="tpu_custom_call" | custom-call | flops 1000000000 | bytes 4194304 | tf_op jit(solution)/shard_map/pallas_call | solution.py:202
  15.3 0.0 collective-permute-done.3.side_one
  15.3 0.0 collective-permute-done.row_two
  15.4 2.4 %shard_map.94 = (bf16[256,32,128]{2,1,0:T(8,128)(2,1)S(1)}, bf16[256,32,128]{2,1,0:T(8,128)(2,1)}) custom-call(s32[1,128]{1,0:T(1,128)S(1)} %get-tuple-element.15.target, f32[68,32,128]{2,1,0:T(8,128)S(1)} %get-tuple-element.18.rest, bf16[64,64]{1,0:T(8,128)(2,1)S(1)} %get-tuple-element.19.coupling, ...), custom_call_target="tpu_custom_call", output_to_operand_aliasing={{0}: (7, {})} | custom-call | flops 200000000 | bytes 2097152 | tf_op jit(solution)/shard_map/pallas_call | solution.py:261
  17.8 0.0 copy-start.4
  17.8 0.0 copy-start.5
  17.8 0.0 copy-start.6
  17.8 0.0 copy-start.1
  17.8 0.0 copy-start.2
  17.9 5.3 %all-to-all-start = ((bf16[128,64,128]{2,1,0:T(8,128)(2,1)}), bf16[128,64,128]{2,1,0:T(8,128)(2,1)S(1)}, u32[]{:S(2)}, u32[]{:S(2)}) async-start(bf16[128,64,128]{2,1,0:T(8,128)(2,1)} %bitcast.20), calls=%async_computation | async-start | bytes 4194304 | tf_op jit(solution)/shard_map/all_to_all | solution.py:370
  23.2 0.1 dot_general.5
  23.3 0.3 fusion
  23.6 0.1 copy.18
  23.7 0.1 pad_maximum_fusion.1
  23.8 29.1 %all-to-all-done = bf16[128,64,128]{2,1,0:T(8,128)(2,1)S(1)} async-done(((bf16[128,64,128]{2,1,0:T(8,128)(2,1)}), bf16[128,64,128]{2,1,0:T(8,128)(2,1)S(1)}, u32[]{:S(2)}, u32[]{:S(2)}) %all-to-all-start) | async-done | bytes 2097184 | tf_op jit(solution)/shard_map/all_to_all | solution.py:370
  52.9 0.1 broadcast_in_dim.2.rate
  53.0 3.7 %shard_map.95 = f32[256,32,128]{2,1,0:T(8,128)} custom-call(s32[256]{0:T(256)S(1)} %copy-done.2, bf16[256,32,128]{2,1,0:T(8,128)(2,1)S(1)} %bitcast.18, f32[64,8,128]{2,1,0:T(8,128)S(1)} %pad_maximum_fusion.ghosts, f32[8,128]{1,0:T(8,128)S(1)} %broadcast_in_dim.2.rate, bf16[256,256]{1,0:T(8,128)(2,1)S(1)} %copy-done.1), custom_call_target="tpu_custom_call" | custom-call | tf_op jit(solution)/shard_map/pallas_call | solution.py:333
  (11 shorter events, 0.1 us)
Async XLA Ops:
  0.0 1.2 %copy-start = (bf16[64,32,256]{2,1,0:T(8,128)(2,1)S(1)}, bf16[64,32,256]{2,1,0:T(8,128)(2,1)}, u32[]{:S(2)}) copy-start(bf16[64,32,256]{2,1,0:T(8,128)(2,1)} %leaf.3) | copy-start | bytes 3145732
  1.2 12.3 %copy-start.3 = (f32[128,4,1024]{2,1,0:T(4,128)S(1)}, f32[128,4,1024]{2,1,0:T(4,128)}, u32[]{:S(2)}) copy-start(f32[128,4,1024]{2,1,0:T(4,128)} %param.9) | copy-start | bytes 6291460
  2.3 13.0 %collective-permute-start.2 = (bf16[64,128]{1,0:T(8,128)(2,1)S(1)}, bf16[64,128]{1,0:T(8,128)(2,1)S(1)}, u32[]{:S(2)}, u32[]{:S(2)}) collective-permute-start(bf16[64,128]{1,0:T(8,128)(2,1)S(1)} %get-tuple-element.22), channel_id=1, source_target_pairs={{1,2},{3,4},{5,6},{7,8},{9,10},{11,12},{13,14},{15,0},{2,1},{4,3},... | collective-permute-start | bytes 49160 | tf_op jit(solution)/shard_map/ppermute | solution.py:158
  8.2 7.2 %collective-permute-start.3 = (bf16[64,128]{1,0:T(8,128)(2,1)S(1)}, bf16[64,128]{1,0:T(8,128)(2,1)S(1)}, u32[]{:S(2)}, u32[]{:S(2)}) collective-permute-start(bf16[64,128]{1,0:T(8,128)(2,1)S(1)} %get-tuple-element.22), channel_id=1, source_target_pairs={{0,1},{2,3},{4,5},{6,7},{8,9},{10,11},{12,13},{14,15},{1,0},{3,2},... | collective-permute-start | bytes 49160 | tf_op jit(solution)/shard_map/ppermute | solution.py:158
  8.2 7.2 %collective-permute-start = (bf16[64,256]{1,0:T(8,128)(2,1)S(1)}, bf16[64,256]{1,0:T(8,128)(2,1)S(1)}, u32[]{:S(2)}, u32[]{:S(2)}) collective-permute-start(bf16[64,256]{1,0:T(8,128)(2,1)S(1)} %get-tuple-element.20), channel_id=1, source_target_pairs={{16,32},{48,64},{80,96},{112,0},{32,16},{64,48},{96,80},{0,112},{1... | collective-permute-start | bytes 98312 | tf_op jit(solution)/shard_map/ppermute | solution.py:158
  10.6 4.7 %collective-permute-start.1 = (bf16[64,256]{1,0:T(8,128)(2,1)S(1)}, bf16[64,256]{1,0:T(8,128)(2,1)S(1)}, u32[]{:S(2)}, u32[]{:S(2)}) collective-permute-start(bf16[64,256]{1,0:T(8,128)(2,1)S(1)} %get-tuple-element.21), channel_id=1, source_target_pairs={{0,16},{32,48},{64,80},{96,112},{16,0},{48,32},{80,64},{112,96},{1... | collective-permute-start | bytes 98312 | tf_op jit(solution)/shard_map/ppermute | solution.py:158
  17.8 5.4 %copy-start.4 = (f32[64,256]{1,0:T(8,128)S(1)}, f32[64,256]{1,0:T(8,128)}, u32[]{:S(2)}) copy-start(f32[64,256]{1,0:T(8,128)} %param.13) | copy-start | bytes 196612
  17.8 5.5 %copy-start.5 = (f32[64,128,1]{1,0,2:T(8,128)S(1)}, f32[64,128,1]{1,0,2:T(8,128)}, u32[]{:S(2)}) copy-start(f32[64,128,1]{1,0,2:T(8,128)} %constant.7) | copy-start | bytes 98308
  17.8 5.8 %copy-start.6 = (f32[4]{0:T(128)S(1)}, f32[4]{0:T(128)}, u32[]{:S(2)}) copy-start(f32[4]{0:T(128)} %param.15) | copy-start | bytes 52
  17.8 35.2 %copy-start.1 = (bf16[256,256]{1,0:T(8,128)(2,1)S(1)}, bf16[256,256]{1,0:T(8,128)(2,1)}, u32[]{:S(2)}) copy-start(bf16[256,256]{1,0:T(8,128)(2,1)} %constant.5.clone.shift) | copy-start | bytes 393220
  17.8 35.2 %copy-start.2 = (s32[256]{0:T(256)S(1)}, s32[256]{0:T(256)}, u32[]{:S(2)}) copy-start(s32[256]{0:T(256)} %strip.1) | copy-start | bytes 3076
  17.9 35.1 %all-to-all-start = ((bf16[128,64,128]{2,1,0:T(8,128)(2,1)}), bf16[128,64,128]{2,1,0:T(8,128)(2,1)S(1)}, u32[]{:S(2)}, u32[]{:S(2)}) async-start(bf16[128,64,128]{2,1,0:T(8,128)(2,1)} %bitcast.20), calls=%async_computation | async-start | bytes 4194304 | tf_op jit(solution)/shard_map/all_to_all | solution.py:370
